TPU v7x, 32 devices: a whole 2x2x4 slice. The times are simulated.
32 devices in a mesh: seq: 8 (over z, y), head: 4 (over x, core).
Axes of the slice: x: 2, y: 2, z: 4, core: 2. Of those that a mesh axis runs over, the one named last changes fastest.
Arguments:
- short_input: bfloat16 [2, 512, 768], P(None, 'seq'), may hold values from -6 to 6
- long_input: bfloat16 [2, 1024, 768], P(None, 'seq'), may hold values from -6 to 6
- short_cotangent: bfloat16 [2, 512, 768], P(None, 'seq'), may hold values from -6 to 6
- long_cotangent: bfloat16 [2, 1024, 768], P(None, 'seq'), may hold values from -6 to 6
- short_lengths: int32 [2], replicated, may hold values from 256 to 512, as said below
- long_lengths: int32 [2], replicated, may hold values from 512 to 1024, as said below
- proj_weight: bfloat16 [3, 768, 768], P(None, 'seq', 'head'), may hold values from -0.3125 to 0.3125
- out_weight: bfloat16 [768, 768], P('head', 'seq'), may hold values from -1.5 to 1.5
- conv_taps: bfloat16 [9, 768], P(None, ('head', 'seq')), may hold values from -3 to 3
- attention_gain: bfloat16 [768], P('seq'), may hold values from 0.25 to 1.75
- up_weight: bfloat16 [768, 3072], P('seq', 'head'), may hold values from -0.21875 to 0.21875
- down_weight: bfloat16 [3072, 768], P('head', 'seq'), may hold values from -0.109375 to 0.109375
- feed_gain: bfloat16 [768], P('seq'), may hold values from 0.25 to 1.75
Outputs:
- short_output: bfloat16 [2, 512, 768], P(None, 'seq')
- long_output: bfloat16 [2, 1024, 768], P(None, 'seq')
- short_input_grad: float32 [2, 512, 768], P(None, 'seq')
- long_input_grad: float32 [2, 1024, 768], P(None, 'seq')
- proj_weight_grad: float32 [3, 768, 768], P(None, 'seq', 'head')
- out_weight_grad: float32 [768, 768], P('head', 'seq')
- conv_taps_grad: float32 [9, 768], P(None, ('head', 'seq'))
- attention_gain_grad: float32 [768], P('seq')
- up_weight_grad: float32 [768, 3072], P('seq', 'head')
- down_weight_grad: float32 [3072, 768], P('head', 'seq')
- feed_gain_grad: float32 [768], P('seq')
Inputs may be any that keep to these rules, and one draw needn't show every extreme that they name: `short_lengths`: one sequence of every draw, which one drawn from the seed, has all 512 positions; the others have fewer. `long_lengths`: one sequence of every draw, which one drawn from the seed, has all 1024 positions; the others have fewer.
All inputs are finite; a program needn't handle non-finite values.
Results may differ from a plain program's by a relative error of at most 0.023.
Values may be sent and summed in bfloat16 or wider, within the bound.
No kernel may reach another device: no remote copies, remote signals or barrier semaphores. Data moves between devices by JAX's collectives and lax.ppermute only.
A program may use at most 128 MiB of HBM per device.

v0:
```python
import jax
import jax.numpy as jnp
from jax import lax
from jax.sharding import PartitionSpec as P

HEAD_DIM = 64


norm_eps = 1e-06
mask_fill = -1e30
block_limit = 2048


def passed_along(block, axis, distance):
    devices = range(lax.axis_size(axis))
    route = [((i - distance) % len(devices), i) for i in devices]
    return lax.ppermute(block, axis, route)


def shifted(array, axis, by):
    peers = lax.axis_size(axis)
    pairs = [(i, i + by) for i in range(peers) if 0 <= i + by < peers]
    return lax.ppermute(array, axis, pairs)


def block_rows(row_count):
    size_rows = min(row_count, block_limit)
    while row_count % size_rows != 0:
        size_rows = size_rows - 1
    return size_rows


def norm_forward(values_in, gain_row):
    inv_root = lax.rsqrt(jnp.mean(values_in * values_in, axis=-1, keepdims=True) + norm_eps)
    return (values_in * inv_root * gain_row, inv_root)


def norm_backward(values_in, inv_root, gain_row, grad_in):
    weighted = grad_in * gain_row
    inner_mean = jnp.mean(weighted * values_in, axis=-1, keepdims=True)
    grad_values = inv_root * weighted - values_in * inv_root * inv_root * inv_root * inner_mean
    grad_gain = jnp.sum(grad_in * values_in * inv_root, axis=(0, 1))
    return (grad_values, grad_gain)


def allowed_mask(query_pos, key_pos, lengths):
    causal = key_pos[None, :] <= query_pos[:, None]
    inside = key_pos[None, :] < lengths[:, None]
    return jnp.logical_and(causal[None, None], inside[:, None, None, :])


def block_scores(query_rows, key_rows, query_pos, key_pos, lengths):
    allowed = allowed_mask(query_pos, key_pos, lengths)
    raw_scores = jnp.einsum(
        "bqhe,bkhe->bhqk", query_rows, key_rows, preferred_element_type=jnp.float32
    ) * HEAD_DIM ** (-0.5)
    return (jnp.where(allowed, raw_scores, mask_fill), allowed)


def block_grads(
    query_rows, grad_rows, log_rows, delta_rows, key_rows, value_rows, query_pos, key_pos, lengths
):
    scores, allowed = block_scores(query_rows, key_rows, query_pos, key_pos, lengths)
    prob_rows = jnp.where(
        allowed, jnp.exp(scores - jnp.transpose(log_rows, (0, 2, 1))[..., None]), 0.0
    )
    grad_probs = jnp.einsum(
        "bqhe,bkhe->bhqk", grad_rows, value_rows, preferred_element_type=jnp.float32
    )
    grad_scores = (
        prob_rows * (grad_probs - jnp.transpose(delta_rows, (0, 2, 1))[..., None])
    ).astype(jnp.bfloat16)
    grad_query = jnp.einsum(
        "bhqk,bkhe->bqhe", grad_scores, key_rows, preferred_element_type=jnp.float32
    ) * HEAD_DIM ** (-0.5)
    grad_key = jnp.einsum(
        "bhqk,bqhe->bkhe", grad_scores, query_rows, preferred_element_type=jnp.float32
    ) * HEAD_DIM ** (-0.5)
    grad_value = jnp.einsum(
        "bhqk,bqhe->bkhe",
        prob_rows.astype(jnp.bfloat16),
        grad_rows,
        preferred_element_type=jnp.float32,
    )
    return (grad_query, grad_key, grad_value)


def attend_forward(queries, keys_here, values_here, query_pos, lengths):
    seq_count, span_rows, head_count, head_width = queries.shape
    initial = (
        jnp.full((seq_count, head_count, span_rows), mask_fill, jnp.float32),
        jnp.zeros((seq_count, head_count, span_rows), jnp.float32),
        jnp.zeros((seq_count, span_rows, head_count, head_width), jnp.float32),
    )
    key_piece = lax.all_gather(keys_here, "seq", axis=1, tiled=True)
    value_piece = lax.all_gather(values_here, "seq", axis=1, tiled=True)
    row_count = key_piece.shape[1]
    size_rows = block_rows(row_count)

    def one_block(block_index, carried_state):
        running_top, running_sum, acc_rows = carried_state
        offset = block_index * size_rows
        key_rows = lax.dynamic_slice_in_dim(key_piece, offset, size_rows, 1)
        value_rows = lax.dynamic_slice_in_dim(value_piece, offset, size_rows, 1)
        key_pos = offset + jnp.arange(size_rows, dtype=jnp.int32)
        scores, allowed = block_scores(queries, key_rows, query_pos, key_pos, lengths)
        new_top = jnp.maximum(running_top, jnp.max(scores, axis=-1))
        exp_terms = jnp.where(allowed, jnp.exp(scores - new_top[..., None]), 0.0)
        shrink = jnp.exp(running_top - new_top)
        running_sum = running_sum * shrink + jnp.sum(exp_terms, axis=-1)
        acc_rows = acc_rows * jnp.transpose(shrink, (0, 2, 1))[..., None] + jnp.einsum(
            "bhqk,bkhe->bqhe",
            exp_terms.astype(jnp.bfloat16),
            value_rows,
            preferred_element_type=jnp.float32,
        )
        return (new_top, running_sum, acc_rows)

    running_top, running_sum, acc_rows = lax.fori_loop(
        0, row_count // size_rows, one_block, initial
    )
    attention = acc_rows / jnp.transpose(running_sum, (0, 2, 1))[..., None]
    log_totals = jnp.transpose(running_top + jnp.log(running_sum), (0, 2, 1))
    return (attention, log_totals)


def pass_sums(grad_keys, grad_values):
    return (
        passed_along(grad_keys.astype(jnp.bfloat16), "seq", 1).astype(grad_keys.dtype),
        passed_along(grad_values.astype(jnp.bfloat16), "seq", 1).astype(grad_values.dtype),
    )


def attend_backward(
    queries, keys_here, values_here, grad_attention, log_totals, delta_rows, query_pos, lengths
):
    seq_count, span_rows, head_count, head_width = queries.shape
    zeros_local = jnp.zeros(queries.shape, jnp.float32)
    seq_size = lax.axis_size("seq")
    my_index = lax.axis_index("seq")
    local_pos = jnp.arange(span_rows, dtype=jnp.int32)

    def step_grads(step, key_piece, value_piece):
        anchor = jnp.mod(my_index - step, seq_size)
        key_pos = anchor * span_rows + local_pos
        return block_grads(
            queries,
            grad_attention,
            log_totals,
            delta_rows,
            key_piece,
            value_piece,
            query_pos,
            key_pos,
            lengths,
        )

    def cycle_step(step, state):
        key_piece, value_piece, grad_keys, grad_values, grad_query = state
        query_part, key_part, value_part = step_grads(step, key_piece, value_piece)
        key_piece, value_piece = shifted((key_piece, value_piece), "seq", 1)
        grad_keys, grad_values = pass_sums(grad_keys + key_part, grad_values + value_part)
        return (key_piece, value_piece, grad_keys, grad_values, grad_query + query_part)

    final_state = lax.fori_loop(
        0, seq_size - 1, cycle_step, (keys_here, values_here, zeros_local, zeros_local, zeros_local)
    )
    key_piece, value_piece, grad_keys, grad_values, grad_query = final_state
    query_part, key_part, value_part = step_grads(seq_size - 1, key_piece, value_piece)
    grad_key, grad_value = pass_sums(grad_keys + key_part, grad_values + value_part)
    grad_query = grad_query + query_part
    return (grad_query, grad_key, grad_value)


def micro_batch(inputs, cotangent, lengths, weights):
    proj_full, out_full, taps_full, attend_gain, up_full, down_full, ffn_gain = weights
    seq_count, span_rows, model_width = inputs.shape
    local_width = proj_full.shape[2]
    heads_here = local_width // HEAD_DIM
    query_pos = lax.axis_index("seq") * span_rows + jnp.arange(span_rows, dtype=jnp.int32)
    valid_rows = (query_pos[None, :] < lengths[:, None])[..., None]
    residual_in = inputs.astype(jnp.float32)
    normed, inv_first = norm_forward(residual_in, attend_gain)
    normed_low = normed.astype(jnp.bfloat16)
    mixed_qkv = jnp.einsum(
        "btd,cde->cbte", normed_low, proj_full, preferred_element_type=jnp.float32
    ).astype(jnp.bfloat16)
    borrowed = shifted(mixed_qkv[:, :, span_rows - 2 :, :], "seq", 1)
    extended = jnp.concatenate([borrowed, mixed_qkv], axis=2).astype(jnp.float32)
    tap_table = taps_full.astype(jnp.float32).reshape(3, 3, local_width)
    tap_now = tap_table[:, 0][:, None, None, :]
    tap_one = tap_table[:, 1][:, None, None, :]
    tap_two = tap_table[:, 2][:, None, None, :]
    conved = (
        tap_now * extended[:, :, 2:]
        + tap_one * extended[:, :, 1:-1]
        + tap_two * extended[:, :, :-2]
    )
    conv_out = conved.astype(jnp.bfloat16).reshape(3, seq_count, span_rows, heads_here, HEAD_DIM)
    queries, keys_here, values_here = (conv_out[0], conv_out[1], conv_out[2])
    attention, log_totals = attend_forward(queries, keys_here, values_here, query_pos, lengths)
    attention_low = attention.astype(jnp.bfloat16).reshape(seq_count, span_rows, local_width)
    attend_part = jnp.einsum(
        "bte,ed->btd", attention_low, out_full, preferred_element_type=jnp.float32
    )
    mid_residual = residual_in + lax.psum(attend_part.astype(jnp.bfloat16), "head").astype(
        jnp.float32
    )
    normed_ffn, inv_second = norm_forward(mid_residual, ffn_gain)
    normed_ffn_low = normed_ffn.astype(jnp.bfloat16)
    up_proj = jnp.einsum("btd,df->btf", normed_ffn_low, up_full, preferred_element_type=jnp.float32)
    relu_up = jnp.maximum(up_proj, 0.0)
    squared = (relu_up * relu_up).astype(jnp.bfloat16)
    ffn_part = jnp.einsum("btf,fd->btd", squared, down_full, preferred_element_type=jnp.float32)
    output = (
        mid_residual + lax.psum(ffn_part.astype(jnp.bfloat16), "head").astype(jnp.float32)
    ).astype(jnp.bfloat16)
    grad_out = jnp.where(valid_rows, cotangent.astype(jnp.float32), 0.0)
    grad_out_low = grad_out.astype(jnp.bfloat16)
    down_term = jnp.einsum("btf,btd->fd", squared, grad_out_low, preferred_element_type=jnp.float32)
    grad_squared = jnp.einsum(
        "btd,fd->btf", grad_out_low, down_full, preferred_element_type=jnp.float32
    )
    grad_up = (grad_squared * 2.0 * relu_up).astype(jnp.bfloat16)
    up_term = jnp.einsum("btd,btf->df", normed_ffn_low, grad_up, preferred_element_type=jnp.float32)
    grad_normed_ffn = lax.psum(
        jnp.einsum("btf,df->btd", grad_up, up_full, preferred_element_type=jnp.float32).astype(
            jnp.bfloat16
        ),
        "head",
    ).astype(jnp.float32)
    grad_through, feed_term = norm_backward(mid_residual, inv_second, ffn_gain, grad_normed_ffn)
    grad_mid = grad_out + grad_through
    grad_mid_low = grad_mid.astype(jnp.bfloat16)
    out_term = jnp.einsum(
        "bte,btd->ed", attention_low, grad_mid_low, preferred_element_type=jnp.float32
    )
    grad_attention = jnp.einsum(
        "btd,ed->bte", grad_mid_low, out_full, preferred_element_type=jnp.float32
    )
    grad_attention = grad_attention.astype(jnp.bfloat16).reshape(
        seq_count, span_rows, heads_here, HEAD_DIM
    )
    delta_rows = jnp.einsum("bqhe,bqhe->bqh", grad_attention.astype(jnp.float32), attention)
    grad_query, grad_key, grad_value = attend_backward(
        queries, keys_here, values_here, grad_attention, log_totals, delta_rows, query_pos, lengths
    )
    grad_conv = jnp.stack([grad_query, grad_key, grad_value]).reshape(
        3, seq_count, span_rows, local_width
    )
    taps_term = jnp.stack(
        [
            jnp.sum(grad_conv * extended[:, :, 2:], axis=(1, 2)),
            jnp.sum(grad_conv * extended[:, :, 1:-1], axis=(1, 2)),
            jnp.sum(grad_conv * extended[:, :, :-2], axis=(1, 2)),
        ],
        axis=1,
    ).reshape(9, local_width)
    full_grad = jnp.pad(grad_conv, ((0, 0), (0, 0), (2, 2), (0, 0)))
    grad_extended = (
        tap_now * full_grad[:, :, 0 : span_rows + 2]
        + tap_one * full_grad[:, :, 1 : span_rows + 3]
        + tap_two * full_grad[:, :, 2 : span_rows + 4]
    )
    returned = shifted(grad_extended[:, :, :2], "seq", -1)
    grad_mixed = jnp.concatenate(
        [grad_extended[:, :, 2:span_rows], grad_extended[:, :, span_rows:] + returned], axis=2
    ).astype(jnp.bfloat16)
    proj_term = jnp.einsum(
        "btd,cbte->cde", normed_low, grad_mixed, preferred_element_type=jnp.float32
    )
    grad_normed = lax.psum(
        jnp.einsum(
            "cbte,cde->btd", grad_mixed, proj_full, preferred_element_type=jnp.float32
        ).astype(jnp.bfloat16),
        "head",
    ).astype(jnp.float32)
    grad_first, attention_term = norm_backward(residual_in, inv_first, attend_gain, grad_normed)
    grad_input = grad_mid + grad_first
    return (
        output,
        grad_input,
        (proj_term, out_term, taps_term, attention_term, up_term, down_term, feed_term),
    )


def shards(
    short_input,
    long_input,
    short_cotangent,
    long_cotangent,
    short_lengths,
    long_lengths,
    proj_weight,
    out_weight,
    conv_taps,
    attention_gain,
    up_weight,
    down_weight,
    feed_gain,
):
    proj_full, out_full, taps_full, attend_gain = (
        lax.all_gather(proj_weight, "seq", axis=1, tiled=True),
        lax.all_gather(out_weight, "seq", axis=1, tiled=True),
        lax.all_gather(conv_taps, "seq", axis=1, tiled=True),
        lax.all_gather(attention_gain, "seq", axis=0, tiled=True),
    )
    up_full, down_full, ffn_gain = (
        lax.all_gather(up_weight, "seq", axis=0, tiled=True),
        lax.all_gather(down_weight, "seq", axis=1, tiled=True),
        lax.all_gather(feed_gain, "seq", axis=0, tiled=True),
    )
    weights = (
        proj_full,
        out_full,
        taps_full,
        attend_gain.astype(jnp.float32),
        up_full,
        down_full,
        ffn_gain.astype(jnp.float32),
    )
    short_output, short_input_grad, short_terms = micro_batch(
        short_input, short_cotangent, short_lengths, weights
    )
    long_output, long_input_grad, long_terms = micro_batch(
        long_input, long_cotangent, long_lengths, weights
    )
    summed = tuple(
        (first_term + second_term for first_term, second_term in zip(short_terms, long_terms))
    )
    reduced = (
        lax.psum_scatter(summed[0], "seq", scatter_dimension=1, tiled=True),
        lax.psum_scatter(summed[1], "seq", scatter_dimension=1, tiled=True),
        lax.psum_scatter(summed[2], "seq", scatter_dimension=1, tiled=True),
        lax.psum_scatter(summed[3], "seq", scatter_dimension=0, tiled=True),
        lax.psum_scatter(summed[4], "seq", scatter_dimension=0, tiled=True),
        lax.psum_scatter(summed[5], "seq", scatter_dimension=1, tiled=True),
        lax.psum_scatter(summed[6], "seq", scatter_dimension=0, tiled=True),
    )
    return (
        short_output,
        long_output,
        short_input_grad,
        long_input_grad,
        reduced[0],
        reduced[1],
        reduced[2],
        reduced[3],
        reduced[4],
        reduced[5],
        reduced[6],
    )


def solution(mesh):
    placed = (
        P(None, "seq", None),
        P(None, "seq", None),
        P(None, "seq", None),
        P(None, "seq", None),
        P(),
        P(),
        P(None, "seq", "head"),
        P("head", "seq"),
        P(None, ("head", "seq")),
        P("seq"),
        P("seq", "head"),
        P("head", "seq"),
        P("seq"),
    )
    return jax.shard_map(
        shards,
        mesh=mesh,
        in_specs=placed,
        out_specs=(
            P(None, "seq", None),
            P(None, "seq", None),
            P(None, "seq", None),
            P(None, "seq", None),
            P(None, "seq", "head"),
            P("head", "seq"),
            P(None, ("head", "seq")),
            P("seq"),
            P("seq", "head"),
            P("head", "seq"),
            P("seq"),
        ),
        check_vma=False,
    )
```

profile of v0, /device:TPU:0, one launch (start us, length us, event | category | flops | bytes accessed | tf_op | source)
XLA Modules:
  0.0 995.5 jit_solution(1963715763780016032)
XLA Ops:
  8.1 35.7 %all_gather.35 = bf16[3,768,192]{2,1,0:T(8,128)(2,1)S(1)} all-gather(bf16[3,96,192]{2,1,0:T(8,128)(2,1)} %param.23), channel_id=1, replica_groups=mesh['seq'=8,'head'=4] {'seq'}, dimensions={1}, use_global_device_ids=true | all-gather | bytes 995328 | tf_op jit(solution)/shard_map/all_gather | solution.py:303
  45.5 21.5 %all-reduce.8 = (bf16[768]{0:T(1024)(128)(2,1)S(1)}, bf16[768]{0:T(1024)(128)(2,1)}) all-reduce(bf16[768]{0:T(1024)(128)(2,1)S(1)} %dynamic-update-slice, bf16[768]{0:T(1024)(128)(2,1)S(1)} %dynamic-update-slice.1), channel_id=1, replica_groups=mesh['seq'=8,'head'=4] {'seq'}, use_global_device_ids=true, to_apply=%add.2 | all-reduce | flops 1536 | bytes 6144
  74.0 30.4 %all-gather = bf16[8,24,9]{1,2,0:T(8,128)(2,1)S(1)} all-gather(bf16[1,24,9]{1,2,0:T(8,128)(2,1)S(1)} %bitcast.374), channel_id=1, replica_groups=mesh['seq'=8,'head'=4] {'seq'}, dimensions={0}, use_global_device_ids=true | all-gather | bytes 3888 | tf_op jit(solution)/shard_map/all_gather | solution.py:305
  108.1 31.1 %all_gather.38 = bf16[192,768]{0,1:T(8,128)(2,1)S(1)} all-gather(bf16[192,96]{0,1:T(8,128)(2,1)S(1)} %copy.130), channel_id=1, replica_groups=mesh['seq'=8,'head'=4] {'seq'}, dimensions={1}, use_global_device_ids=true | all-gather | bytes 331776 | tf_op jit(solution)/shard_map/all_gather | solution.py:304
  141.2 32.1 %all_gather.36 = bf16[2,512,3,64]{3,1,2,0:T(8,128)(2,1)S(1)} all-gather(bf16[2,64,3,64]{3,1,2,0:T(8,128)(2,1)S(1)} %copy.125), channel_id=1, replica_groups=mesh['seq'=8,'head'=4] {'seq'}, dimensions={1}, use_global_device_ids=true | all-gather | bytes 442368 | tf_op jit(solution)/shard_map/all_gather | solution.py:95
  178.9 28.0 %all_gather.42 = bf16[2,1024,3,64]{1,3,2,0:T(8,128)(2,1)S(1)} all-gather(bf16[2,128,3,64]{1,3,2,0:T(8,128)(2,1)} %bitcast.23), channel_id=1, replica_groups=mesh['seq'=8,'head'=4] {'seq'}, dimensions={1}, use_global_device_ids=true | all-gather | bytes 884736 | tf_op jit(solution)/shard_map/all_gather | solution.py:95
  214.0 32.6 %all_gather.37 = bf16[2,512,3,64]{3,0,2,1:T(2,128)(2,1)S(1)} all-gather(bf16[2,64,3,64]{3,0,2,1:T(2,128)(2,1)} %copy.128), channel_id=1, replica_groups=mesh['seq'=8,'head'=4] {'seq'}, dimensions={1}, use_global_device_ids=true | all-gather | bytes 442368 | tf_op jit(solution)/shard_map/all_gather | solution.py:96
  246.5 27.9 %all_gather.43 = bf16[2,1024,3,64]{1,3,2,0:T(8,128)(2,1)S(1)} all-gather(bf16[2,128,3,64]{1,3,2,0:T(8,128)(2,1)} %bitcast.25), channel_id=1, replica_groups=mesh['seq'=8,'head'=4] {'seq'}, dimensions={1}, use_global_device_ids=true | all-gather | bytes 884736 | tf_op jit(solution)/shard_map/all_gather | solution.py:96
  284.2 26.5 %all-reduce.20.cloned.1.call-done = (bf16[2,64,768]{2,1,0:T(8,128)(2,1)}, bf16[2,128,768]{2,1,0:T(8,128)(2,1)}) async-done(((bf16[2,64,768]{2,1,0:T(8,128)(2,1)}, bf16[2,128,768]{2,1,0:T(8,128)(2,1)}), (bf16[2,64,768]{2,1,0:T(8,128)(2,1)}, bf16[2,128,768]{2,1,0:T(8,128)(2,1)})) %all-reduce.20.cloned.1.call-update) | async-done | bytes 589840 | tf_op jit(solution)/shard_map/psum | solution.py:206
  313.0 8.0 all-gather.4.cloned.1.call-done
  324.3 38.9 %all-gather.6.cloned.1.call-done = bf16[768,768]{0,1:T(8,128)(2,1)} async-done(((bf16[768,96]{0,1:T(8,128)(2,1)}), bf16[768,768]{0,1:T(8,128)(2,1)}) %all-gather.6.cloned.1.call-update) | async-done | bytes 1179664 | tf_op jit(solution)/shard_map/all_gather | solution.py:310
  372.6 28.6 %all-reduce.18.cloned.1.call-done = (bf16[2,64,768]{2,1,0:T(8,128)(2,1)}, bf16[2,128,768]{2,1,0:T(8,128)(2,1)}) async-done(((bf16[2,64,768]{2,1,0:T(8,128)(2,1)}, bf16[2,128,768]{2,1,0:T(8,128)(2,1)}), (bf16[2,64,768]{2,1,0:T(8,128)(2,1)}, bf16[2,128,768]{2,1,0:T(8,128)(2,1)})) %all-reduce.18.cloned.1.call-update) | async-done | bytes 589840 | tf_op jit(solution)/shard_map/psum | solution.py:226
  404.9 112.8 %while.14 = (s32[]{:T(128)}, bf16[2,64,3,64]{3,1,2,0:T(8,128)(2,1)S(1)}, bf16[2,64,3,64]{3,1,2,0:T(8,128)(2,1)S(1)}, f32[2,64,3,64]{3,1,2,0:T(8,128)S(1)}, f32[2...) while((s32[]{:T(128)}, ...), condition=%wide.region_15.16_spmd.clone, body=%wide.region_14.15_spmd.clone.sunk | while | flops 16232720 | bytes 2585574 | solution.py:165
  527.7 144.5 %while.15 = (s32[]{:T(128)}, bf16[2,128,3,64]{1,3,2,0:T(8,128)(2,1)}, bf16[2,128,3,64]{1,3,2,0:T(8,128)(2,1)}, f32[2,128,3,64]{1,3,2,0:T(8,128)S(1)}, f32[2,128,...) while((s32[]{:T(128)}, ...), condition=%wide.region_21.22_spmd.clone, body=%wide.region_20.21_spmd.clone.sunk | while | flops 64340496 | bytes 6497794 | solution.py:165
  540.2 5.2 collective-permute-done.6
  582.9 7.0 collective-permute-done.6
  602.9 7.6 collective-permute-done.6
  626.5 4.4 collective-permute-done.6
  715.9 4.7 reshape.632
  729.2 16.2 %all-reduce.16.cloned.1.call-done = (bf16[2,64,768]{2,1,0:T(8,128)(2,1)}, bf16[2,128,768]{2,1,0:T(8,128)(2,1)}, bf16[2,64,768]{2,1,0:T(8,128)(2,1)}, bf16[2,128,768]{2,1,0:T(8,128)(2,1)}) async-done(((bf16[2,64,768]{2,1,0:T(8,128)(2,1)}, bf16[2,128,768]{2,1,0:T(8,128)(2,1)}, bf16[2,64,768]{2,1,0:T(8,128)(2,1)}, bf16[2,128,768]{2,1,0:T(8,128)(2,1)}), (bf16[2,64,768]{2,1,0:T(8,128)(2,1)}, ...) | async-done | bytes 1179664 | tf_op jit(solution)/shard_map/psum | solution.py:216
  748.0 37.2 %all-reduce.7 = (f32[9,192]{1,0:T(8,128)S(1)}, f32[768]{0:T(1024)S(1)}, f32[768]{0:T(1024)S(1)}) all-reduce(f32[9,192]{1,0:T(8,128)S(1)} %add.492, f32[768]{0:T(1024)S(1)} %add.493, f32[768]{0:T(1024)S(1)} %add.496), channel_id=4, replica_groups=mesh['seq'=8,'head'=4] {'seq'}, use_global_device_ids=true, to_apply=%region_32.33.clone | all-reduce | flops 3264 | bytes 26112
  792.5 51.1 %reduce-scatter.14.cloned.1.call-done = f32[96,576]{1,0:T(8,128)} async-done(((f32[768,576]{1,0:T(8,128)}), f32[96,576]{1,0:T(8,128)}) %reduce-scatter.14.cloned.1.call-update) | async-done | bytes 221200
  845.5 70.5 %reduce-scatter.10.cloned.1.call-done = f32[96,768]{1,0:T(8,128)} async-done(((f32[768,768]{1,0:T(8,128)}), f32[96,768]{1,0:T(8,128)}) %reduce-scatter.10.cloned.1.call-update) | async-done | bytes 294928 | tf_op jit(solution)/shard_map/reduce_scatter | solution.py:336
  916.0 72.4 %reduce-scatter.12.cloned.1.call-done = f32[768,96]{0,1:T(8,128)} async-done(((f32[768,768]{0,1:T(8,128)}), f32[768,96]{0,1:T(8,128)}) %reduce-scatter.12.cloned.1.call-update) | async-done | bytes 294928 | tf_op jit(solution)/shard_map/reduce_scatter | solution.py:337
  (735 shorter events, 357.6 us)
Async XLA Ops:
  8.1 302.6 %all-reduce.20.cloned.1.call-start = ((), (), s32[]{:S(2)}) async-start(), calls=%async_computation.12 | async-start | bytes 1179648 | tf_op jit(solution)/shard_map/psum | solution.py:206
  67.5 71.7 %collective-permute-start.8 = (bf16[3,2,2,192]{3,2,0,1:T(2,128)(2,1)S(1)}, bf16[3,2,2,192]{3,2,0,1:T(2,128)(2,1)S(1)}, u32[]{:S(2)}, u32[]{:S(2)}) collective-permute-start(bf16[3,2,2,192]{3,2,0,1:T(2,128)(2,1)S(1)} %slice.134), channel_id=1, source_target_pairs={{0,4},{4,8},{8,12},{12,16},{16,20},{20,24},{24,28},{1,5},{5,9},{9,... | collective-permute-start | bytes 13832 | tf_op jit(solution)/shard_map/ppermute | solution.py:23
  70.6 105.7 %collective-permute-start.9 = (bf16[3,2,2,192]{2,3,0,1:T(8,128)(2,1)}, bf16[3,2,2,192]{2,3,0,1:T(8,128)(2,1)}, u32[]{:S(2)}, u32[]{:S(2)}) collective-permute-start(bf16[3,2,2,192]{2,3,0,1:T(8,128)(2,1)} %slice.143), channel_id=1, source_target_pairs={{0,4},{4,8},{8,12},{12,16},{16,20},{20,24},{24,28},{1,5},{5,9},{9,... | collective-permute-start | bytes 13832 | tf_op jit(solution)/shard_map/ppermute | solution.py:23
  279.6 41.5 %all-gather.4.cloned.1.call-start = ((), (), s32[]{:S(2)}) async-start(), calls=%async_computation.4 | async-start | bytes 1327104 | tf_op jit(solution)/shard_map/all_gather | solution.py:309
  280.2 83.0 %all-gather.6.cloned.1.call-start = ((), (), s32[]{:S(2)}) async-start(), calls=%async_computation.5 | async-start | bytes 1327104 | tf_op jit(solution)/shard_map/all_gather | solution.py:310
  280.8 120.4 %all-reduce.18.cloned.1.call-start = ((), (), s32[]{:S(2)}) async-start(), calls=%async_computation.11 | async-start | bytes 1179648 | tf_op jit(solution)/shard_map/psum | solution.py:226
  368.9 376.4 %all-reduce.16.cloned.1.call-start = ((), (), s32[]{:S(2)}) async-start(), calls=%async_computation.10 | async-start | bytes 2359296 | tf_op jit(solution)/shard_map/psum | solution.py:216
  404.9 18.2 %collective-permute-start = (bf16[2,64,3,64]{3,1,2,0:T(8,128)(2,1)S(1)}, bf16[2,64,3,64]{3,1,2,0:T(8,128)(2,1)S(1)}, u32[]{:S(2)}, u32[]{:S(2)}) collective-permute-start(bf16[2,64,3,64]{3,1,2,0:T(8,128)(2,1)S(1)} %copy.225), channel_id=1, source_target_pairs={{0,4},{4,8},{8,12},{12,16},{16,20},{20,24},{24,28},{1,5},{5,9},{9,... | collective-permute-start | bytes 147464 | tf_op jit(solution)/shard_map/while/body/eval_jaxpr/ppermute | solution.py:23
  499.6 18.1 %collective-permute-start = (bf16[2,64,3,64]{3,1,2,0:T(8,128)(2,1)S(1)}, bf16[2,64,3,64]{3,1,2,0:T(8,128)(2,1)S(1)}, u32[]{:S(2)}, u32[]{:S(2)}) collective-permute-start(bf16[2,64,3,64]{3,1,2,0:T(8,128)(2,1)S(1)} %copy.225), channel_id=1, source_target_pairs={{0,4},{4,8},{8,12},{12,16},{16,20},{20,24},{24,28},{1,5},{5,9},{9,... | collective-permute-start | bytes 147464 | tf_op jit(solution)/shard_map/while/body/eval_jaxpr/ppermute | solution.py:23
  520.8 162.1 %collective-permute-start.11 = (bf16[2,64,3,64]{1,3,2,0:T(8,128)(2,1)}, bf16[2,64,3,64]{1,3,2,0:T(8,128)(2,1)}, u32[]{:S(2)}, u32[]{:S(2)}) collective-permute-start(bf16[2,64,3,64]{1,3,2,0:T(8,128)(2,1)} %fusion.119), channel_id=1, source_target_pairs={{28,0},{0,4},{4,8},{8,12},{12,16},{16,20},{20,24},{24,28},{29,1},{... | collective-permute-start | bytes 147464 | tf_op jit(solution)/shard_map/ppermute | solution.py:17
  528.6 19.8 %collective-permute-start.4 = (bf16[2,128,3,64]{1,3,2,0:T(8,128)(2,1)S(1)}, bf16[2,128,3,64]{1,3,2,0:T(8,128)(2,1)}, u32[]{:S(2)}, u32[]{:S(2)}) collective-permute-start(bf16[2,128,3,64]{1,3,2,0:T(8,128)(2,1)S(1)} %copy.243), channel_id=1, source_target_pairs={{0,4},{4,8},{8,12},{12,16},{16,20},{20,24},{24,28},{1,5},{5,9},{9,... | collective-permute-start | bytes 294920 | tf_op jit(solution)/shard_map/while/body/eval_jaxpr/ppermute | solution.py:23
  549.3 20.6 %collective-permute-start.4 = (bf16[2,128,3,64]{1,3,2,0:T(8,128)(2,1)S(1)}, bf16[2,128,3,64]{1,3,2,0:T(8,128)(2,1)}, u32[]{:S(2)}, u32[]{:S(2)}) collective-permute-start(bf16[2,128,3,64]{1,3,2,0:T(8,128)(2,1)S(1)} %copy.243), channel_id=1, source_target_pairs={{0,4},{4,8},{8,12},{12,16},{16,20},{20,24},{24,28},{1,5},{5,9},{9,... | collective-permute-start | bytes 294920 | tf_op jit(solution)/shard_map/while/body/eval_jaxpr/ppermute | solution.py:23
  552.1 17.9 %collective-permute-start.5 = (bf16[2,128,3,64]{1,3,2,0:T(8,128)(2,1)S(1)}, bf16[2,128,3,64]{1,3,2,0:T(8,128)(2,1)}, u32[]{:S(2)}, u32[]{:S(2)}) collective-permute-start(bf16[2,128,3,64]{1,3,2,0:T(8,128)(2,1)S(1)} %copy.244), channel_id=1, source_target_pairs={{0,4},{4,8},{8,12},{12,16},{16,20},{20,24},{24,28},{1,5},{5,9},{9,... | collective-permute-start | bytes 294920 | tf_op jit(solution)/shard_map/while/body/eval_jaxpr/ppermute | solution.py:23
  570.8 22.1 %collective-permute-start.4 = (bf16[2,128,3,64]{1,3,2,0:T(8,128)(2,1)S(1)}, bf16[2,128,3,64]{1,3,2,0:T(8,128)(2,1)}, u32[]{:S(2)}, u32[]{:S(2)}) collective-permute-start(bf16[2,128,3,64]{1,3,2,0:T(8,128)(2,1)S(1)} %copy.243), channel_id=1, source_target_pairs={{0,4},{4,8},{8,12},{12,16},{16,20},{20,24},{24,28},{1,5},{5,9},{9,... | collective-permute-start | bytes 294920 | tf_op jit(solution)/shard_map/while/body/eval_jaxpr/ppermute | solution.py:23
  575.4 17.6 %collective-permute-start.5 = (bf16[2,128,3,64]{1,3,2,0:T(8,128)(2,1)S(1)}, bf16[2,128,3,64]{1,3,2,0:T(8,128)(2,1)}, u32[]{:S(2)}, u32[]{:S(2)}) collective-permute-start(bf16[2,128,3,64]{1,3,2,0:T(8,128)(2,1)S(1)} %copy.244), channel_id=1, source_target_pairs={{0,4},{4,8},{8,12},{12,16},{16,20},{20,24},{24,28},{1,5},{5,9},{9,... | collective-permute-start | bytes 294920 | tf_op jit(solution)/shard_map/while/body/eval_jaxpr/ppermute | solution.py:23
  593.9 19.5 %collective-permute-start.4 = (bf16[2,128,3,64]{1,3,2,0:T(8,128)(2,1)S(1)}, bf16[2,128,3,64]{1,3,2,0:T(8,128)(2,1)}, u32[]{:S(2)}, u32[]{:S(2)}) collective-permute-start(bf16[2,128,3,64]{1,3,2,0:T(8,128)(2,1)S(1)} %copy.243), channel_id=1, source_target_pairs={{0,4},{4,8},{8,12},{12,16},{16,20},{20,24},{24,28},{1,5},{5,9},{9,... | collective-permute-start | bytes 294920 | tf_op jit(solution)/shard_map/while/body/eval_jaxpr/ppermute | solution.py:23
  596.7 16.7 %collective-permute-start.5 = (bf16[2,128,3,64]{1,3,2,0:T(8,128)(2,1)S(1)}, bf16[2,128,3,64]{1,3,2,0:T(8,128)(2,1)}, u32[]{:S(2)}, u32[]{:S(2)}) collective-permute-start(bf16[2,128,3,64]{1,3,2,0:T(8,128)(2,1)S(1)} %copy.244), channel_id=1, source_target_pairs={{0,4},{4,8},{8,12},{12,16},{16,20},{20,24},{24,28},{1,5},{5,9},{9,... | collective-permute-start | bytes 294920 | tf_op jit(solution)/shard_map/while/body/eval_jaxpr/ppermute | solution.py:23
  614.3 18.6 %collective-permute-start.4 = (bf16[2,128,3,64]{1,3,2,0:T(8,128)(2,1)S(1)}, bf16[2,128,3,64]{1,3,2,0:T(8,128)(2,1)}, u32[]{:S(2)}, u32[]{:S(2)}) collective-permute-start(bf16[2,128,3,64]{1,3,2,0:T(8,128)(2,1)S(1)} %copy.243), channel_id=1, source_target_pairs={{0,4},{4,8},{8,12},{12,16},{16,20},{20,24},{24,28},{1,5},{5,9},{9,... | collective-permute-start | bytes 294920 | tf_op jit(solution)/shard_map/while/body/eval_jaxpr/ppermute | solution.py:23
  633.8 18.4 %collective-permute-start.4 = (bf16[2,128,3,64]{1,3,2,0:T(8,128)(2,1)S(1)}, bf16[2,128,3,64]{1,3,2,0:T(8,128)(2,1)}, u32[]{:S(2)}, u32[]{:S(2)}) collective-permute-start(bf16[2,128,3,64]{1,3,2,0:T(8,128)(2,1)S(1)} %copy.243), channel_id=1, source_target_pairs={{0,4},{4,8},{8,12},{12,16},{16,20},{20,24},{24,28},{1,5},{5,9},{9,... | collective-permute-start | bytes 294920 | tf_op jit(solution)/shard_map/while/body/eval_jaxpr/ppermute | solution.py:23
  653.2 19.0 %collective-permute-start.4 = (bf16[2,128,3,64]{1,3,2,0:T(8,128)(2,1)S(1)}, bf16[2,128,3,64]{1,3,2,0:T(8,128)(2,1)}, u32[]{:S(2)}, u32[]{:S(2)}) collective-permute-start(bf16[2,128,3,64]{1,3,2,0:T(8,128)(2,1)S(1)} %copy.243), channel_id=1, source_target_pairs={{0,4},{4,8},{8,12},{12,16},{16,20},{20,24},{24,28},{1,5},{5,9},{9,... | collective-permute-start | bytes 294920 | tf_op jit(solution)/shard_map/while/body/eval_jaxpr/ppermute | solution.py:23
  705.7 85.2 %reduce-scatter.16.cloned.1.call-start = ((), (), s32[]{:S(2)}) async-start(), calls=%async_computation.9 | async-start | bytes 884736
  709.0 134.6 %reduce-scatter.14.cloned.1.call-start = ((), (), s32[]{:S(2)}) async-start(), calls=%async_computation.8 | async-start | bytes 2211840
  720.6 195.5 %reduce-scatter.10.cloned.1.call-start = ((), (), s32[]{:S(2)}) async-start(), calls=%async_computation.6 | async-start | bytes 2654208 | tf_op jit(solution)/shard_map/reduce_scatter | solution.py:336
  724.1 264.3 %reduce-scatter.12.cloned.1.call-start = ((), (), s32[]{:S(2)}) async-start(), calls=%async_computation.7 | async-start | bytes 2654208 | tf_op jit(solution)/shard_map/reduce_scatter | solution.py:337
  (168 other events, 1927.4 us)
Sparse Core Ops, SparseCore 0:
  279.7 30.8 all-reduce.19
  369.1 32.0 all-reduce.17
  705.8 39.4 all-reduce.15
Sparse Core Ops, SparseCore 1:
  282.2 38.7 all-gather.3
  323.1 40.0 all-gather.5
  709.5 64.2 reduce-scatter.15
  777.7 65.9 reduce-scatter.13
  847.7 68.2 reduce-scatter.9
  920.1 68.2 reduce-scatter.11
where the time goes:
time: 999 us; the launch traced here: 996 us
  waiting for transfers between devices  383 us (38%)
  blocking collectives  276 us (28%)
  starting transfers between devices  118 us (12%)
  matrix products  92 us (9%)
  local copies, waits for them, and re-layouts  52.7 us (5%)
  other arithmetic  52.7 us (5%)
  between operations  19 us (2%)
    ppermute x32, starting transfers between devices, shifted(): return lax.ppermute(array, axis, pairs)  77.6 us
    reduce_scatter x1, waiting for transfers between devices, shards(): lax.psum_scatter(summed[5], 'seq', scatter_dimension=1, tiled=True)  72.4 us
    reduce_scatter x1, waiting for transfers between devices, shards(): lax.psum_scatter(summed[4], 'seq', scatter_dimension=0, tiled=True)  70.5 us
    ppermute x32, waiting for transfers between devices, passed_along(): return lax.ppermute(block, axis, route)  64 us
    all_gather x2, blocking collectives, attend_forward(): value_piece = lax.all_gather(values_here, 'seq', axis=1, tiled=True)  60.4 us
    all_gather x2, blocking collectives, attend_forward(): key_piece = lax.all_gather(keys_here, 'seq', axis=1, tiled=True)  60.1 us
    unnamed x2, blocking collectives  58.7 us
    unnamed x11, waiting for transfers between devices  52.3 us
  transfers between devices with their start and end apart: 73, of which 36 were waited for; matrix products, arithmetic and copies ran while one was open for 16% of the time, Pallas kernels for 0%

commit v1 on v0

--- a/solution.py
+++ b/solution.py
@@ -1,6 +1,11 @@
+import functools
+
 import jax
 import jax.numpy as jnp
+import numpy as np
 from jax import lax
+from jax.experimental import pallas as pl
+from jax.experimental.pallas import tpu as pltpu
 from jax.sharding import PartitionSpec as P
 
 HEAD_DIM = 64
@@ -284,7 +289,7 @@
     )
 
 
-def shards(
+def ring_shards(
     short_input,
     long_input,
     short_cotangent,
@@ -352,6 +357,884 @@
     )
 
 
+LANES = 128
+NT = (((1,), (1,)), ((), ()))
+TN = (((0,), (0,)), ((), ()))
+F32 = jnp.float32
+BF16 = jnp.bfloat16
+
+
+def dot(a, b, dims=(((1,), (0,)), ((), ()))):
+    return lax.dot_general(a, b, dims, preferred_element_type=F32)
+
+
+def in_vmem(body, outs, scalars, arrays, scratch=(), limit_mib=16):
+    return pl.pallas_call(
+        body,
+        out_shape=[
+            pltpu.HBM(*out[:2]) if len(out) == 3 else jax.ShapeDtypeStruct(*out) for out in outs
+        ],
+        in_specs=[pl.BlockSpec(memory_space=pltpu.SMEM)] * len(scalars)
+        + [pl.BlockSpec(memory_space=pltpu.VMEM)] * len(arrays),
+        out_specs=[pl.BlockSpec(memory_space=pltpu.VMEM)] * len(outs),
+        scratch_shapes=[pltpu.VMEM(shape, kind) for shape, kind in scratch],
+        compiler_params=pltpu.CompilerParams(vmem_limit_bytes=limit_mib * 1024 * 1024),
+        cost_estimate=pl.CostEstimate(flops=0, bytes_accessed=0, transcendentals=0),
+    )(*scalars, *arrays)
+
+
+def far(*arrays):
+    return tuple(pltpu.with_memory_space_constraint(array, pltpu.HBM) for array in arrays)
+
+
+def after(array, *others):
+    return lax.optimization_barrier((array, *others))[0]
+
+
+def exchange(array, axis, mask):
+    size = lax.axis_size(axis)
+    return lax.ppermute(array, axis, [(i, i ^ mask) for i in range(size)])
+
+
+def add_low(a, b):
+    return (a.astype(F32) + b.astype(F32)).astype(BF16)
+
+
+def shift_back(rows, by):
+    index = lax.broadcasted_iota(jnp.int32, rows.shape, 0)
+    return jnp.where(index >= by, pltpu.roll(rows, by, axis=0), 0.0)
+
+
+def shift_ahead(rows, by):
+    count = rows.shape[0]
+    index = lax.broadcasted_iota(jnp.int32, rows.shape, 0)
+    return jnp.where(index < count - by, pltpu.roll(rows, count - by, axis=0), 0.0)
+
+
+def fold(rows):
+    half = rows.shape[0] // 2
+    return jnp.concatenate([rows[:half], rows[half:]], axis=1)
+
+
+def unfold(rows):
+    return jnp.concatenate([rows[:, :HEAD_DIM], rows[:, HEAD_DIM:]], axis=0)
+
+
+def pack_proj_body(proj, gain, packed):
+    rows = proj.shape[1]
+    for c in range(3):
+        packed[c * rows : (c + 1) * rows, :] = proj[c, :, :LANES]
+    narrow = jnp.concatenate([proj[c, :, LANES:] for c in range(3)], axis=0)
+    packed[3 * rows : 9 * rows // 2, :] = fold(narrow)
+    gain_row = gain[...].astype(F32).reshape(1, rows)
+    gain_row = jnp.concatenate([gain_row, jnp.zeros((1, LANES - rows), F32)], axis=1)
+    packed[9 * rows // 2 :, :] = jnp.broadcast_to(gain_row, (16, LANES)).astype(BF16)
+
+
+def unpack_proj(packed, rows):
+    narrow = unfold(packed[3 * rows : 9 * rows // 2, :])
+    return [
+        (packed[c * rows : (c + 1) * rows, :], narrow[c * rows : (c + 1) * rows, :])
+        for c in range(3)
+    ]
+
+
+def narrow_pack(block, store):
+    groups = block.shape[0] // 16
+    for g in range(groups):
+        rows = block[16 * g : 16 * g + 16, :]
+        store(0, LANES * g, rows[:, :LANES])
+        tail = rows[:, LANES:]
+        store(16, LANES * g, jnp.concatenate([tail, jnp.zeros_like(tail)], axis=1))
+
+
+def pack_ffn_body(up, down, out, gain, packed):
+    rows = up.shape[0]
+    gain_column = gain[...].astype(F32).reshape(1, rows).T
+    packed[:rows, :] = (up[...].astype(F32) * gain_column).astype(BF16)
+    packed[rows : 2 * rows, :] = down[...]
+
+    def store(row, lane, value):
+        packed[2 * rows + row : 2 * rows + row + 16, lane : lane + LANES] = value
+
+    narrow_pack(out[...].astype(F32).T.astype(BF16), store)
+
+
+def place_ffn_body(place, *refs):
+    parts = refs[:8]
+    up, down, out = refs[8:]
+    rows = up.shape[0] // 8
+    for i in range(8):
+        first = pl.multiple_of(jnp.bitwise_xor(place[0], i) * rows, rows)
+        part = parts[i]
+        up[pl.ds(first, rows), :] = part[:rows, :]
+        down[pl.ds(first, rows), :] = part[rows : 2 * rows, :]
+        for g in range(rows // 16):
+            at = pl.ds(pl.multiple_of(first + 16 * g, 16), 16)
+            lanes = slice(LANES * g, LANES * g + LANES)
+            out[at, :LANES] = part[2 * rows : 2 * rows + 16, lanes]
+            out[at, LANES:] = part[2 * rows + 16 : 2 * rows + 32, LANES * g : LANES * g + HEAD_DIM]
+
+
+def project_body(place, *refs):
+    parts = refs[:8]
+    long_in, short_in, taps, send, normed, weight, gain, gain_rows = refs[8:]
+    seqs, long_rows, _ = long_in.shape
+    rows = long_rows + short_in.shape[1]
+    for i in range(8):
+        packed = parts[i][...]
+        shard = weight.shape[1] // 8
+        owner = jnp.bitwise_xor(place[0], i)
+        gain_rows[pl.ds(owner, 1), :] = packed[9 * shard // 2 :, :].astype(F32)[:1]
+        first = pl.multiple_of(owner * shard, shard)
+        for c, (wide, narrow) in enumerate(unpack_proj(packed, shard)):
+            weight[c, pl.ds(first, shard), :LANES] = wide
+            weight[c, pl.ds(first, shard), LANES:] = narrow
+    gain[...] = jnp.concatenate([gain_rows[j : j + 1, :shard] for j in range(8)], axis=1)
+    for b in range(seqs):
+        values = jnp.concatenate([long_in[b], short_in[b]], axis=0).astype(F32)
+        root = lax.rsqrt(jnp.mean(values * values, axis=-1, keepdims=True) + norm_eps)
+        normed[b * rows : (b + 1) * rows, :] = (values * root * gain[...]).astype(BF16)
+    mixed = [dot(normed[...], weight[c]).astype(BF16) for c in range(3)]
+    tap_rows = jnp.concatenate(
+        [taps[...], jnp.zeros((16 - taps.shape[0], taps.shape[1]), BF16)], axis=0
+    )
+    tap_rows = jnp.concatenate(
+        [tap_rows, jnp.zeros((16, LANES - taps.shape[1]), BF16)], axis=1
+    )
+    half = rows // 2
+    for dest in range(8):
+        if dest < 3 * seqs:
+            e, b = dest // seqs, dest % seqs
+            lanes = slice(e * HEAD_DIM, (e + 1) * HEAD_DIM)
+            q, k, v = [m[b * rows : (b + 1) * rows, lanes] for m in mixed]
+            send[dest, :rows, :] = jnp.concatenate([k, v], axis=1)
+            send[dest, rows : rows + half, :] = fold(q)
+        else:
+            send[dest, : rows + half, :] = jnp.zeros((rows + half, LANES), BF16)
+        send[dest, rows + half :, :] = tap_rows
+
+
+def head_taps(place, came, rows, seqs):
+    first = rows + rows // 2
+    width = 3 * HEAD_DIM // 8
+    whole = jnp.concatenate(
+        [came[j, first:, :].astype(F32)[:, :width] for j in range(8)], axis=1
+    )
+    e = place[0] // seqs
+    mine = whole[:, :HEAD_DIM]
+    for other in (1, 2):
+        mine = jnp.where(
+            e == other, whole[:, other * HEAD_DIM : (other + 1) * HEAD_DIM], mine
+        )
+    taps_q = [mine[m : m + 1, :] for m in range(3)]
+    taps_kv = [
+        jnp.concatenate([mine[3 + m : 4 + m, :], mine[6 + m : 7 + m, :]], axis=1) for m in range(3)
+    ]
+    return taps_q, taps_kv
+
+
+def own_pair(came, long_rows, rows):
+    q_rows = [unfold(came[j, rows : rows + rows // 2, :]) for j in range(8)]
+    result = []
+    for part in (slice(0, long_rows), slice(long_rows, rows)):
+        q = jnp.concatenate([piece[part] for piece in q_rows], axis=0).astype(F32)
+        kv = jnp.concatenate([came[j, part, :] for j in range(8)], axis=0).astype(F32)
+        result.append((q, kv))
+    return result
+
+
+def convolve(rows, taps):
+    return taps[0] * rows + taps[1] * shift_back(rows, 1) + taps[2] * shift_back(rows, 2)
+
+
+def attend_body(
+    long_rows, seqs, place, long_lengths, short_lengths, came, send, q_all, kv_all, att_t, log_row, kept
+):
+    rows = (came.shape[1] - 16) * 2 // 3
+    kept[...] = came[...]
+    taps_q, taps_kv = head_taps(place, came, rows, seqs)
+    b = place[0] % seqs
+    first = 0
+    results = []
+    for lengths, (q_mixed, kv_mixed) in zip(
+        (long_lengths, short_lengths), own_pair(came, long_rows, rows)
+    ):
+        count = q_mixed.shape[0]
+        block = min(256, count)
+        length = lengths[b]
+        q = (convolve(q_mixed, taps_q).astype(BF16).astype(F32) * HEAD_DIM ** (-0.5)).astype(BF16)
+        kv = convolve(kv_mixed, taps_kv).astype(BF16)
+        kv_t = kv.astype(F32).T.astype(BF16)
+        q_all[first : first + count, :] = q
+        kv_all[first : first + count, :] = kv
+        k = kv[:, :HEAD_DIM]
+        v_t = kv_t[HEAD_DIM:, :]
+        pieces = []
+        for start in range(0, count, block):
+            stop = start + block
+            scores = dot(k[:stop], q[start:stop], NT)
+            key_pos = lax.broadcasted_iota(jnp.int32, scores.shape, 0)
+            query_pos = lax.broadcasted_iota(jnp.int32, scores.shape, 1) + start
+            allowed = jnp.logical_and(key_pos <= query_pos, key_pos < length)
+            scores = jnp.where(allowed, scores, mask_fill)
+            top = jnp.max(scores, axis=0, keepdims=True)
+            terms = jnp.exp(scores - top)
+            total = jnp.sum(terms, axis=0, keepdims=True)
+            out_t = dot(v_t[:, :stop], terms.astype(BF16)) / total
+            att_t[:, first + start : first + stop] = out_t
+            log_row[:, first + start : first + stop] = top + jnp.log(total)
+            pieces.append(out_t.T.astype(BF16))
+        results.append(jnp.concatenate(pieces, axis=0))
+        first += count
+    short_rows = rows - long_rows
+    for j in range(8):
+        mine = jnp.concatenate(
+            [
+                results[0][j * long_rows : (j + 1) * long_rows],
+                results[1][j * short_rows : (j + 1) * short_rows],
+            ],
+            axis=0,
+        )
+        send[j, :, :] = fold(mine)
+
+
+def pair_rows(came, seqs):
+    columns = []
+    for e in range(3):
+        columns.append(
+            jnp.concatenate([unfold(came[seqs * e + b]) for b in range(seqs)], axis=0)
+        )
+    return jnp.concatenate(columns, axis=1)
+
+
+def feed_body(
+    long_rows,
+    place,
+    long_lengths,
+    short_lengths,
+    att_0,
+    att_1,
+    att_2,
+    att_3,
+    out_0,
+    out_1,
+    out_2,
+    out_3,
+    long_in,
+    short_in,
+    long_cot,
+    short_cot,
+    up,
+    down,
+    mid_ref,
+    normed_ref,
+    squared_ref,
+    grad_up_ref,
+    grad_out_ref,
+    att_ref,
+    keep,
+    send,
+    scratch,
+    sums,
+):
+    seqs = long_in.shape[0]
+    rows = long_rows + short_in.shape[1]
+    att_ref[...] = pair_rows(att_0, seqs)
+    sums[place[1]] = dot(att_ref[...], out_0[...], NT)
+    for i, att, out in ((1, att_1, out_1), (2, att_2, out_2), (3, att_3, out_3)):
+        sums[jnp.bitwise_xor(place[1], i)] = dot(pair_rows(att, seqs), out[...], NT)
+    for b in range(seqs):
+        at = slice(b * rows, (b + 1) * rows)
+        residual = jnp.concatenate([long_in[b], short_in[b]], axis=0).astype(F32)
+        mid = residual + ((sums[0, at, :] + sums[1, at, :]) + (sums[2, at, :] + sums[3, at, :]))
+        mid_ref[at, :] = mid
+        root = lax.rsqrt(jnp.mean(mid * mid, axis=-1, keepdims=True) + norm_eps)
+        normed_ref[at, :] = (mid * root).astype(BF16)
+        for cot, lengths, first, count in (
+            (long_cot, long_lengths, b * rows, long_rows),
+            (short_cot, short_lengths, b * rows + long_rows, rows - long_rows),
+        ):
+            value = cot[b]
+            position = lax.broadcasted_iota(jnp.int32, value.shape, 0) + place[0] * count
+            grad_out_ref[first : first + count, :] = jnp.where(
+                position < lengths[b], value.astype(F32), 0.0
+            ).astype(BF16)
+    relu = jnp.maximum(dot(normed_ref[...], up[...]), 0.0)
+    squared_ref[...] = (relu * relu).astype(BF16)
+    grad_squared = dot(grad_out_ref[...], down[...])
+    grad_up_ref[...] = (grad_squared * 2.0 * relu).astype(BF16)
+    scratch[...] = dot(grad_up_ref[...], up[...], NT).astype(BF16)
+    split_halves(place, scratch, keep, send)
+
+
+def split_halves(place, whole, keep, send):
+    half = whole.shape[0] // 2
+    core = place[1] % 2
+    keep[...] = whole[pl.ds(pl.multiple_of(core * half, half), half), :]
+    send[...] = whole[pl.ds(pl.multiple_of((1 - core) * half, half), half), :]
+
+
+def join_halves(place, whole, own, other):
+    half = own.shape[0]
+    core = place[1] % 2
+    whole[pl.ds(pl.multiple_of(core * half, half), half), :] = own[...].astype(whole.dtype)
+    whole[pl.ds(pl.multiple_of((1 - core) * half, half), half), :] = other[...].astype(whole.dtype)
+
+
+def split_y(place, blocks, keep, send):
+    y = place[0] % 2
+    for z in range(4):
+        keep[z] = blocks[2 * z + y]
+        send[z] = blocks[2 * z + 1 - y]
+
+
+def feed_terms_body(
+    place, normed, squared, grad_up, grad_out, down, f_keep, f_send, keep, send, scratch, blocks
+):
+    scratch[...] = dot(squared[...], down[...], NT).astype(BF16)
+    split_halves(place, scratch, f_keep, f_send)
+    rows = down.shape[0] // 8
+    up_term = dot(normed[...], grad_up[...], TN).astype(BF16)
+    down_term = dot(grad_out[...], squared[...], TN).astype(BF16)
+    for s in range(8):
+        blocks[s, :rows, :] = up_term[s * rows : (s + 1) * rows]
+        blocks[s, rows:, :] = down_term[s * rows : (s + 1) * rows]
+    split_y(place, blocks, keep, send)
+
+
+def middle_body(place, own, other, mid_ref, grad_out, out, grad_mid_ref, low_ref, send, scratch):
+    join_halves(place, scratch, own, other)
+    seqs = 2
+    rows = mid_ref.shape[0] // seqs
+    for b in range(seqs):
+        at = slice(b * rows, (b + 1) * rows)
+        mid = mid_ref[at, :]
+        weighted = scratch[at, :]
+        root = lax.rsqrt(jnp.mean(mid * mid, axis=-1, keepdims=True) + norm_eps)
+        inner = jnp.mean(weighted * mid, axis=-1, keepdims=True)
+        grad_mid = grad_out[at, :].astype(F32) + (
+            root * weighted - mid * (root * root * root * inner)
+        )
+        grad_mid_ref[at, :] = grad_mid
+        low_ref[at, :] = grad_mid.astype(BF16)
+    grad_att = dot(low_ref[...], out[...]).astype(BF16)
+    for dest in range(8):
+        if dest < 3 * seqs:
+            e, b = dest // seqs, dest % seqs
+            send[dest] = fold(
+                grad_att[b * rows : (b + 1) * rows, e * HEAD_DIM : (e + 1) * HEAD_DIM]
+            )
+        else:
+            send[dest] = jnp.zeros_like(send[dest])
+
+
+def out_term_body(place, low, att, keep, send, blocks):
+    term = dot(low[...], att[...], TN).astype(BF16)
+    rows = term.shape[0] // 8
+    for s in range(8):
+
+        def store(row, lane, value):
+            blocks[s, row : row + 16, lane : lane + LANES] = value
+
+        narrow_pack(term[s * rows : (s + 1) * rows], store)
+    split_y(place, blocks, keep, send)
+
+
+def attend_back_body(
+    long_rows,
+    seqs,
+    place,
+    long_lengths,
+    short_lengths,
+    came,
+    q_all,
+    kv_all,
+    att_t,
+    log_row,
+    grad_came,
+    send,
+):
+    rows = (came.shape[1] - 16) * 2 // 3
+    short_rows = rows - long_rows
+    taps_q, taps_kv = head_taps(place, came, rows, seqs)
+    b = place[0] % seqs
+    e = place[0] // seqs
+    grads = [unfold(grad_came[j]) for j in range(8)]
+    first = 0
+    terms_q = [0.0, 0.0, 0.0]
+    terms_kv = [0.0, 0.0, 0.0]
+    results = []
+    for lengths, part, (q_mixed, kv_mixed) in zip(
+        (long_lengths, short_lengths),
+        (slice(0, long_rows), slice(long_rows, rows)),
+        own_pair(came, long_rows, rows),
+    ):
+        count = q_mixed.shape[0]
+        block = min(256, count)
+        length = lengths[b]
+        at = slice(first, first + count)
+        grad = jnp.concatenate([g[part] for g in grads], axis=0)
+        q = q_all[at, :]
+        kv = kv_all[at, :]
+        kv_t = kv.astype(F32).T.astype(BF16)
+        delta = jnp.sum(grad.astype(F32).T * att_t[:, at], axis=0, keepdims=True)
+        log_total = log_row[:, at]
+        k, v = kv[:, :HEAD_DIM], kv[:, HEAD_DIM:]
+        k_t = kv_t[:HEAD_DIM, :]
+        grad_q = None
+        grad_kv = []
+        for start in range(0, count, block):
+            stop = start + block
+            scores = dot(k[start:stop], q[start:], NT)
+            key_pos = lax.broadcasted_iota(jnp.int32, scores.shape, 0)
+            query_pos = lax.broadcasted_iota(jnp.int32, scores.shape, 1)
+            allowed = jnp.logical_and(key_pos <= query_pos, key_pos + start < length)
+            prob = jnp.where(allowed, jnp.exp(scores - log_total[:, start:]), 0.0)
+            grad_prob = dot(v[start:stop], grad[start:], NT)
+            grad_scores = (prob * (grad_prob - delta[:, start:])).astype(BF16)
+            grad_k = dot(grad_scores, q[start:])
+            grad_v = dot(prob.astype(BF16), grad[start:])
+            grad_kv.append(jnp.concatenate([grad_k, grad_v], axis=1))
+            part_q = dot(k_t[:, start:stop], grad_scores)
+            if start == 0:
+                grad_q = part_q
+            else:
+                grad_q = jnp.concatenate(
+                    [grad_q[:, :start], grad_q[:, start:] + part_q], axis=1
+                )
+        grad_q = grad_q.T * HEAD_DIM ** (-0.5)
+        grad_kv = jnp.concatenate(grad_kv, axis=0)
+        pair = []
+        for grad_conv, mixed, taps, terms in (
+            (grad_q, q_mixed, taps_q, terms_q),
+            (grad_kv, kv_mixed, taps_kv, terms_kv),
+        ):
+            for m in range(3):
+                back = mixed if m == 0 else shift_back(mixed, m)
+                terms[m] = terms[m] + jnp.sum(grad_conv * back, axis=0, keepdims=True)
+            pair.append(
+                (
+                    taps[0] * grad_conv
+                    + taps[1] * shift_ahead(grad_conv, 1)
+                    + taps[2] * shift_ahead(grad_conv, 2)
+                ).astype(BF16)
+            )
+        results.append(pair)
+        first += count
+    table = jnp.concatenate(
+        terms_q
+        + [t[:, :HEAD_DIM] for t in terms_kv]
+        + [t[:, HEAD_DIM:] for t in terms_kv]
+        + [jnp.zeros((7, HEAD_DIM), F32)],
+        axis=0,
+    )
+    table = jnp.concatenate([jnp.where(e == i, table, 0.0) for i in range(3)], axis=1)
+    width = 3 * HEAD_DIM // 8
+    for j in range(8):
+        mine = [
+            jnp.concatenate(
+                [
+                    results[0][i][j * long_rows : (j + 1) * long_rows],
+                    results[1][i][j * short_rows : (j + 1) * short_rows],
+                ],
+                axis=0,
+            )
+            for i in range(2)
+        ]
+        send[j, :rows, :] = mine[1]
+        send[j, rows : rows + rows // 2, :] = fold(mine[0])
+        send[j, rows + rows // 2 :, :] = jnp.concatenate(
+            [table[:, j * width : (j + 1) * width], jnp.zeros((16, LANES - width), F32)], axis=1
+        ).astype(BF16)
+
+
+def project_back_body(
+    place, came, normed, weight, keep, send, keep_w, send_w, taps, scratch, grad_mixed, blocks
+):
+    seqs = 2
+    rows = (came.shape[1] - 16) * 2 // 3
+    for e in range(3):
+        for b in range(seqs):
+            j = seqs * e + b
+            at = slice(b * rows, (b + 1) * rows)
+            lanes = slice(e * HEAD_DIM, (e + 1) * HEAD_DIM)
+            grad_mixed[0, at, lanes] = unfold(came[j, rows : rows + rows // 2, :])
+            grad_mixed[1, at, lanes] = came[j, :rows, :HEAD_DIM]
+            grad_mixed[2, at, lanes] = came[j, :rows, HEAD_DIM:]
+    total = came[0, rows + rows // 2 :, :].astype(F32)
+    for j in range(1, 3 * seqs):
+        total = total + came[j, rows + rows // 2 :, :].astype(F32)
+    taps[...] = total[: taps.shape[0], : taps.shape[1]]
+    shard = weight.shape[1] // 8
+    terms = [dot(normed[...], grad_mixed[c], TN).astype(BF16) for c in range(3)]
+    for s in range(8):
+        at = slice(s * shard, (s + 1) * shard)
+        for c in range(3):
+            blocks[s, c * shard : (c + 1) * shard, :] = terms[c][at, :LANES]
+        blocks[s, 3 * shard :, :] = fold(
+            jnp.concatenate([terms[c][at, LANES:] for c in range(3)], axis=0)
+        )
+    split_y(place, blocks, keep, send)
+    total = dot(grad_mixed[0], weight[0], NT)
+    for c in (1, 2):
+        total = total + dot(grad_mixed[c], weight[c], NT)
+    scratch[...] = total.astype(BF16)
+    split_halves(place, scratch, keep_w, send_w)
+
+
+def input_grad_body(
+    place, own, other, grad_mid, gain, long_in, short_in, long_out, short_out, scratch
+):
+    join_halves(place, scratch, own, other)
+    seqs, long_rows, _ = long_in.shape
+    rows = long_rows + short_in.shape[1]
+    for b in range(seqs):
+        at = slice(b * rows, (b + 1) * rows)
+        values = jnp.concatenate([long_in[b], short_in[b]], axis=0).astype(F32)
+        weighted = scratch[at, :] * gain[...]
+        root = lax.rsqrt(jnp.mean(values * values, axis=-1, keepdims=True) + norm_eps)
+        inner = jnp.mean(weighted * values, axis=-1, keepdims=True)
+        grad = grad_mid[at, :] + (root * weighted - values * (root * root * root * inner))
+        long_out[b] = grad[:long_rows]
+        short_out[b] = grad[long_rows:]
+
+
+def scatter_z_body(place, *refs):
+    count = (len(refs) - 4) // 2
+    outs = refs[2 * count :]
+    z = place[0] // 2
+    for i in range(4):
+        block = jnp.bitwise_xor(z, i)
+        first = 0
+        for a in range(count):
+            keep, came = refs[2 * a], refs[2 * a + 1]
+            rows = keep.shape[1]
+            outs[i][first : first + rows, :] = (
+                keep[block].astype(F32) + came[block].astype(F32)
+            ).astype(BF16)
+            first += rows
+
+
+def sum_blocks(blocks):
+    return (blocks[0][...].astype(F32) + blocks[1][...].astype(F32)) + (
+        blocks[2][...].astype(F32) + blocks[3][...].astype(F32)
+    )
+
+
+def proj_grad_body(b0, b1, b2, b3, proj, gain, grad, gain_grad):
+    total = sum_blocks((b0, b1, b2, b3))
+    rows = proj.shape[1]
+    column = 0.0
+    for c, (wide, narrow) in enumerate(unpack_proj(total, rows)):
+        term = jnp.concatenate([wide, narrow], axis=1)
+        column = column + jnp.sum(term * proj[c].astype(F32), axis=1, keepdims=True)
+        grad[c] = term
+    gain_grad[...] = column.T / gain[...].astype(F32).reshape(1, rows)
+
+
+def ffn_grad_body(b0, b1, b2, b3, up, gain, up_grad, down_grad, out_grad, gain_grad):
+    total = sum_blocks((b0, b1, b2, b3))
+    rows = up.shape[0]
+    raw = total[:rows]
+    gain_grad[...] = jnp.sum(raw * up[...].astype(F32), axis=1, keepdims=True).T
+    up_grad[...] = raw * gain[...].astype(F32).reshape(1, rows).T
+    down_grad[...] = total[rows : 2 * rows]
+    wide = total[2 * rows : 2 * rows + 16]
+    narrow = total[2 * rows + 16 :]
+    out = jnp.concatenate(
+        [
+            jnp.concatenate(
+                [
+                    wide[:, LANES * g : LANES * (g + 1)],
+                    narrow[:, LANES * g : LANES * g + HEAD_DIM],
+                ],
+                axis=1,
+            )
+            for g in range(rows // 16)
+        ],
+        axis=0,
+    )
+    out_grad[...] = out.T
+
+
+def pair_shards(
+    short_input,
+    long_input,
+    short_cotangent,
+    long_cotangent,
+    short_lengths,
+    long_lengths,
+    proj_weight,
+    out_weight,
+    conv_taps,
+    attention_gain,
+    up_weight,
+    down_weight,
+    feed_gain,
+):
+    seqs, long_rows, width = long_input.shape
+    short_rows = short_input.shape[1]
+    rows = long_rows + short_rows
+    tokens = seqs * rows
+    shard = proj_weight.shape[1]
+    local = proj_weight.shape[2]
+    hidden = up_weight.shape[1]
+    long_len, short_len = 8 * long_rows, 8 * short_rows
+    total_len = long_len + short_len
+    place = jnp.stack([lax.axis_index("seq"), lax.axis_index("head")]).astype(jnp.int32)
+    packed_rows = shard * 9 // 2
+    chunk = rows + rows // 2 + 16
+    down_t = down_weight.T
+
+    (proj_packed,) = in_vmem(
+        pack_proj_body, [((packed_rows + 16, LANES), BF16)], (), (proj_weight, attention_gain)
+    )
+    proj_z = [proj_packed] + [exchange(proj_packed, "seq", mask) for mask in (2, 4, 6)]
+    proj_parts = []
+    for piece in proj_z:
+        proj_parts += [piece, exchange(piece, "seq", 1)]
+    (ffn_packed,) = in_vmem(
+        pack_ffn_body,
+        [((2 * shard + 32, hidden), BF16)],
+        (),
+        far(up_weight, down_t, out_weight) + (feed_gain,),
+    )
+    send, normed, proj_full, gain = in_vmem(
+        project_body,
+        [
+            ((8, chunk, LANES), BF16),
+            ((tokens, width), BF16, "far"),
+            ((3, width, local), BF16, "far"),
+            ((1, width), F32, "far"),
+        ],
+        (place,),
+        (*proj_parts, *far(long_input, short_input, conv_taps)),
+        scratch=[((8, LANES), F32)],
+    )
+    came = lax.all_to_all(send, "seq", 0, 0, tiled=True)
+    ffn_0 = after(ffn_packed, *proj_z)
+    ffn_2 = exchange(ffn_0, "seq", 2)
+    ffn_4 = exchange(ffn_0, "seq", 4)
+    ffn_1 = exchange(ffn_0, "seq", 1)
+    att_send, q_all, kv_all, att_t, log_row, mixed = in_vmem(
+        functools.partial(attend_body, long_rows, seqs),
+        [
+            ((8, rows // 2, LANES), BF16),
+            ((total_len, HEAD_DIM), BF16, "far"),
+            ((total_len, 2 * HEAD_DIM), BF16, "far"),
+            ((HEAD_DIM, total_len), F32, "far"),
+            ((1, total_len), F32, "far"),
+            ((8, chunk, LANES), BF16, "far"),
+        ],
+        (place, long_lengths, short_lengths),
+        (came,),
+    )
+    att_0 = lax.all_to_all(att_send, "seq", 0, 0, tiled=True)
+    ffn_2, ffn_4 = after(ffn_2, att_send), after(ffn_4, att_send)
+    ffn_6 = exchange(ffn_4, "seq", 2)
+    ffn_3 = exchange(ffn_2, "seq", 1)
+    ffn_5 = exchange(ffn_4, "seq", 1)
+    ffn_7 = exchange(ffn_6, "seq", 1)
+    up_full, down_full, out_full = in_vmem(
+        place_ffn_body,
+        [
+            ((width, hidden), BF16, "far"),
+            ((width, hidden), BF16, "far"),
+            ((width, local), BF16, "far"),
+        ],
+        (place,),
+        far(ffn_0, ffn_1, ffn_2, ffn_3, ffn_4, ffn_5, ffn_6, ffn_7),
+    )
+    out_2 = exchange(out_full, "head", 2)
+    out_1 = exchange(out_full, "head", 1)
+    out_3 = exchange(out_2, "head", 1)
+    att_2 = exchange(att_0, "head", 2)
+    att_1 = exchange(att_0, "head", 1)
+    att_3 = exchange(att_2, "head", 1)
+    mid, normed_ffn, squared, grad_up, grad_out, att, keep, send = in_vmem(
+        functools.partial(feed_body, long_rows),
+        [
+            ((tokens, width), F32, "far"),
+            ((tokens, width), BF16, "far"),
+            ((tokens, hidden), BF16, "far"),
+            ((tokens, hidden), BF16, "far"),
+            ((tokens, width), BF16, "far"),
+            ((tokens, local), BF16, "far"),
+            ((tokens // 2, width), BF16),
+            ((tokens // 2, width), BF16),
+        ],
+        (place, long_lengths, short_lengths),
+        (att_0, att_1, att_2, att_3)
+        + far(
+            out_full,
+            out_1,
+            out_2,
+            out_3,
+            long_input,
+            short_input,
+            long_cotangent,
+            short_cotangent,
+            up_full,
+            down_full,
+        ),
+        scratch=[((tokens, width), BF16), ((4, tokens, width), F32)],
+        limit_mib=32,
+    )
+    half = add_low(keep, exchange(send, "head", 1))
+    f_keep, f_send, ffn_keep, ffn_send = in_vmem(
+        feed_terms_body,
+        [
+            ((tokens // 2, width), BF16, "far"),
+            ((tokens // 2, width), BF16, "far"),
+            ((4, 2 * shard, hidden), BF16, "far"),
+            ((4, 2 * shard, hidden), BF16, "far"),
+        ],
+        (place,),
+        far(normed_ffn, squared, grad_up, grad_out, down_full),
+        scratch=[((tokens, width), BF16), ((8, 2 * shard, hidden), BF16)],
+        limit_mib=32,
+    )
+    ffn_came = exchange(ffn_send, "seq", 1)
+    own = add_low(half, after(exchange(half, "head", 2), ffn_send))
+    other = exchange(own, "head", 1)
+    grad_mid, grad_mid_low, send = in_vmem(
+        middle_body,
+        [
+            ((tokens, width), F32, "far"),
+            ((tokens, width), BF16, "far"),
+            ((8, rows // 2, LANES), BF16),
+        ],
+        (place,),
+        (own, other) + far(mid, grad_out, out_full),
+        scratch=[((tokens, width), F32)],
+    )
+    grad_came = lax.all_to_all(send, "seq", 0, 0, tiled=True)
+    out_keep, out_send = in_vmem(
+        out_term_body,
+        [((4, 32, hidden), BF16, "far"), ((4, 32, hidden), BF16, "far")],
+        (place,),
+        far(grad_mid_low, att),
+        scratch=[((8, 32, hidden), BF16)],
+    )
+    out_came = exchange(out_send, "seq", 1)
+    f_half = add_low(f_keep, exchange(f_send, "head", 1))
+    f_own = add_low(f_half, exchange(f_half, "head", 2))
+    f_other = exchange(f_own, "head", 1)
+    (send,) = in_vmem(
+        functools.partial(attend_back_body, long_rows, seqs),
+        [((8, chunk, LANES), BF16)],
+        (place, long_lengths, short_lengths),
+        far(mixed, q_all, kv_all, att_t, log_row) + (after(grad_came, out_send),),
+    )
+    mixed_came = lax.all_to_all(send, "seq", 0, 0, tiled=True)
+    ffn_blocks = in_vmem(
+        scatter_z_body,
+        [((2 * shard + 32, hidden), BF16, "far")] * 4,
+        (place,),
+        far(ffn_keep, ffn_came, out_keep, out_came),
+    )
+    ffn_blocks = [ffn_blocks[0]] + [exchange(ffn_blocks[i], "seq", 2 * i) for i in (1, 2, 3)]
+    proj_keep, proj_send, keep, send, taps_grad = in_vmem(
+        project_back_body,
+        [
+            ((4, packed_rows, LANES), BF16, "far"),
+            ((4, packed_rows, LANES), BF16, "far"),
+            ((tokens // 2, width), BF16),
+            ((tokens // 2, width), BF16),
+            (conv_taps.shape, F32),
+        ],
+        (place,),
+        (mixed_came,) + far(normed, proj_full),
+        scratch=[
+            ((tokens, width), BF16),
+            ((3, tokens, local), BF16),
+            ((8, packed_rows, LANES), BF16),
+        ],
+    )
+    proj_came = exchange(proj_send, "seq", 1)
+    half = add_low(keep, exchange(send, "head", 1))
+    own = add_low(half, exchange(half, "head", 2))
+    other = exchange(own, "head", 1)
+    proj_blocks = in_vmem(
+        scatter_z_body,
+        [((packed_rows, LANES), BF16)] * 4,
+        (place,),
+        far(proj_keep) + (proj_came,),
+    )
+    proj_blocks = [proj_blocks[0]] + [exchange(proj_blocks[i], "seq", 2 * i) for i in (1, 2, 3)]
+    long_input_grad, short_input_grad = in_vmem(
+        input_grad_body,
+        [(long_input.shape, F32), (short_input.shape, F32)],
+        (place,),
+        (own, other) + far(grad_mid, gain, long_input, short_input),
+        scratch=[((tokens, width), F32)],
+    )
+    up_grad, down_grad, out_grad, feed_part = in_vmem(
+        ffn_grad_body,
+        [
+            (up_weight.shape, F32),
+            (down_t.shape, F32),
+            (out_weight.shape, F32),
+            ((1, shard), F32),
+        ],
+        (),
+        far(*ffn_blocks, up_weight) + (feed_gain,),
+    )
+    proj_grad, attention_part = in_vmem(
+        proj_grad_body,
+        [(proj_weight.shape, F32), ((1, shard), F32)],
+        (),
+        (*proj_blocks, *far(proj_weight), attention_gain),
+    )
+    gains = jnp.concatenate([attention_part, feed_part], axis=0)
+    gains = gains + exchange(gains, "head", 1)
+    gains = gains + exchange(gains, "head", 2)
+
+    f_own, f_other = f_own.astype(F32), f_other.astype(F32)
+    core = lax.axis_index("head") % 2
+    first = jnp.where(core == 0, f_own, f_other)
+    second = jnp.where(core == 0, f_other, f_own)
+    output = (mid + jnp.concatenate([first, second], axis=0)).astype(BF16)
+    output = output.reshape(seqs, rows, width)
+    return (
+        output[:, long_rows:],
+        output[:, :long_rows],
+        short_input_grad,
+        long_input_grad,
+        proj_grad,
+        out_grad,
+        taps_grad,
+        gains[0],
+        up_grad,
+        down_grad.T,
+        gains[1],
+    )
+
+
+def fits_pairs(short_input, long_input, proj_weight):
+    seqs, long_rows, _ = long_input.shape
+    short_seqs, short_rows, _ = short_input.shape
+    return (
+        lax.axis_size("seq") == 8
+        and lax.axis_size("head") == 4
+        and seqs == 2
+        and short_seqs == 2
+        and proj_weight.shape[2] == 3 * HEAD_DIM
+        and proj_weight.shape[1] % 32 == 0
+        and long_rows % 32 == 0
+        and short_rows % 32 == 0
+        and 8 * long_rows <= 2048
+    )
+
+
+def shards(short_input, long_input, *rest):
+    proj_weight = rest[4]
+    if fits_pairs(short_input, long_input, proj_weight):
+        return pair_shards(short_input, long_input, *rest)
+    return ring_shards(short_input, long_input, *rest)
+
+
 def solution(mesh):
     placed = (
         P(None, "seq", None),

time: 999 us -> 259 us (0.26)
  blocking collectives: 276 us -> 0 us
  waiting for transfers between devices: 383 us -> 133 us
  matrix products: 92 us -> 0 us
  starting transfers between devices: 118 us -> 64.2 us
  other arithmetic: 52.7 us -> 0.75 us
  Pallas kernels: 0 us -> 51.4 us
  local copies, waits for them, and re-layouts: 52.7 us -> 7.28 us
  between operations: 19 us -> 0.94 us
    all_gather x7 -> x0, blocking collectives: 218 us -> none  [the longest x2 60.4 us: attend_forward(): value_piece = lax.all_gather(values_here, 'seq', axis=1, tiled=True)]
    reduce_scatter x2 -> x0, waiting for transfers between devices: 143 us -> none  [the longest x1 72.4 us: shards(): lax.psum_scatter(summed[5], 'seq', scatter_dimension=1, tiled=True)]
    dot_general x108 -> x0, matrix products: 92 us -> none  [the longest x16 16.2 us: block_grads(): jnp.einsum('bhqk,bkhe->bqhe', grad_scores, key_rows, preferred_element_ty...]
    ppermute x64 -> x40, starting transfers between devices: 118 us -> 45.9 us  [exchange(): return lax.ppermute(array, axis, [(i, i ^ mask) for i in range(size)])]
    psum x3 -> x0, waiting for transfers between devices: 71.2 us -> none  [the longest x1 28.6 us: micro_batch(): lax.psum(jnp.einsum('btf,df->btd', grad_up, up_full, preferred_element_ty...]
    unnamed x2 -> x0, blocking collectives: 58.7 us -> none
    unnamed x11 -> x0, waiting for transfers between devices: 52.3 us -> none
    pallas_call x0 -> x16, Pallas kernels: none -> 51.4 us  [in_vmem(): pl.pallas_call(body, out_shape=[pltpu.HBM(*out[:2]) if len(out) == 3 else...]
  transfers between devices with their start and end apart: 73 -> 44, of which waited for: 36 -> 23; matrix products, arithmetic and copies ran while one was open for 16% -> 1% of each run, Pallas kernels for 0% -> 14%
where the time goes in v1:
time: 259 us; the launch traced here: 258 us
  waiting for transfers between devices  133 us (51%)
  starting transfers between devices  64.2 us (25%)
  Pallas kernels  51.4 us (20%)
  local copies, waits for them, and re-layouts  7.28 us (3%)
    ppermute x40, waiting for transfers between devices, exchange(): return lax.ppermute(array, axis, [(i, i ^ mask) for i in range(size)])  103 us
    pallas_call x16, Pallas kernels, in_vmem(): pl.pallas_call(body, out_shape=[pltpu.HBM(*out[:2]) if len(out) == 3 else...  51.4 us
    ppermute x40, starting transfers between devices, exchange(): return lax.ppermute(array, axis, [(i, i ^ mask) for i in range(size)])  45.9 us
    all_to_all x1, waiting for transfers between devices, pair_shards(): came = lax.all_to_all(send, 'seq', 0, 0, tiled=True)  18.9 us
    all_to_all x1, starting transfers between devices, pair_shards(): grad_came = lax.all_to_all(send, 'seq', 0, 0, tiled=True)  6.09 us
    all_to_all x1, waiting for transfers between devices, pair_shards(): mixed_came = lax.all_to_all(send, 'seq', 0, 0, tiled=True)  5.98 us
    all_to_all x1, waiting for transfers between devices, pair_shards(): grad_came = lax.all_to_all(send, 'seq', 0, 0, tiled=True)  5.85 us
    unnamed x52, local copies, waits for them, and re-layouts  5.3 us
  transfers between devices with their start and end apart: 44, of which 23 were waited for; matrix products, arithmetic and copies ran while one was open for 1% of the time, Pallas kernels for 14%

profile of v1, /device:TPU:0, one launch (start us, length us, event | category | flops | bytes accessed | tf_op | source)
XLA Modules:
  0.0 257.9 jit_solution(14370344188631252990)
XLA Ops:
  2.3 5.1 %collective-permute-start.5 = (bf16[448,128]{1,0:T(8,128)(2,1)S(1)}, bf16[448,128]{1,0:T(8,128)(2,1)S(1)}, u32[]{:S(2)}, u32[]{:S(2)}) collective-permute-start(bf16[448,128]{1,0:T(8,128)(2,1)S(1)} %shard_map.212.refs_0_), channel_id=1, source_target_pairs={{0,24},{4,28},{8,16},{12,20},{16,8},{20,12},{24,0},{28,4},{1,25},{... | collective-permute-start | bytes 344072 | tf_op jit(solution)/shard_map/ppermute | solution.py:396
  13.2 3.9 %collective-permute-done.3.refs_4_ = bf16[448,128]{1,0:T(8,128)(2,1)S(1)} collective-permute-done((bf16[448,128]{1,0:T(8,128)(2,1)S(1)}, bf16[448,128]{1,0:T(8,128)(2,1)S(1)}, u32[]{:S(2)}, u32[]{:S(2)}) %collective-permute-start.3) | collective-permute-done | bytes 114720 | tf_op jit(solution)/shard_map/ppermute | solution.py:396
  26.8 4.6 %all-to-all-start = ((bf16[8,304,128]{2,1,0:T(8,128)(2,1)}), bf16[8,304,128]{2,1,0:T(8,128)(2,1)S(1)}, u32[]{:S(2)}, u32[]{:S(2)}) async-start(bf16[8,304,128]{2,1,0:T(8,128)(2,1)} %get-tuple-element.67), calls=%async_computation | async-start | bytes 1245184 | tf_op jit(solution)/shard_map/all_to_all | solution.py:1015
  37.1 18.9 %all-to-all-done.came = bf16[8,304,128]{2,1,0:T(8,128)(2,1)S(1)} async-done(((bf16[8,304,128]{2,1,0:T(8,128)(2,1)}), bf16[8,304,128]{2,1,0:T(8,128)(2,1)S(1)}, u32[]{:S(2)}, u32[]{:S(2)}) %all-to-all-start) | async-done | bytes 622624 | tf_op jit(solution)/shard_map/all_to_all | solution.py:1015
  56.1 4.5 %shard_map.214 = (bf16[8,96,128]{2,1,0:T(8,128)(2,1)}, bf16[1536,64]{1,0:T(8,128)(2,1)}, bf16[1536,128]{1,0:T(8,128)(2,1)}, f32[64,1536]{1,0:T(8,128)}, f32[1,1536]{1,0:T(1,128)}, /*index=5*/bf16[8,304,128]{2,1,0:T(8,128)(2,1)}) custom-call(s32[2]{0:T(128)S(1)} %pad_add_fusion.place, s32[2]{0:T(128)S(1)} %copy-done.2, s32[2]{0:T(128)S(1)} %copy-done.3, ...), custom_call_target="tpu_custom_call" | custom-call | tf_op jit(solution)/shard_map/pallas_call | solution.py:372
  64.5 4.1 %collective-permute-done.15.refs_6_ = bf16[224,768]{1,0:T(8,128)(2,1)S(1)} collective-permute-done((bf16[224,768]{1,0:T(8,128)(2,1)S(1)}, bf16[224,768]{1,0:T(8,128)(2,1)S(1)}, u32[]{:S(2)}, u32[]{:S(2)}) %collective-permute-start.15) | collective-permute-done | bytes 344096 | tf_op jit(solution)/shard_map/ppermute | solution.py:396
  70.6 3.7 %all-to-all-start.1 = ((bf16[8,96,128]{2,1,0:T(8,128)(2,1)}), bf16[8,96,128]{2,1,0:T(8,128)(2,1)S(1)}, u32[]{:S(2)}, u32[]{:S(2)}) async-start(bf16[8,96,128]{2,1,0:T(8,128)(2,1)} %get-tuple-element.68), calls=%async_computation.1 | async-start | bytes 393216 | tf_op jit(solution)/shard_map/all_to_all | solution.py:1033
  74.4 14.0 %collective-permute-done.12.refs_3_ = bf16[224,768]{1,0:T(8,128)(2,1)S(1)} collective-permute-done((bf16[224,768]{1,0:T(8,128)(2,1)S(1)}, bf16[224,768]{1,0:T(8,128)(2,1)S(1)}, u32[]{:S(2)}, u32[]{:S(2)}) %collective-permute-start.12) | collective-permute-done | bytes 344096 | tf_op jit(solution)/shard_map/ppermute | solution.py:396
  88.3 4.5 %collective-permute-done.16.refs_7_ = bf16[224,768]{1,0:T(8,128)(2,1)S(1)} collective-permute-done((bf16[224,768]{1,0:T(8,128)(2,1)S(1)}, bf16[224,768]{1,0:T(8,128)(2,1)S(1)}, u32[]{:S(2)}, u32[]{:S(2)}) %collective-permute-start.16) | collective-permute-done | bytes 344096 | tf_op jit(solution)/shard_map/ppermute | solution.py:396
  99.2 8.1 %collective-permute-done.18.out_2 = bf16[768,192]{1,0:T(8,128)(2,1)S(1)} collective-permute-done((bf16[768,192]{1,0:T(8,128)(2,1)}, bf16[768,192]{1,0:T(8,128)(2,1)S(1)}, u32[]{:S(2)}, u32[]{:S(2)}) %collective-permute-start.18) | collective-permute-done | bytes 294944 | tf_op jit(solution)/shard_map/ppermute | solution.py:396
  111.7 6.1 %shard_map.217 = (f32[384,768]{1,0:T(8,128)}, bf16[384,768]{1,0:T(8,128)(2,1)}, bf16[384,768]{1,0:T(8,128)(2,1)}, bf16[384,768]{1,0:T(8,128)(2,1)}, bf16[384,768...) custom-call(s32[2]{0:T(128)S(1)} %pad_add_fusion.place, ...), custom_call_target="tpu_custom_call" | custom-call | tf_op jit(solution)/shard_map/pallas_call | solution.py:372
  121.0 5.8 %shard_map.218 = (bf16[192,768]{1,0:T(8,128)(2,1)}, bf16[192,768]{1,0:T(8,128)(2,1)}, bf16[4,192,768]{2,1,0:T(8,128)(2,1)}, bf16[4,192,768]{2,1,0:T(8,128)(2,1)}) custom-call(s32[2]{0:T(128)S(1)} %pad_add_fusion.place, bf16[384,768]{1,0:T(8,128)(2,1)} %get-tuple-element.76.normed, bf16[384,768]{1,0:T(8,128)(2,1)} %get-tuple-element.77.squared, ...), custom_call_target="tpu_custom_call" | custom-call | tf_op jit(solution)/shard_map/pallas_call | solution.py:372
  133.7 6.1 %all-to-all-start.2 = ((bf16[8,96,128]{2,1,0:T(8,128)(2,1)}), bf16[8,96,128]{2,1,0:T(8,128)(2,1)S(1)}, u32[]{:S(2)}, u32[]{:S(2)}) async-start(bf16[8,96,128]{2,1,0:T(8,128)(2,1)} %get-tuple-element.91), calls=%async_computation.2 | async-start | bytes 393216 | tf_op jit(solution)/shard_map/all_to_all | solution.py:1112
  142.2 5.9 %all-to-all-done.2.grad_came = bf16[8,96,128]{2,1,0:T(8,128)(2,1)S(1)} async-done(((bf16[8,96,128]{2,1,0:T(8,128)(2,1)}), bf16[8,96,128]{2,1,0:T(8,128)(2,1)S(1)}, u32[]{:S(2)}, u32[]{:S(2)}) %all-to-all-start.2) | async-done | bytes 196640 | tf_op jit(solution)/shard_map/all_to_all | solution.py:1112
  148.0 6.0 %shard_map.221 = bf16[8,304,128]{2,1,0:T(8,128)(2,1)} custom-call(s32[2]{0:T(128)S(1)} %pad_add_fusion.place, s32[2]{0:T(128)S(1)} %copy-done.2, s32[2]{0:T(128)S(1)} %copy-done.3, bf16[8,304,128]{2,1,0:T(8,128)(2,1)} %get-tuple-element.82.came, bf16[1536,64]{1,0:T(8,128)(2,1)} %get-tuple-element.83.q_all, bf16[1536,128]{1,0:T(8,128)(2,1)} %get-tuple-element.84.kv_all, ...), custom_call_target="tpu_custom_call" | custom-call | tf_op jit(solution)/shard_map/pallas_call | solution.py:372
  154.0 3.9 %all-to-all-start.3 = ((bf16[8,304,128]{2,1,0:T(8,128)(2,1)}), bf16[8,304,128]{2,1,0:T(8,128)(2,1)S(1)}, u32[]{:S(2)}, u32[]{:S(2)}) async-start(bf16[8,304,128]{2,1,0:T(8,128)(2,1)} %shard_map.221), calls=%async_computation.3 | async-start | bytes 1245184 | tf_op jit(solution)/shard_map/all_to_all | solution.py:1130
  161.2 5.9 %collective-permute-done.21 = bf16[192,768]{1,0:T(8,128)(2,1)S(1)} collective-permute-done((bf16[192,768]{1,0:T(8,128)(2,1)S(1)}, bf16[192,768]{1,0:T(8,128)(2,1)S(1)}, u32[]{:S(2)}, u32[]{:S(2)}) %collective-permute-start.21) | collective-permute-done | bytes 294944 | tf_op jit(solution)/shard_map/ppermute | solution.py:396
  167.7 6.0 %all-to-all-done.3.came = bf16[8,304,128]{2,1,0:T(8,128)(2,1)S(1)} async-done(((bf16[8,304,128]{2,1,0:T(8,128)(2,1)}), bf16[8,304,128]{2,1,0:T(8,128)(2,1)S(1)}, u32[]{:S(2)}, u32[]{:S(2)}) %all-to-all-start.3) | async-done | bytes 622624 | tf_op jit(solution)/shard_map/all_to_all | solution.py:1130
  173.7 4.2 %shard_map.222 = (bf16[4,432,128]{2,1,0:T(8,128)(2,1)}, bf16[4,432,128]{2,1,0:T(8,128)(2,1)}, bf16[192,768]{1,0:T(8,128)(2,1)S(1)}, bf16[192,768]{1,0:T(8,128)(2,1)S(1)}, f32[9,24]{1,0:T(8,128)}) custom-call(s32[2]{0:T(128)S(1)} %pad_add_fusion.place, bf16[8,304,128]{2,1,0:T(8,128)(2,1)S(1)} %all-to-all-done.3.came, ...), custom_call_target="tpu_custom_call" | custom-call | tf_op jit(solution)/shard_map/pallas_call | solution.py:372
  179.2 18.2 %collective-permute-done.34.refs_3_ = bf16[4,32,768]{2,1,0:T(8,128)(2,1)S(1)} collective-permute-done((bf16[4,32,768]{2,1,0:T(8,128)(2,1)S(1)}, bf16[4,32,768]{2,1,0:T(8,128)(2,1)S(1)}, u32[]{:S(2)}, u32[]{:S(2)}) %collective-permute-start.34) | collective-permute-done | bytes 196640 | tf_op jit(solution)/shard_map/ppermute | solution.py:396
  206.1 7.0 %collective-permute-done.35.b1 = bf16[224,768]{1,0:T(8,128)(2,1)S(1)} collective-permute-done((bf16[224,768]{1,0:T(8,128)(2,1)}, bf16[224,768]{1,0:T(8,128)(2,1)S(1)}, u32[]{:S(2)}, u32[]{:S(2)}) %collective-permute-start.35) | collective-permute-done | bytes 344096 | tf_op jit(solution)/shard_map/ppermute | solution.py:396
  213.1 15.5 %collective-permute-done.36.b2 = bf16[224,768]{1,0:T(8,128)(2,1)S(1)} collective-permute-done((bf16[224,768]{1,0:T(8,128)(2,1)}, bf16[224,768]{1,0:T(8,128)(2,1)S(1)}, u32[]{:S(2)}, u32[]{:S(2)}) %collective-permute-start.36) | collective-permute-done | bytes 344096 | tf_op jit(solution)/shard_map/ppermute | solution.py:396
  233.1 4.2 %collective-permute-start.30 = (bf16[432,128]{1,0:T(8,128)(2,1)S(1)}, bf16[432,128]{1,0:T(8,128)(2,1)S(1)}, u32[]{:S(2)}, u32[]{:S(2)}) collective-permute-start(bf16[432,128]{1,0:T(8,128)(2,1)S(1)} %get-tuple-element.107), channel_id=1, source_target_pairs={{0,8},{4,12},{8,0},{12,4},{16,24},{20,28},{24,16},{28,20},{1,9},{5... | collective-permute-start | bytes 331784 | tf_op jit(solution)/shard_map/ppermute | solution.py:396
  242.1 5.2 %collective-permute-done.31.b2 = bf16[432,128]{1,0:T(8,128)(2,1)S(1)} collective-permute-done((bf16[432,128]{1,0:T(8,128)(2,1)S(1)}, bf16[432,128]{1,0:T(8,128)(2,1)S(1)}, u32[]{:S(2)}, u32[]{:S(2)}) %collective-permute-start.31) | collective-permute-done | bytes 110624 | tf_op jit(solution)/shard_map/ppermute | solution.py:396
  (147 shorter events, 85.7 us)
Async XLA Ops:
  7.4 11.2 %collective-permute-start.1 = (bf16[448,128]{1,0:T(8,128)(2,1)S(1)}, bf16[448,128]{1,0:T(8,128)(2,1)S(1)}, u32[]{:S(2)}, u32[]{:S(2)}) collective-permute-start(bf16[448,128]{1,0:T(8,128)(2,1)S(1)} %shard_map.212.refs_0_), channel_id=1, source_target_pairs={{0,8},{4,12},{8,0},{12,4},{16,24},{20,28},{24,16},{28,20},{1,9},{5... | collective-permute-start | bytes 344072 | tf_op jit(solution)/shard_map/ppermute | solution.py:396
  8.1 11.2 %collective-permute-start = (bf16[448,128]{1,0:T(8,128)(2,1)S(1)}, bf16[448,128]{1,0:T(8,128)(2,1)S(1)}, u32[]{:S(2)}, u32[]{:S(2)}) collective-permute-start(bf16[448,128]{1,0:T(8,128)(2,1)S(1)} %shard_map.212.refs_0_), channel_id=1, source_target_pairs={{0,4},{4,0},{8,12},{12,8},{16,20},{20,16},{24,28},{28,24},{1,5},{5... | collective-permute-start | bytes 344072 | tf_op jit(solution)/shard_map/ppermute | solution.py:396
  26.8 29.3 %all-to-all-start = ((bf16[8,304,128]{2,1,0:T(8,128)(2,1)}), bf16[8,304,128]{2,1,0:T(8,128)(2,1)S(1)}, u32[]{:S(2)}, u32[]{:S(2)}) async-start(bf16[8,304,128]{2,1,0:T(8,128)(2,1)} %get-tuple-element.67), calls=%async_computation | async-start | bytes 1245184 | tf_op jit(solution)/shard_map/all_to_all | solution.py:1015
  32.7 28.3 %collective-permute-start.13 = (bf16[224,768]{1,0:T(8,128)(2,1)S(1)}, bf16[224,768]{1,0:T(8,128)(2,1)S(1)}, u32[]{:S(2)}, u32[]{:S(2)}) collective-permute-start(bf16[224,768]{1,0:T(8,128)(2,1)S(1)} %shard_map.215.refs_0_), channel_id=1, source_target_pairs={{0,16},{4,20},{8,24},{12,28},{16,0},{20,4},{24,8},{28,12},{1,17},{... | collective-permute-start | bytes 1032200 | tf_op jit(solution)/shard_map/ppermute | solution.py:396
  35.6 27.4 %collective-permute-start.11 = (bf16[224,768]{1,0:T(8,128)(2,1)S(1)}, bf16[224,768]{1,0:T(8,128)(2,1)S(1)}, u32[]{:S(2)}, u32[]{:S(2)}) collective-permute-start(bf16[224,768]{1,0:T(8,128)(2,1)S(1)} %shard_map.215.refs_0_), channel_id=1, source_target_pairs={{0,8},{4,12},{8,0},{12,4},{16,24},{20,28},{24,16},{28,20},{1,9},{5... | collective-permute-start | bytes 1032200 | tf_op jit(solution)/shard_map/ppermute | solution.py:396
  61.0 13.4 %collective-permute-start.10 = (bf16[224,768]{1,0:T(8,128)(2,1)S(1)}, bf16[224,768]{1,0:T(8,128)(2,1)S(1)}, u32[]{:S(2)}, u32[]{:S(2)}) collective-permute-start(bf16[224,768]{1,0:T(8,128)(2,1)S(1)} %shard_map.215.refs_0_), channel_id=1, source_target_pairs={{0,4},{4,0},{8,12},{12,8},{16,20},{20,16},{24,28},{28,24},{1,5},{5... | collective-permute-start | bytes 1032200 | tf_op jit(solution)/shard_map/ppermute | solution.py:396
  62.5 25.9 %collective-permute-start.14 = (bf16[224,768]{1,0:T(8,128)(2,1)S(1)}, bf16[224,768]{1,0:T(8,128)(2,1)S(1)}, u32[]{:S(2)}, u32[]{:S(2)}) collective-permute-start(bf16[224,768]{1,0:T(8,128)(2,1)S(1)} %collective-permute-done.13.refs_4_), channel_id=1, source_target_pairs={{0,4},{4,0},{8,12},{12,8},{16,20},{20,16},{24,28},{28,24},{1,5},{5... | collective-permute-start | bytes 1032200 | tf_op jit(solution)/shard_map/ppermute | solution.py:396
  63.0 25.3 %collective-permute-start.12 = (bf16[224,768]{1,0:T(8,128)(2,1)S(1)}, bf16[224,768]{1,0:T(8,128)(2,1)S(1)}, u32[]{:S(2)}, u32[]{:S(2)}) collective-permute-start(bf16[224,768]{1,0:T(8,128)(2,1)S(1)} %collective-permute-done.11.refs_2_), channel_id=1, source_target_pairs={{0,4},{4,0},{8,12},{12,8},{16,20},{20,16},{24,28},{28,24},{1,5},{5... | collective-permute-start | bytes 1032200 | tf_op jit(solution)/shard_map/ppermute | solution.py:396
  68.6 24.2 %collective-permute-start.16 = (bf16[224,768]{1,0:T(8,128)(2,1)S(1)}, bf16[224,768]{1,0:T(8,128)(2,1)S(1)}, u32[]{:S(2)}, u32[]{:S(2)}) collective-permute-start(bf16[224,768]{1,0:T(8,128)(2,1)S(1)} %collective-permute-done.15.refs_6_), channel_id=1, source_target_pairs={{0,4},{4,0},{8,12},{12,8},{16,20},{20,16},{24,28},{28,24},{1,5},{5... | collective-permute-start | bytes 1032200 | tf_op jit(solution)/shard_map/ppermute | solution.py:396
  70.6 28.0 %all-to-all-start.1 = ((bf16[8,96,128]{2,1,0:T(8,128)(2,1)}), bf16[8,96,128]{2,1,0:T(8,128)(2,1)S(1)}, u32[]{:S(2)}, u32[]{:S(2)}) async-start(bf16[8,96,128]{2,1,0:T(8,128)(2,1)} %get-tuple-element.68), calls=%async_computation.1 | async-start | bytes 393216 | tf_op jit(solution)/shard_map/all_to_all | solution.py:1033
  98.6 10.7 %collective-permute-start.8 = (bf16[8,96,128]{2,1,0:T(8,128)(2,1)S(1)}, bf16[8,96,128]{2,1,0:T(8,128)(2,1)S(1)}, u32[]{:S(2)}, u32[]{:S(2)}) collective-permute-start(bf16[8,96,128]{2,1,0:T(8,128)(2,1)S(1)} %all-to-all-done.1.att_0), channel_id=1, source_target_pairs={{0,2},{1,3},{2,0},{3,1},{4,6},{5,7},{6,4},{7,5},{8,10},{9,11},{10,... | collective-permute-start | bytes 589832 | tf_op jit(solution)/shard_map/ppermute | solution.py:396
  99.2 11.6 %collective-permute-start.17 = (bf16[768,192]{1,0:T(8,128)(2,1)}, bf16[768,192]{1,0:T(8,128)(2,1)S(1)}, u32[]{:S(2)}, u32[]{:S(2)}) collective-permute-start(bf16[768,192]{1,0:T(8,128)(2,1)} %get-tuple-element.72.out_0.out), channel_id=1, source_target_pairs={{0,1},{1,0},{2,3},{3,2},{4,5},{5,4},{6,7},{7,6},{8,9},{9,8},{10,11... | collective-permute-start | bytes 884744 | tf_op jit(solution)/shard_map/ppermute | solution.py:396
  133.7 14.3 %all-to-all-start.2 = ((bf16[8,96,128]{2,1,0:T(8,128)(2,1)}), bf16[8,96,128]{2,1,0:T(8,128)(2,1)S(1)}, u32[]{:S(2)}, u32[]{:S(2)}) async-start(bf16[8,96,128]{2,1,0:T(8,128)(2,1)} %get-tuple-element.91), calls=%async_computation.2 | async-start | bytes 393216 | tf_op jit(solution)/shard_map/all_to_all | solution.py:1112
  139.8 19.8 %collective-permute-start.20 = (bf16[192,768]{1,0:T(8,128)(2,1)S(1)}, bf16[192,768]{1,0:T(8,128)(2,1)S(1)}, u32[]{:S(2)}, u32[]{:S(2)}) collective-permute-start(bf16[192,768]{1,0:T(8,128)(2,1)S(1)} %copy-done.24), channel_id=1, source_target_pairs={{0,1},{1,0},{2,3},{3,2},{4,5},{5,4},{6,7},{7,6},{8,9},{9,8},{10,11... | collective-permute-start | bytes 884744 | tf_op jit(solution)/shard_map/ppermute | solution.py:396
  154.0 19.7 %all-to-all-start.3 = ((bf16[8,304,128]{2,1,0:T(8,128)(2,1)}), bf16[8,304,128]{2,1,0:T(8,128)(2,1)S(1)}, u32[]{:S(2)}, u32[]{:S(2)}) async-start(bf16[8,304,128]{2,1,0:T(8,128)(2,1)} %shard_map.221), calls=%async_computation.3 | async-start | bytes 1245184 | tf_op jit(solution)/shard_map/all_to_all | solution.py:1130
  157.9 39.5 %collective-permute-start.33 = (bf16[4,192,768]{2,1,0:T(8,128)(2,1)}, bf16[4,192,768]{2,1,0:T(8,128)(2,1)S(1)}, u32[]{:S(2)}, u32[]{:S(2)}) collective-permute-start(bf16[4,192,768]{2,1,0:T(8,128)(2,1)} %get-tuple-element.89), channel_id=1, source_target_pairs={{0,4},{4,0},{8,12},{12,8},{16,20},{20,16},{24,28},{28,24},{1,5},{5... | collective-permute-start | bytes 3538952 | tf_op jit(solution)/shard_map/ppermute | solution.py:396
  167.2 38.8 %collective-permute-start.22 = (bf16[192,768]{1,0:T(8,128)(2,1)S(1)}, bf16[192,768]{1,0:T(8,128)(2,1)S(1)}, u32[]{:S(2)}, u32[]{:S(2)}) collective-permute-start(bf16[192,768]{1,0:T(8,128)(2,1)S(1)} %add_convert_fusion.4), channel_id=1, source_target_pairs={{0,1},{1,0},{2,3},{3,2},{4,5},{5,4},{6,7},{7,6},{8,9},{9,8},{10,11... | collective-permute-start | bytes 884744 | tf_op jit(solution)/shard_map/ppermute | solution.py:396
  167.3 30.2 %collective-permute-start.34 = (bf16[4,32,768]{2,1,0:T(8,128)(2,1)S(1)}, bf16[4,32,768]{2,1,0:T(8,128)(2,1)S(1)}, u32[]{:S(2)}, u32[]{:S(2)}) collective-permute-start(bf16[4,32,768]{2,1,0:T(8,128)(2,1)S(1)} %copy-done.25), channel_id=1, source_target_pairs={{0,4},{4,0},{8,12},{12,8},{16,20},{20,16},{24,28},{28,24},{1,5},{5... | collective-permute-start | bytes 589832 | tf_op jit(solution)/shard_map/ppermute | solution.py:396
  177.8 54.1 %collective-permute-start.29 = (bf16[4,432,128]{2,1,0:T(8,128)(2,1)}, bf16[4,432,128]{2,1,0:T(8,128)(2,1)S(1)}, u32[]{:S(2)}, u32[]{:S(2)}) collective-permute-start(bf16[4,432,128]{2,1,0:T(8,128)(2,1)} %get-tuple-element.105), channel_id=1, source_target_pairs={{0,4},{4,0},{8,12},{12,8},{16,20},{20,16},{24,28},{28,24},{1,5},{5... | collective-permute-start | bytes 1327112 | tf_op jit(solution)/shard_map/ppermute | solution.py:396
  201.6 11.5 %collective-permute-start.35 = (bf16[224,768]{1,0:T(8,128)(2,1)}, bf16[224,768]{1,0:T(8,128)(2,1)S(1)}, u32[]{:S(2)}, u32[]{:S(2)}) collective-permute-start(bf16[224,768]{1,0:T(8,128)(2,1)} %get-tuple-element.114), channel_id=1, source_target_pairs={{0,8},{4,12},{8,0},{12,4},{16,24},{20,28},{24,16},{28,20},{1,9},{5... | collective-permute-start | bytes 1032200 | tf_op jit(solution)/shard_map/ppermute | solution.py:396
  203.2 25.4 %collective-permute-start.36 = (bf16[224,768]{1,0:T(8,128)(2,1)}, bf16[224,768]{1,0:T(8,128)(2,1)S(1)}, u32[]{:S(2)}, u32[]{:S(2)}) collective-permute-start(bf16[224,768]{1,0:T(8,128)(2,1)} %get-tuple-element.115), channel_id=1, source_target_pairs={{0,16},{4,20},{8,24},{12,28},{16,0},{20,4},{24,8},{28,12},{1,17},{... | collective-permute-start | bytes 1032200 | tf_op jit(solution)/shard_map/ppermute | solution.py:396
  205.4 23.2 %collective-permute-start.37 = (bf16[224,768]{1,0:T(8,128)(2,1)}, bf16[224,768]{1,0:T(8,128)(2,1)S(1)}, u32[]{:S(2)}, u32[]{:S(2)}) collective-permute-start(bf16[224,768]{1,0:T(8,128)(2,1)} %get-tuple-element.116), channel_id=1, source_target_pairs={{0,24},{4,28},{8,16},{12,20},{16,8},{20,12},{24,0},{28,4},{1,25},{... | collective-permute-start | bytes 1032200 | tf_op jit(solution)/shard_map/ppermute | solution.py:396
  206.0 34.5 %collective-permute-start.26 = (bf16[192,768]{1,0:T(8,128)(2,1)S(1)}, bf16[192,768]{1,0:T(8,128)(2,1)S(1)}, u32[]{:S(2)}, u32[]{:S(2)}) collective-permute-start(bf16[192,768]{1,0:T(8,128)(2,1)S(1)} %get-tuple-element.99), channel_id=1, source_target_pairs={{0,1},{1,0},{2,3},{3,2},{4,5},{5,4},{6,7},{7,6},{8,9},{9,8},{10,11... | collective-permute-start | bytes 884744 | tf_op jit(solution)/shard_map/ppermute | solution.py:396
  240.6 11.8 %collective-permute-start.27 = (bf16[192,768]{1,0:T(8,128)(2,1)S(1)}, bf16[192,768]{1,0:T(8,128)(2,1)S(1)}, u32[]{:S(2)}, u32[]{:S(2)}) collective-permute-start(bf16[192,768]{1,0:T(8,128)(2,1)S(1)} %add_convert_fusion.1), channel_id=1, source_target_pairs={{0,2},{1,3},{2,0},{3,1},{4,6},{5,7},{6,4},{7,5},{8,10},{9,11},{10,... | collective-permute-start | bytes 884744 | tf_op jit(solution)/shard_map/ppermute | solution.py:396
  (46 other events, 445.1 us)

commit v2 on v1

--- a/solution.py
+++ b/solution.py
@@ -358,6 +358,7 @@
 
 
 LANES = 128
+FENCE = 10**11
 NT = (((1,), (1,)), ((), ()))
 TN = (((0,), (0,)), ((), ()))
 F32 = jnp.float32
@@ -368,7 +369,7 @@
     return lax.dot_general(a, b, dims, preferred_element_type=F32)
 
 
-def in_vmem(body, outs, scalars, arrays, scratch=(), limit_mib=16):
+def in_vmem(body, outs, scalars, arrays, scratch=(), limit_mib=16, fence=False):
     return pl.pallas_call(
         body,
         out_shape=[
@@ -379,7 +380,9 @@
         out_specs=[pl.BlockSpec(memory_space=pltpu.VMEM)] * len(outs),
         scratch_shapes=[pltpu.VMEM(shape, kind) for shape, kind in scratch],
         compiler_params=pltpu.CompilerParams(vmem_limit_bytes=limit_mib * 1024 * 1024),
-        cost_estimate=pl.CostEstimate(flops=0, bytes_accessed=0, transcendentals=0),
+        cost_estimate=pl.CostEstimate(
+            flops=FENCE if fence else 0, bytes_accessed=0, transcendentals=0
+        ),
     )(*scalars, *arrays)
 
 
@@ -389,6 +392,19 @@
 
 def after(array, *others):
     return lax.optimization_barrier((array, *others))[0]
+
+
+def marker(*arrays):
+    def body(*refs):
+        refs[-1][...] = jnp.zeros_like(refs[-1])
+
+    return pl.pallas_call(
+        body,
+        out_shape=jax.ShapeDtypeStruct((8, LANES), F32),
+        in_specs=[pl.BlockSpec(memory_space=pl.ANY)] * len(arrays),
+        out_specs=pl.BlockSpec(memory_space=pltpu.VMEM),
+        cost_estimate=pl.CostEstimate(flops=FENCE, bytes_accessed=0, transcendentals=0),
+    )(*arrays)
 
 
 def exchange(array, axis, mask):
@@ -431,11 +447,11 @@
     packed[9 * rows // 2 :, :] = jnp.broadcast_to(gain_row, (16, LANES)).astype(BF16)
 
 
-def unpack_proj(packed, rows):
-    narrow = unfold(packed[3 * rows : 9 * rows // 2, :])
+def unpack_blocks(packed, rows, count):
+    narrow = unfold(packed[count * rows : 3 * count * rows // 2, :])
     return [
-        (packed[c * rows : (c + 1) * rows, :], narrow[c * rows : (c + 1) * rows, :])
-        for c in range(3)
+        (packed[i * rows : (i + 1) * rows, :], narrow[i * rows : (i + 1) * rows, :])
+        for i in range(count)
     ]
 
 
@@ -461,19 +477,16 @@
 
 
 def place_ffn_body(place, *refs):
-    parts = refs[:8]
-    up, down, out = refs[8:]
-    rows = up.shape[0] // 8
+    whole, out = refs[8:]
+    rows = out.shape[0] // 8
     for i in range(8):
-        first = pl.multiple_of(jnp.bitwise_xor(place[0], i) * rows, rows)
-        part = parts[i]
-        up[pl.ds(first, rows), :] = part[:rows, :]
-        down[pl.ds(first, rows), :] = part[rows : 2 * rows, :]
+        owner = jnp.bitwise_xor(place[0], i)
+        part = refs[i]
+        whole[owner] = part[: 2 * rows, :]
         for g in range(rows // 16):
-            at = pl.ds(pl.multiple_of(first + 16 * g, 16), 16)
-            lanes = slice(LANES * g, LANES * g + LANES)
-            out[at, :LANES] = part[2 * rows : 2 * rows + 16, lanes]
-            out[at, LANES:] = part[2 * rows + 16 : 2 * rows + 32, LANES * g : LANES * g + HEAD_DIM]
+            at = pl.ds(pl.multiple_of(owner * rows + 16 * g, 16), 16)
+            out[at, :LANES] = part[2 * rows : 2 * rows + 16, LANES * g : LANES * g + LANES]
+            out[at, LANES:] = part[2 * rows + 16 :, LANES * g : LANES * g + HEAD_DIM]
 
 
 def project_body(place, *refs):
@@ -486,10 +499,10 @@
         shard = weight.shape[1] // 8
         owner = jnp.bitwise_xor(place[0], i)
         gain_rows[pl.ds(owner, 1), :] = packed[9 * shard // 2 :, :].astype(F32)[:1]
-        first = pl.multiple_of(owner * shard, shard)
-        for c, (wide, narrow) in enumerate(unpack_proj(packed, shard)):
-            weight[c, pl.ds(first, shard), :LANES] = wide
-            weight[c, pl.ds(first, shard), LANES:] = narrow
+        at = pl.ds(pl.multiple_of(owner * shard, shard), shard)
+        for c, (wide, narrow) in enumerate(unpack_blocks(packed, shard, 3)):
+            weight[c, at, :LANES] = wide
+            weight[c, at, LANES:] = narrow
     gain[...] = jnp.concatenate([gain_rows[j : j + 1, :shard] for j in range(8)], axis=1)
     for b in range(seqs):
         values = jnp.concatenate([long_in[b], short_in[b]], axis=0).astype(F32)
@@ -608,46 +621,47 @@
     return jnp.concatenate(columns, axis=1)
 
 
+def out_proj_body(place, came, out, att, keep, send, scratch):
+    att[...] = pair_rows(came, 2)
+    scratch[...] = dot(att[...], out[...], NT).astype(BF16)
+    split_halves(place, scratch, keep, send)
+
+
 def feed_body(
     long_rows,
     place,
     long_lengths,
     short_lengths,
-    att_0,
-    att_1,
-    att_2,
-    att_3,
-    out_0,
-    out_1,
-    out_2,
-    out_3,
+    own,
+    other,
     long_in,
     short_in,
     long_cot,
     short_cot,
-    up,
-    down,
+    gathered,
     mid_ref,
     normed_ref,
     squared_ref,
     grad_up_ref,
     grad_out_ref,
-    att_ref,
     keep,
     send,
     scratch,
-    sums,
+    attended,
+    up,
+    down,
 ):
     seqs = long_in.shape[0]
+    shard = gathered.shape[1] // 2
+    for s in range(8):
+        up[s * shard : (s + 1) * shard, :] = gathered[s, :shard, :]
+        down[s * shard : (s + 1) * shard, :] = gathered[s, shard:, :]
     rows = long_rows + short_in.shape[1]
-    att_ref[...] = pair_rows(att_0, seqs)
-    sums[place[1]] = dot(att_ref[...], out_0[...], NT)
-    for i, att, out in ((1, att_1, out_1), (2, att_2, out_2), (3, att_3, out_3)):
-        sums[jnp.bitwise_xor(place[1], i)] = dot(pair_rows(att, seqs), out[...], NT)
+    join_halves(place, attended, own, other)
     for b in range(seqs):
         at = slice(b * rows, (b + 1) * rows)
         residual = jnp.concatenate([long_in[b], short_in[b]], axis=0).astype(F32)
-        mid = residual + ((sums[0, at, :] + sums[1, at, :]) + (sums[2, at, :] + sums[3, at, :]))
+        mid = residual + attended[at, :]
         mid_ref[at, :] = mid
         root = lax.rsqrt(jnp.mean(mid * mid, axis=-1, keepdims=True) + norm_eps)
         normed_ref[at, :] = (mid * root).astype(BF16)
@@ -689,21 +703,31 @@
         send[z] = blocks[2 * z + 1 - y]
 
 
-def feed_terms_body(
-    place, normed, squared, grad_up, grad_out, down, f_keep, f_send, keep, send, scratch, blocks
+def up_term_body(place, normed, grad_up, keep, send, blocks):
+    rows = blocks.shape[1]
+    term = dot(normed[...], grad_up[...], TN).astype(BF16)
+    for s in range(8):
+        blocks[s] = term[s * rows : (s + 1) * rows]
+    split_y(place, blocks, keep, send)
+
+
+def down_term_body(
+    place, squared, grad_out, gathered, keep, send, f_keep, f_send, scratch, down, blocks
 ):
+    rows = gathered.shape[1] // 2
+    for s in range(8):
+        down[s * rows : (s + 1) * rows, :] = gathered[s, rows:, :]
+    term = dot(grad_out[...], squared[...], TN).astype(BF16)
+    for s in range(8):
+        blocks[s] = term[s * rows : (s + 1) * rows]
+    split_y(place, blocks, keep, send)
     scratch[...] = dot(squared[...], down[...], NT).astype(BF16)
     split_halves(place, scratch, f_keep, f_send)
-    rows = down.shape[0] // 8
-    up_term = dot(normed[...], grad_up[...], TN).astype(BF16)
-    down_term = dot(grad_out[...], squared[...], TN).astype(BF16)
-    for s in range(8):
-        blocks[s, :rows, :] = up_term[s * rows : (s + 1) * rows]
-        blocks[s, rows:, :] = down_term[s * rows : (s + 1) * rows]
-    split_y(place, blocks, keep, send)
-
-
-def middle_body(place, own, other, mid_ref, grad_out, out, grad_mid_ref, low_ref, send, scratch):
+
+
+def middle_body(
+    place, own, other, mid_ref, grad_out, out, att, grad_mid_ref, send, keep_out, send_out, scratch, low_ref, blocks
+):
     join_halves(place, scratch, own, other)
     seqs = 2
     rows = mid_ref.shape[0] // seqs
@@ -727,18 +751,15 @@
             )
         else:
             send[dest] = jnp.zeros_like(send[dest])
-
-
-def out_term_body(place, low, att, keep, send, blocks):
-    term = dot(low[...], att[...], TN).astype(BF16)
-    rows = term.shape[0] // 8
+    term = dot(low_ref[...], att[...], TN).astype(BF16)
+    shard = term.shape[0] // 8
     for s in range(8):
 
         def store(row, lane, value):
             blocks[s, row : row + 16, lane : lane + LANES] = value
 
-        narrow_pack(term[s * rows : (s + 1) * rows], store)
-    split_y(place, blocks, keep, send)
+        narrow_pack(term[s * shard : (s + 1) * shard], store)
+    split_y(place, blocks, keep_out, send_out)
 
 
 def attend_back_body(
@@ -849,9 +870,7 @@
         ).astype(BF16)
 
 
-def project_back_body(
-    place, came, normed, weight, keep, send, keep_w, send_w, taps, scratch, grad_mixed, blocks
-):
+def place_grad_mixed(came, grad_mixed):
     seqs = 2
     rows = (came.shape[1] - 16) * 2 // 3
     for e in range(3):
@@ -862,11 +881,11 @@
             grad_mixed[0, at, lanes] = unfold(came[j, rows : rows + rows // 2, :])
             grad_mixed[1, at, lanes] = came[j, :rows, :HEAD_DIM]
             grad_mixed[2, at, lanes] = came[j, :rows, HEAD_DIM:]
-    total = came[0, rows + rows // 2 :, :].astype(F32)
-    for j in range(1, 3 * seqs):
-        total = total + came[j, rows + rows // 2 :, :].astype(F32)
-    taps[...] = total[: taps.shape[0], : taps.shape[1]]
-    shard = weight.shape[1] // 8
+
+
+def proj_term_body(place, came, normed, keep, send, grad_mixed, blocks):
+    place_grad_mixed(came, grad_mixed)
+    shard = normed.shape[1] // 8
     terms = [dot(normed[...], grad_mixed[c], TN).astype(BF16) for c in range(3)]
     for s in range(8):
         at = slice(s * shard, (s + 1) * shard)
@@ -876,11 +895,20 @@
             jnp.concatenate([terms[c][at, LANES:] for c in range(3)], axis=0)
         )
     split_y(place, blocks, keep, send)
+
+
+def project_back_body(place, came, weight, keep, send, taps, scratch, grad_mixed):
+    place_grad_mixed(came, grad_mixed)
+    rows = (came.shape[1] - 16) * 2 // 3
+    total = came[0, rows + rows // 2 :, :].astype(F32)
+    for j in range(1, 6):
+        total = total + came[j, rows + rows // 2 :, :].astype(F32)
+    taps[...] = total[: taps.shape[0], : taps.shape[1]]
     total = dot(grad_mixed[0], weight[0], NT)
     for c in (1, 2):
         total = total + dot(grad_mixed[c], weight[c], NT)
     scratch[...] = total.astype(BF16)
-    split_halves(place, scratch, keep_w, send_w)
+    split_halves(place, scratch, keep, send)
 
 
 def input_grad_body(
@@ -900,6 +928,17 @@
         short_out[b] = grad[long_rows:]
 
 
+def output_body(place, own, other, mid, long_out, short_out, scratch):
+    join_halves(place, scratch, own, other)
+    seqs, long_rows, _ = long_out.shape
+    rows = long_rows + short_out.shape[1]
+    for b in range(seqs):
+        at = slice(b * rows, (b + 1) * rows)
+        value = (mid[at, :] + scratch[at, :]).astype(BF16)
+        long_out[b] = value[:long_rows]
+        short_out[b] = value[long_rows:]
+
+
 def scatter_z_body(place, *refs):
     count = (len(refs) - 4) // 2
     outs = refs[2 * count :]
@@ -916,6 +955,26 @@
             first += rows
 
 
+def near_body(place, *refs):
+    pairs = len(refs[:-3]) // 2
+    near, own, across = refs[-3:]
+    z = place[0] // 2
+    for i, target in ((0, own), (1, near.at[0]), (2, across), (3, near.at[1])):
+        block = jnp.bitwise_xor(z, i)
+        first = 0
+        for p in range(pairs):
+            keep, came = refs[2 * p], refs[2 * p + 1]
+            rows = keep.shape[1]
+            target[first : first + rows, :] = (
+                keep[block].astype(F32) + came[block].astype(F32)
+            ).astype(BF16)
+            first += rows
+
+
+def across_body(across, near, out):
+    out[...] = (across[...].astype(F32) + near[1].astype(F32)).astype(BF16)
+
+
 def sum_blocks(blocks):
     return (blocks[0][...].astype(F32) + blocks[1][...].astype(F32)) + (
         blocks[2][...].astype(F32) + blocks[3][...].astype(F32)
@@ -926,22 +985,24 @@
     total = sum_blocks((b0, b1, b2, b3))
     rows = proj.shape[1]
     column = 0.0
-    for c, (wide, narrow) in enumerate(unpack_proj(total, rows)):
+    for c, (wide, narrow) in enumerate(unpack_blocks(total, rows, 3)):
         term = jnp.concatenate([wide, narrow], axis=1)
         column = column + jnp.sum(term * proj[c].astype(F32), axis=1, keepdims=True)
         grad[c] = term
     gain_grad[...] = column.T / gain[...].astype(F32).reshape(1, rows)
 
 
-def ffn_grad_body(b0, b1, b2, b3, up, gain, up_grad, down_grad, out_grad, gain_grad):
-    total = sum_blocks((b0, b1, b2, b3))
+def ffn_grad_body(
+    up_own, up_near, up_across, own, near, across, up, gain, up_grad, down_grad, out_grad, gain_grad
+):
     rows = up.shape[0]
-    raw = total[:rows]
+    raw = up_own[...].astype(F32) + up_near[0].astype(F32) + up_across[...].astype(F32)
+    total = own[...].astype(F32) + near[0].astype(F32) + across[...].astype(F32)
     gain_grad[...] = jnp.sum(raw * up[...].astype(F32), axis=1, keepdims=True).T
     up_grad[...] = raw * gain[...].astype(F32).reshape(1, rows).T
-    down_grad[...] = total[rows : 2 * rows]
-    wide = total[2 * rows : 2 * rows + 16]
-    narrow = total[2 * rows + 16 :]
+    down_grad[...] = total[:rows]
+    wide = total[rows : rows + 16]
+    narrow = total[rows + 16 :]
     out = jnp.concatenate(
         [
             jnp.concatenate(
@@ -988,18 +1049,25 @@
     down_t = down_weight.T
 
     (proj_packed,) = in_vmem(
-        pack_proj_body, [((packed_rows + 16, LANES), BF16)], (), (proj_weight, attention_gain)
-    )
-    proj_z = [proj_packed] + [exchange(proj_packed, "seq", mask) for mask in (2, 4, 6)]
-    proj_parts = []
-    for piece in proj_z:
-        proj_parts += [piece, exchange(piece, "seq", 1)]
+        pack_proj_body,
+        [((packed_rows + 16, LANES), BF16)],
+        (),
+        far(proj_weight) + (attention_gain,),
+    )
     (ffn_packed,) = in_vmem(
         pack_ffn_body,
         [((2 * shard + 32, hidden), BF16)],
         (),
         far(up_weight, down_t, out_weight) + (feed_gain,),
     )
+    proj_z = [proj_packed] + [exchange(proj_packed, "seq", mask) for mask in (2, 4, 6)]
+    proj_parts = [proj_packed, exchange(proj_packed, "seq", 1)]
+    for piece in proj_z[1:]:
+        proj_parts += [piece, exchange(piece, "seq", 1)]
+    ffn_0 = after(ffn_packed, *proj_z)
+    ffn_1 = exchange(ffn_0, "seq", 1)
+    ffn_2 = exchange(ffn_0, "seq", 2)
+    ffn_4 = exchange(ffn_0, "seq", 4)
     send, normed, proj_full, gain = in_vmem(
         project_body,
         [
@@ -1011,12 +1079,15 @@
         (place,),
         (*proj_parts, *far(long_input, short_input, conv_taps)),
         scratch=[((8, LANES), F32)],
+        fence=True,
     )
     came = lax.all_to_all(send, "seq", 0, 0, tiled=True)
-    ffn_0 = after(ffn_packed, *proj_z)
-    ffn_2 = exchange(ffn_0, "seq", 2)
-    ffn_4 = exchange(ffn_0, "seq", 4)
-    ffn_1 = exchange(ffn_0, "seq", 1)
+    across_z = marker(ffn_4, ffn_1, send)
+    ffn_2, ffn_4 = after(ffn_2, across_z), after(ffn_4, across_z)
+    ffn_6 = exchange(ffn_4, "seq", 2)
+    ffn_3 = exchange(ffn_2, "seq", 1)
+    ffn_5 = exchange(ffn_4, "seq", 1)
+    ffn_7 = exchange(ffn_6, "seq", 1)
     att_send, q_all, kv_all, att_t, log_row, mixed = in_vmem(
         functools.partial(attend_body, long_rows, seqs),
         [
@@ -1029,30 +1100,31 @@
         ],
         (place, long_lengths, short_lengths),
         (came,),
+        fence=True,
     )
     att_0 = lax.all_to_all(att_send, "seq", 0, 0, tiled=True)
-    ffn_2, ffn_4 = after(ffn_2, att_send), after(ffn_4, att_send)
-    ffn_6 = exchange(ffn_4, "seq", 2)
-    ffn_3 = exchange(ffn_2, "seq", 1)
-    ffn_5 = exchange(ffn_4, "seq", 1)
-    ffn_7 = exchange(ffn_6, "seq", 1)
-    up_full, down_full, out_full = in_vmem(
+    ffn_full, out_full = in_vmem(
         place_ffn_body,
+        [((8, 2 * shard, hidden), BF16, "far"), ((width, local), BF16, "far")],
+        (place,),
+        far(after(ffn_packed, att_send), ffn_1, ffn_2, ffn_3, ffn_4, ffn_5, ffn_6, ffn_7),
+    )
+    att_0 = after(att_0, out_full)
+    att, keep, send = in_vmem(
+        out_proj_body,
         [
-            ((width, hidden), BF16, "far"),
-            ((width, hidden), BF16, "far"),
-            ((width, local), BF16, "far"),
+            ((tokens, local), BF16, "far"),
+            ((tokens // 2, width), BF16),
+            ((tokens // 2, width), BF16),
         ],
         (place,),
-        far(ffn_0, ffn_1, ffn_2, ffn_3, ffn_4, ffn_5, ffn_6, ffn_7),
-    )
-    out_2 = exchange(out_full, "head", 2)
-    out_1 = exchange(out_full, "head", 1)
-    out_3 = exchange(out_2, "head", 1)
-    att_2 = exchange(att_0, "head", 2)
-    att_1 = exchange(att_0, "head", 1)
-    att_3 = exchange(att_2, "head", 1)
-    mid, normed_ffn, squared, grad_up, grad_out, att, keep, send = in_vmem(
+        (att_0,) + far(out_full),
+        scratch=[((tokens, width), BF16)],
+    )
+    half = add_low(keep, exchange(send, "head", 1))
+    own = add_low(half, exchange(half, "head", 2))
+    other = exchange(own, "head", 1)
+    mid, normed_ffn, squared, grad_up, grad_out, keep, send = in_vmem(
         functools.partial(feed_body, long_rows),
         [
             ((tokens, width), F32, "far"),
@@ -1060,100 +1132,123 @@
             ((tokens, hidden), BF16, "far"),
             ((tokens, hidden), BF16, "far"),
             ((tokens, width), BF16, "far"),
-            ((tokens, local), BF16, "far"),
             ((tokens // 2, width), BF16),
             ((tokens // 2, width), BF16),
         ],
         (place, long_lengths, short_lengths),
-        (att_0, att_1, att_2, att_3)
-        + far(
-            out_full,
-            out_1,
-            out_2,
-            out_3,
-            long_input,
-            short_input,
-            long_cotangent,
-            short_cotangent,
-            up_full,
-            down_full,
-        ),
-        scratch=[((tokens, width), BF16), ((4, tokens, width), F32)],
+        (own, other)
+        + far(long_input, short_input, long_cotangent, short_cotangent, ffn_full),
+        scratch=[
+            ((tokens, width), BF16),
+            ((tokens, width), F32),
+            ((width, hidden), BF16),
+            ((width, hidden), BF16),
+        ],
         limit_mib=32,
     )
     half = add_low(keep, exchange(send, "head", 1))
-    f_keep, f_send, ffn_keep, ffn_send = in_vmem(
-        feed_terms_body,
-        [
-            ((tokens // 2, width), BF16, "far"),
-            ((tokens // 2, width), BF16, "far"),
-            ((4, 2 * shard, hidden), BF16, "far"),
-            ((4, 2 * shard, hidden), BF16, "far"),
+    up_keep, up_send = in_vmem(
+        up_term_body,
+        [((4, shard, hidden), BF16, "far")] * 2,
+        (place,),
+        far(after(normed_ffn, half), grad_up),
+        scratch=[((8, shard, hidden), BF16)],
+    )
+    up_came = exchange(up_send, "seq", 1)
+    down_keep, down_send, f_keep, f_send = in_vmem(
+        down_term_body,
+        [((4, shard, hidden), BF16, "far")] * 2 + [((tokens // 2, width), BF16, "far")] * 2,
+        (place,),
+        far(after(squared, up_send), grad_out, ffn_full),
+        scratch=[
+            ((tokens, width), BF16),
+            ((width, hidden), BF16),
+            ((8, shard, hidden), BF16),
         ],
-        (place,),
-        far(normed_ffn, squared, grad_up, grad_out, down_full),
-        scratch=[((tokens, width), BF16), ((8, 2 * shard, hidden), BF16)],
-        limit_mib=32,
-    )
-    ffn_came = exchange(ffn_send, "seq", 1)
-    own = add_low(half, after(exchange(half, "head", 2), ffn_send))
+        fence=True,
+    )
+    own = add_low(half, after(exchange(half, "head", 2), down_send))
     other = exchange(own, "head", 1)
-    grad_mid, grad_mid_low, send = in_vmem(
+    grad_mid, send, out_keep, out_send = in_vmem(
         middle_body,
         [
             ((tokens, width), F32, "far"),
-            ((tokens, width), BF16, "far"),
             ((8, rows // 2, LANES), BF16),
+            ((4, 32, hidden), BF16, "far"),
+            ((4, 32, hidden), BF16, "far"),
         ],
         (place,),
-        (own, other) + far(mid, grad_out, out_full),
-        scratch=[((tokens, width), F32)],
+        (own, other) + far(mid, grad_out, out_full, att),
+        scratch=[((tokens, width), F32), ((tokens, width), BF16), ((8, 32, hidden), BF16)],
+        fence=True,
     )
     grad_came = lax.all_to_all(send, "seq", 0, 0, tiled=True)
-    out_keep, out_send = in_vmem(
-        out_term_body,
-        [((4, 32, hidden), BF16, "far"), ((4, 32, hidden), BF16, "far")],
+    down_came = exchange(after(down_send, send), "seq", 1)
+    out_came = exchange(out_send, "seq", 1)
+    up_near, up_own, up_across = in_vmem(
+        near_body,
+        [((2, shard, hidden), BF16, "far")] + [((shard, hidden), BF16, "far")] * 2,
         (place,),
-        far(grad_mid_low, att),
-        scratch=[((8, 32, hidden), BF16)],
-    )
-    out_came = exchange(out_send, "seq", 1)
+        far(up_keep, after(up_came, grad_mid)),
+        fence=True,
+    )
+    up_near = exchange(up_near, "seq", 2)
+    grad_came = after(grad_came, up_own)
     f_half = add_low(f_keep, exchange(f_send, "head", 1))
     f_own = add_low(f_half, exchange(f_half, "head", 2))
     f_other = exchange(f_own, "head", 1)
+    long_output, short_output = in_vmem(
+        output_body,
+        [(long_input.shape, BF16), (short_input.shape, BF16)],
+        (place,),
+        (f_own, f_other) + far(mid),
+        scratch=[((tokens, width), F32)],
+    )
     (send,) = in_vmem(
         functools.partial(attend_back_body, long_rows, seqs),
         [((8, chunk, LANES), BF16)],
         (place, long_lengths, short_lengths),
-        far(mixed, q_all, kv_all, att_t, log_row) + (after(grad_came, out_send),),
-    )
-    mixed_came = lax.all_to_all(send, "seq", 0, 0, tiled=True)
-    ffn_blocks = in_vmem(
-        scatter_z_body,
-        [((2 * shard + 32, hidden), BF16, "far")] * 4,
+        far(mixed, q_all, kv_all, att_t, log_row) + (grad_came,),
+    )
+    mixed_came = lax.all_to_all(after(send, up_near), "seq", 0, 0, tiled=True)
+    near, ffn_own, across = in_vmem(
+        near_body,
+        [((2, shard + 32, hidden), BF16, "far")] + [((shard + 32, hidden), BF16, "far")] * 2,
         (place,),
-        far(ffn_keep, ffn_came, out_keep, out_came),
-    )
-    ffn_blocks = [ffn_blocks[0]] + [exchange(ffn_blocks[i], "seq", 2 * i) for i in (1, 2, 3)]
-    proj_keep, proj_send, keep, send, taps_grad = in_vmem(
+        far(down_keep, after(down_came, send), out_keep, out_came),
+        fence=True,
+    )
+    near = exchange(near, "seq", 2)
+    (up_across,) = in_vmem(
+        across_body, [((shard, hidden), BF16, "far")], (), far(after(up_across, across), up_near)
+    )
+    up_across = exchange(up_across, "seq", 4)
+    mixed_came = after(mixed_came, long_output, ffn_own)
+    proj_keep, proj_send = in_vmem(
+        proj_term_body,
+        [((4, packed_rows, LANES), BF16, "far"), ((4, packed_rows, LANES), BF16, "far")],
+        (place,),
+        (mixed_came,) + far(normed),
+        scratch=[((3, tokens, local), BF16), ((8, packed_rows, LANES), BF16)],
+    )
+    proj_came = exchange(proj_send, "seq", 1)
+    keep, send, taps_grad = in_vmem(
         project_back_body,
         [
-            ((4, packed_rows, LANES), BF16, "far"),
-            ((4, packed_rows, LANES), BF16, "far"),
             ((tokens // 2, width), BF16),
             ((tokens // 2, width), BF16),
             (conv_taps.shape, F32),
         ],
         (place,),
-        (mixed_came,) + far(normed, proj_full),
-        scratch=[
-            ((tokens, width), BF16),
-            ((3, tokens, local), BF16),
-            ((8, packed_rows, LANES), BF16),
-        ],
-    )
-    proj_came = exchange(proj_send, "seq", 1)
+        (after(mixed_came, proj_send, up_across, near),) + far(proj_full),
+        scratch=[((tokens, width), BF16), ((3, tokens, local), BF16)],
+        fence=True,
+    )
     half = add_low(keep, exchange(send, "head", 1))
+    (across,) = in_vmem(
+        across_body, [((shard + 32, hidden), BF16, "far")], (), far(after(across, send), near)
+    )
+    across = exchange(across, "seq", 4)
     own = add_low(half, exchange(half, "head", 2))
     other = exchange(own, "head", 1)
     proj_blocks = in_vmem(
@@ -1163,13 +1258,6 @@
         far(proj_keep) + (proj_came,),
     )
     proj_blocks = [proj_blocks[0]] + [exchange(proj_blocks[i], "seq", 2 * i) for i in (1, 2, 3)]
-    long_input_grad, short_input_grad = in_vmem(
-        input_grad_body,
-        [(long_input.shape, F32), (short_input.shape, F32)],
-        (place,),
-        (own, other) + far(grad_mid, gain, long_input, short_input),
-        scratch=[((tokens, width), F32)],
-    )
     up_grad, down_grad, out_grad, feed_part = in_vmem(
         ffn_grad_body,
         [
@@ -1179,27 +1267,30 @@
             ((1, shard), F32),
         ],
         (),
-        far(*ffn_blocks, up_weight) + (feed_gain,),
-    )
+        far(after(up_own, proj_blocks[0]), up_near, up_across, ffn_own, near, across, up_weight)
+        + (feed_gain,),
+    )
+    proj_blocks[3] = after(proj_blocks[3], up_grad)
     proj_grad, attention_part = in_vmem(
         proj_grad_body,
         [(proj_weight.shape, F32), ((1, shard), F32)],
         (),
         (*proj_blocks, *far(proj_weight), attention_gain),
     )
+    long_input_grad, short_input_grad = in_vmem(
+        input_grad_body,
+        [(long_input.shape, F32), (short_input.shape, F32)],
+        (place,),
+        (own, other) + far(after(grad_mid, attention_part), gain, long_input, short_input),
+        scratch=[((tokens, width), F32)],
+    )
     gains = jnp.concatenate([attention_part, feed_part], axis=0)
     gains = gains + exchange(gains, "head", 1)
-    gains = gains + exchange(gains, "head", 2)
-
-    f_own, f_other = f_own.astype(F32), f_other.astype(F32)
-    core = lax.axis_index("head") % 2
-    first = jnp.where(core == 0, f_own, f_other)
-    second = jnp.where(core == 0, f_other, f_own)
-    output = (mid + jnp.concatenate([first, second], axis=0)).astype(BF16)
-    output = output.reshape(seqs, rows, width)
+    gains = gains + after(exchange(gains, "head", 2), long_input_grad)
+
     return (
-        output[:, long_rows:],
-        output[:, :long_rows],
+        short_output,
+        long_output,
         short_input_grad,
         long_input_grad,
         proj_grad,

time: 259 us -> 199 us (0.77)
  waiting for transfers between devices: 133 us -> 74.2 us
  Pallas kernels: 51.4 us -> 62.1 us
  starting transfers between devices: 64.2 us -> 54.9 us
  local copies, waits for them, and re-layouts: 7.28 us -> 4.08 us
    ppermute x40 -> x39, waiting for transfers between devices: 103 us -> 67.5 us  [exchange(): return lax.ppermute(array, axis, [(i, i ^ mask) for i in range(size)])]
    all_to_all x1, waiting for transfers between devices: 18.9 us -> 0.01 us  [pair_shards(): came = lax.all_to_all(send, 'seq', 0, 0, tiled=True)]
    pallas_call x16 -> x22, Pallas kernels: 51.4 us -> 62.1 us  [in_vmem(): pl.pallas_call(body, out_shape=[pltpu.HBM(*out[:2]) if len(out) == 3 else...]
    all_to_all x1, waiting for transfers between devices: 5.85 us -> 0.01 us  [pair_shards(): grad_came = lax.all_to_all(send, 'seq', 0, 0, tiled=True)]
    ppermute x40 -> x39, starting transfers between devices: 45.9 us -> 40.7 us  [exchange(): return lax.ppermute(array, axis, [(i, i ^ mask) for i in range(size)])]
    unnamed x52 -> x50, local copies, waits for them, and re-layouts: 5.3 us -> 3.56 us
  transfers between devices with their start and end apart: 44 -> 43, of which waited for: 23 -> 22; matrix products, arithmetic and copies ran while one was open for 1% -> 1% of each run, Pallas kernels for 14% -> 26%
where the time goes in v2:
time: 199 us; the launch traced here: 198 us
  waiting for transfers between devices  74.2 us (37%)
  Pallas kernels  62.1 us (31%)
  starting transfers between devices  54.9 us (28%)
  local copies, waits for them, and re-layouts  4.08 us (2%)
    ppermute x39, waiting for transfers between devices, exchange(): return lax.ppermute(array, axis, [(i, i ^ mask) for i in range(size)])  67.5 us
    pallas_call x22, Pallas kernels, in_vmem(): pl.pallas_call(body, out_shape=[pltpu.HBM(*out[:2]) if len(out) == 3 else...  62.1 us
    ppermute x39, starting transfers between devices, exchange(): return lax.ppermute(array, axis, [(i, i ^ mask) for i in range(size)])  40.7 us
    all_to_all x1, waiting for transfers between devices, pair_shards(): mixed_came = lax.all_to_all(after(send, up_near), 'seq', 0, 0, tiled=True)  5.14 us
  transfers between devices with their start and end apart: 43, of which 22 were waited for; matrix products, arithmetic and copies ran while one was open for 1% of the time, Pallas kernels for 26%

profile of v2, /device:TPU:0, one launch (start us, length us, event | category | flops | bytes accessed | tf_op | source)
XLA Modules:
  0.0 197.9 jit_solution(10490628307556551784)
XLA Ops:
  2.3 5.1 %collective-permute-start.5 = (bf16[448,128]{1,0:T(8,128)(2,1)S(1)}, bf16[448,128]{1,0:T(8,128)(2,1)S(1)}, u32[]{:S(2)}, u32[]{:S(2)}) collective-permute-start(bf16[448,128]{1,0:T(8,128)(2,1)S(1)} %shard_map.212.refs_0_), channel_id=1, source_target_pairs={{0,24},{4,28},{8,16},{12,20},{16,8},{20,12},{24,0},{28,4},{1,25},{... | collective-permute-start | bytes 344072 | tf_op jit(solution)/shard_map/ppermute | solution.py:412
  13.2 3.9 %collective-permute-done.3.refs_4_ = bf16[448,128]{1,0:T(8,128)(2,1)S(1)} collective-permute-done((bf16[448,128]{1,0:T(8,128)(2,1)S(1)}, bf16[448,128]{1,0:T(8,128)(2,1)S(1)}, u32[]{:S(2)}, u32[]{:S(2)}) %collective-permute-start.3) | collective-permute-done | bytes 114720 | tf_op jit(solution)/shard_map/ppermute | solution.py:412
  25.6 3.1 %shard_map.213 = (bf16[8,304,128]{2,1,0:T(8,128)(2,1)}, bf16[384,768]{1,0:T(8,128)(2,1)}, bf16[3,768,192]{2,1,0:T(8,128)(2,1)}, f32[1,768]{1,0:T(1,128)}) custom-call(s32[2]{0:T(128)S(1)} %pad_add_fusion.place, bf16[448,128]{1,0:T(8,128)(2,1)S(1)} %shard_map.212.refs_0_, bf16[448,128]{1,0:T(8,128)(2,1)S(1)} %collective-permute-done.refs_1_, ...), custom_call_target="tpu_custom_call" | custom-call | flops 99999997952 | tf_op jit(solution)/shard_map/pallas_call | solution.py:373
  28.7 3.7 %all-to-all-start = ((bf16[8,304,128]{2,1,0:T(8,128)(2,1)}), bf16[8,304,128]{2,1,0:T(8,128)(2,1)S(1)}, u32[]{:S(2)}, u32[]{:S(2)}) async-start(bf16[8,304,128]{2,1,0:T(8,128)(2,1)} %get-tuple-element.89), calls=%async_computation | async-start | bytes 1245184 | tf_op jit(solution)/shard_map/all_to_all | solution.py:1084
  32.4 6.1 %collective-permute-done.9.refs_4_ = bf16[224,768]{1,0:T(8,128)(2,1)S(1)} collective-permute-done((bf16[224,768]{1,0:T(8,128)(2,1)S(1)}, bf16[224,768]{1,0:T(8,128)(2,1)S(1)}, u32[]{:S(2)}, u32[]{:S(2)}) %collective-permute-start.9) | collective-permute-done | bytes 344096 | tf_op jit(solution)/shard_map/ppermute | solution.py:412
  40.7 14.5 %collective-permute-done.12.refs_6_ = bf16[224,768]{1,0:T(8,128)(2,1)S(1)} collective-permute-done((bf16[224,768]{1,0:T(8,128)(2,1)S(1)}, bf16[224,768]{1,0:T(8,128)(2,1)S(1)}, u32[]{:S(2)}, u32[]{:S(2)}) %collective-permute-start.12) | collective-permute-done | bytes 344096 | tf_op jit(solution)/shard_map/ppermute | solution.py:412
  56.7 4.5 %shard_map.214 = (bf16[8,96,128]{2,1,0:T(8,128)(2,1)}, bf16[1536,64]{1,0:T(8,128)(2,1)}, bf16[1536,128]{1,0:T(8,128)(2,1)}, f32[64,1536]{1,0:T(8,128)}, f32[1,1536]{1,0:T(1,128)}, /*index=5*/bf16[8,304,128]{2,1,0:T(8,128)(2,1)}) custom-call(s32[2]{0:T(128)S(1)} %pad_add_fusion.place, s32[2]{0:T(128)S(1)} %copy-done.1, s32[2]{0:T(128)S(1)} %copy-done.2, ...), custom_call_target="tpu_custom_call" | custom-call | flops 99999997952 | tf_op jit(solution)/shard_map/pallas_call | solution.py:373
  61.3 3.4 %all-to-all-start.1 = ((bf16[8,96,128]{2,1,0:T(8,128)(2,1)}), bf16[8,96,128]{2,1,0:T(8,128)(2,1)S(1)}, u32[]{:S(2)}, u32[]{:S(2)}) async-start(bf16[8,96,128]{2,1,0:T(8,128)(2,1)} %get-tuple-element.90), calls=%async_computation.1 | async-start | bytes 393216 | tf_op jit(solution)/shard_map/all_to_all | solution.py:1105
  67.7 3.5 %shard_map.216 = (bf16[8,192,768]{2,1,0:T(8,128)(2,1)}, bf16[768,192]{1,0:T(8,128)(2,1)}) custom-call(s32[2]{0:T(128)S(1)} %pad_add_fusion.place, bf16[224,768]{1,0:T(8,128)(2,1)} %copy-done, bf16[224,768]{1,0:T(8,128)(2,1)} %copy-done.11, bf16[224,768]{1,0:T(8,128)(2,1)} %copy-done.10, bf16[224,768]{1,0:T(8,128)(2,1)} %copy-done.14, ...), custom_call_target="tpu_custom_call" | custom-call | tf_op jit(solution)/shard_map/pallas_call | solution.py:373
  77.9 7.6 %collective-permute-done.15 = bf16[192,768]{1,0:T(8,128)(2,1)S(1)} collective-permute-done((bf16[192,768]{1,0:T(8,128)(2,1)S(1)}, bf16[192,768]{1,0:T(8,128)(2,1)S(1)}, u32[]{:S(2)}, u32[]{:S(2)}) %collective-permute-start.15) | collective-permute-done | bytes 294944 | tf_op jit(solution)/shard_map/ppermute | solution.py:412
  87.2 4.9 %shard_map.218 = (f32[384,768]{1,0:T(8,128)}, bf16[384,768]{1,0:T(8,128)(2,1)}, bf16[384,768]{1,0:T(8,128)(2,1)}, bf16[384,768]{1,0:T(8,128)(2,1)}, bf16[384,768...) custom-call(s32[2]{0:T(128)S(1)} %pad_add_fusion.place, s32[2]{0:T(128)S(1)} %copy-done.1, ...), custom_call_target="tpu_custom_call" | custom-call | tf_op jit(solution)/shard_map/pallas_call | solution.py:373
  95.3 3.3 %shard_map.219 = (bf16[4,96,768]{2,1,0:T(8,128)(2,1)}, bf16[4,96,768]{2,1,0:T(8,128)(2,1)}) custom-call(s32[2]{0:T(128)S(1)} %pad_add_fusion.place, bf16[384,768]{1,0:T(8,128)(2,1)} %get-tuple-element.104.normed, bf16[384,768]{1,0:T(8,128)(2,1)} %get-tuple-element.105.grad_up), custom_call_target="tpu_custom_call" | custom-call | tf_op jit(solution)/shard_map/pallas_call | solution.py:373
  98.6 4.6 %shard_map.220 = (bf16[4,96,768]{2,1,0:T(8,128)(2,1)}, bf16[4,96,768]{2,1,0:T(8,128)(2,1)}, bf16[192,768]{1,0:T(8,128)(2,1)}, bf16[192,768]{1,0:T(8,128)(2,1)}) custom-call(s32[2]{0:T(128)S(1)} %pad_add_fusion.place, bf16[384,768]{1,0:T(8,128)(2,1)} %get-tuple-element.107.squared, bf16[384,768]{1,0:T(8,128)(2,1)} %get-tuple-element.108.grad_out, ...), custom_call_target="tpu_custom_call" | custom-call | flops 99999997952 | tf_op jit(solution)/shard_map/pallas_call | solution.py:373
  104.9 3.6 %shard_map.222 = (f32[384,768]{1,0:T(8,128)}, bf16[8,96,128]{2,1,0:T(8,128)(2,1)}, bf16[4,32,768]{2,1,0:T(8,128)(2,1)}, bf16[4,32,768]{2,1,0:T(8,128)(2,1)}) custom-call(s32[2]{0:T(128)S(1)} %pad_add_fusion.place, bf16[192,768]{1,0:T(8,128)(2,1)S(1)} %add_convert_fusion.2.own, bf16[192,768]{1,0:T(8,128)(2,1)S(1)} %collective-permute-done.22.other, ...), custom_call_target="tpu_custom_call" | custom-call | flops 99999997952 | tf_op jit(solution)/shard_map/pallas_call | solution.py:373
  108.4 3.6 %all-to-all-start.2 = ((bf16[8,96,128]{2,1,0:T(8,128)(2,1)}), bf16[8,96,128]{2,1,0:T(8,128)(2,1)S(1)}, u32[]{:S(2)}, u32[]{:S(2)}) async-start(bf16[8,96,128]{2,1,0:T(8,128)(2,1)} %get-tuple-element.122), calls=%async_computation.2 | async-start | bytes 393216 | tf_op jit(solution)/shard_map/all_to_all | solution.py:1185
  113.9 7.2 %collective-permute-done.23.refs_1_ = bf16[4,96,768]{2,1,0:T(8,128)(2,1)S(1)} collective-permute-done((bf16[4,96,768]{2,1,0:T(8,128)(2,1)S(1)}, bf16[4,96,768]{2,1,0:T(8,128)(2,1)S(1)}, u32[]{:S(2)}, u32[]{:S(2)}) %collective-permute-start.23) | collective-permute-done | bytes 589856 | tf_op jit(solution)/shard_map/ppermute | solution.py:412
  127.8 5.9 %shard_map.224 = bf16[8,304,128]{2,1,0:T(8,128)(2,1)} custom-call(s32[2]{0:T(128)S(1)} %pad_add_fusion.place, s32[2]{0:T(128)S(1)} %copy-done.1, s32[2]{0:T(128)S(1)} %copy-done.2, bf16[8,304,128]{2,1,0:T(8,128)(2,1)} %get-tuple-element.114.came, bf16[1536,64]{1,0:T(8,128)(2,1)} %get-tuple-element.115.q_all, bf16[1536,128]{1,0:T(8,128)(2,1)} %get-tuple-element.116.kv_all, ...), custom_call_target="tpu_custom_call" | custom-call | tf_op jit(solution)/shard_map/pallas_call | solution.py:373
  133.7 3.5 %all-to-all-start.3 = ((bf16[8,304,128]{2,1,0:T(8,128)(2,1)}), bf16[8,304,128]{2,1,0:T(8,128)(2,1)S(1)}, u32[]{:S(2)}, u32[]{:S(2)}) async-start(bf16[8,304,128]{2,1,0:T(8,128)(2,1)} %shard_map.224), calls=%async_computation.3 | async-start | bytes 1245184 | tf_op jit(solution)/shard_map/all_to_all | solution.py:1213
  149.0 5.1 %all-to-all-done.3.came = bf16[8,304,128]{2,1,0:T(8,128)(2,1)S(1)} async-done(((bf16[8,304,128]{2,1,0:T(8,128)(2,1)}), bf16[8,304,128]{2,1,0:T(8,128)(2,1)S(1)}, u32[]{:S(2)}, u32[]{:S(2)}) %all-to-all-start.3) | async-done | bytes 622624 | tf_op jit(solution)/shard_map/all_to_all | solution.py:1213
  154.2 3.3 %shard_map.226 = (bf16[4,432,128]{2,1,0:T(8,128)(2,1)}, bf16[4,432,128]{2,1,0:T(8,128)(2,1)}) custom-call(s32[2]{0:T(128)S(1)} %pad_add_fusion.place, bf16[8,304,128]{2,1,0:T(8,128)(2,1)S(1)} %all-to-all-done.3.came, bf16[384,768]{1,0:T(8,128)(2,1)} %get-tuple-element.137.normed), custom_call_target="tpu_custom_call" | custom-call | tf_op jit(solution)/shard_map/pallas_call | solution.py:373
  157.8 3.0 %collective-permute-done.28.near = bf16[2,128,768]{2,1,0:T(8,128)(2,1)S(1)} collective-permute-done((bf16[2,128,768]{2,1,0:T(8,128)(2,1)}, bf16[2,128,768]{2,1,0:T(8,128)(2,1)S(1)}, u32[]{:S(2)}, u32[]{:S(2)}) %collective-permute-start.28) | collective-permute-done | bytes 393248 | tf_op jit(solution)/shard_map/ppermute | solution.py:412
  168.5 7.6 %collective-permute-done.32.refs_1_ = bf16[4,432,128]{2,1,0:T(8,128)(2,1)S(1)} collective-permute-done((bf16[4,432,128]{2,1,0:T(8,128)(2,1)S(1)}, bf16[4,432,128]{2,1,0:T(8,128)(2,1)S(1)}, u32[]{:S(2)}, u32[]{:S(2)}) %collective-permute-start.32) | collective-permute-done | bytes 442400 | tf_op jit(solution)/shard_map/ppermute | solution.py:412
  185.8 4.3 %collective-permute-done.34.b2 = bf16[432,128]{1,0:T(8,128)(2,1)S(1)} collective-permute-done((bf16[432,128]{1,0:T(8,128)(2,1)S(1)}, bf16[432,128]{1,0:T(8,128)(2,1)S(1)}, u32[]{:S(2)}, u32[]{:S(2)}) %collective-permute-start.34) | collective-permute-done | bytes 110624 | tf_op jit(solution)/shard_map/ppermute | solution.py:412
  194.4 3.0 %shard_map.233 = (f32[2,128,768]{2,1,0:T(8,128)}, f32[2,64,768]{2,1,0:T(8,128)}) custom-call(s32[2]{0:T(128)S(1)} %pad_add_fusion.place, bf16[192,768]{1,0:T(8,128)(2,1)S(1)} %add_convert_fusion.own, bf16[192,768]{1,0:T(8,128)(2,1)S(1)} %collective-permute-done.31.other, f32[384,768]{1,0:T(8,128)} %get-tuple-element.157.grad_mid, ...), custom_call_target="tpu_custom_call" | custom-call | tf_op jit(solution)/shard_map/pallas_call | solution.py:373
  (147 shorter events, 78.9 us)
Async XLA Ops:
  7.4 11.2 %collective-permute-start.1 = (bf16[448,128]{1,0:T(8,128)(2,1)S(1)}, bf16[448,128]{1,0:T(8,128)(2,1)S(1)}, u32[]{:S(2)}, u32[]{:S(2)}) collective-permute-start(bf16[448,128]{1,0:T(8,128)(2,1)S(1)} %shard_map.212.refs_0_), channel_id=1, source_target_pairs={{0,8},{4,12},{8,0},{12,4},{16,24},{20,28},{24,16},{28,20},{1,9},{5... | collective-permute-start | bytes 344072 | tf_op jit(solution)/shard_map/ppermute | solution.py:412
  8.1 14.8 %collective-permute-start = (bf16[448,128]{1,0:T(8,128)(2,1)S(1)}, bf16[448,128]{1,0:T(8,128)(2,1)S(1)}, u32[]{:S(2)}, u32[]{:S(2)}) collective-permute-start(bf16[448,128]{1,0:T(8,128)(2,1)S(1)} %shard_map.212.refs_0_), channel_id=1, source_target_pairs={{0,4},{4,0},{8,12},{12,8},{16,20},{20,16},{24,28},{28,24},{1,5},{5... | collective-permute-start | bytes 344072 | tf_op jit(solution)/shard_map/ppermute | solution.py:412
  11.5 12.6 %collective-permute-start.6 = (bf16[448,128]{1,0:T(8,128)(2,1)S(1)}, bf16[448,128]{1,0:T(8,128)(2,1)S(1)}, u32[]{:S(2)}, u32[]{:S(2)}) collective-permute-start(bf16[448,128]{1,0:T(8,128)(2,1)S(1)} %collective-permute-done.5.refs_6_), channel_id=1, source_target_pairs={{0,4},{4,0},{8,12},{12,8},{16,20},{20,16},{24,28},{28,24},{1,5},{5... | collective-permute-start | bytes 344072 | tf_op jit(solution)/shard_map/ppermute | solution.py:412
  21.1 17.4 %collective-permute-start.9 = (bf16[224,768]{1,0:T(8,128)(2,1)S(1)}, bf16[224,768]{1,0:T(8,128)(2,1)S(1)}, u32[]{:S(2)}, u32[]{:S(2)}) collective-permute-start(bf16[224,768]{1,0:T(8,128)(2,1)S(1)} %shard_map.215.refs_0_), channel_id=1, source_target_pairs={{0,16},{4,20},{8,24},{12,28},{16,0},{20,4},{24,8},{28,12},{1,17},{... | collective-permute-start | bytes 1032200 | tf_op jit(solution)/shard_map/ppermute | solution.py:412
  22.9 17.4 %collective-permute-start.8 = (bf16[224,768]{1,0:T(8,128)(2,1)S(1)}, bf16[224,768]{1,0:T(8,128)(2,1)S(1)}, u32[]{:S(2)}, u32[]{:S(2)}) collective-permute-start(bf16[224,768]{1,0:T(8,128)(2,1)S(1)} %shard_map.215.refs_0_), channel_id=1, source_target_pairs={{0,8},{4,12},{8,0},{12,4},{16,24},{20,28},{24,16},{28,20},{1,9},{5... | collective-permute-start | bytes 1032200 | tf_op jit(solution)/shard_map/ppermute | solution.py:412
  24.1 14.4 %collective-permute-start.7 = (bf16[224,768]{1,0:T(8,128)(2,1)S(1)}, bf16[224,768]{1,0:T(8,128)(2,1)S(1)}, u32[]{:S(2)}, u32[]{:S(2)}) collective-permute-start(bf16[224,768]{1,0:T(8,128)(2,1)S(1)} %shard_map.215.refs_0_), channel_id=1, source_target_pairs={{0,4},{4,0},{8,12},{12,8},{16,20},{20,16},{24,28},{28,24},{1,5},{5... | collective-permute-start | bytes 1032200 | tf_op jit(solution)/shard_map/ppermute | solution.py:412
  28.7 28.0 %all-to-all-start = ((bf16[8,304,128]{2,1,0:T(8,128)(2,1)}), bf16[8,304,128]{2,1,0:T(8,128)(2,1)S(1)}, u32[]{:S(2)}, u32[]{:S(2)}) async-start(bf16[8,304,128]{2,1,0:T(8,128)(2,1)} %get-tuple-element.89), calls=%async_computation | async-start | bytes 1245184 | tf_op jit(solution)/shard_map/all_to_all | solution.py:1084
  38.5 16.7 %collective-permute-start.12 = (bf16[224,768]{1,0:T(8,128)(2,1)S(1)}, bf16[224,768]{1,0:T(8,128)(2,1)S(1)}, u32[]{:S(2)}, u32[]{:S(2)}) collective-permute-start(bf16[224,768]{1,0:T(8,128)(2,1)S(1)} %collective-permute-done.9.refs_4_), channel_id=1, source_target_pairs={{0,8},{4,12},{8,0},{12,4},{16,24},{20,28},{24,16},{28,20},{1,9},{5... | collective-permute-start | bytes 1032200 | tf_op jit(solution)/shard_map/ppermute | solution.py:412
  38.6 26.2 %collective-permute-start.11 = (bf16[224,768]{1,0:T(8,128)(2,1)S(1)}, bf16[224,768]{1,0:T(8,128)(2,1)S(1)}, u32[]{:S(2)}, u32[]{:S(2)}) collective-permute-start(bf16[224,768]{1,0:T(8,128)(2,1)S(1)} %collective-permute-done.9.refs_4_), channel_id=1, source_target_pairs={{0,4},{4,0},{8,12},{12,8},{16,20},{20,16},{24,28},{28,24},{1,5},{5... | collective-permute-start | bytes 1032200 | tf_op jit(solution)/shard_map/ppermute | solution.py:412
  40.2 24.5 %collective-permute-start.10 = (bf16[224,768]{1,0:T(8,128)(2,1)S(1)}, bf16[224,768]{1,0:T(8,128)(2,1)S(1)}, u32[]{:S(2)}, u32[]{:S(2)}) collective-permute-start(bf16[224,768]{1,0:T(8,128)(2,1)S(1)} %collective-permute-done.8.refs_2_), channel_id=1, source_target_pairs={{0,4},{4,0},{8,12},{12,8},{16,20},{20,16},{24,28},{28,24},{1,5},{5... | collective-permute-start | bytes 1032200 | tf_op jit(solution)/shard_map/ppermute | solution.py:412
  55.2 12.4 %collective-permute-start.13 = (bf16[224,768]{1,0:T(8,128)(2,1)S(1)}, bf16[224,768]{1,0:T(8,128)(2,1)}, u32[]{:S(2)}, u32[]{:S(2)}) collective-permute-start(bf16[224,768]{1,0:T(8,128)(2,1)S(1)} %collective-permute-done.12.refs_6_), channel_id=1, source_target_pairs={{0,4},{4,0},{8,12},{12,8},{16,20},{20,16},{24,28},{28,24},{1,5},{5... | collective-permute-start | bytes 1032200 | tf_op jit(solution)/shard_map/ppermute | solution.py:412
  61.3 11.4 %all-to-all-start.1 = ((bf16[8,96,128]{2,1,0:T(8,128)(2,1)}), bf16[8,96,128]{2,1,0:T(8,128)(2,1)S(1)}, u32[]{:S(2)}, u32[]{:S(2)}) async-start(bf16[8,96,128]{2,1,0:T(8,128)(2,1)} %get-tuple-element.90), calls=%async_computation.1 | async-start | bytes 393216 | tf_op jit(solution)/shard_map/all_to_all | solution.py:1105
  103.3 17.8 %collective-permute-start.23 = (bf16[4,96,768]{2,1,0:T(8,128)(2,1)S(1)}, bf16[4,96,768]{2,1,0:T(8,128)(2,1)S(1)}, u32[]{:S(2)}, u32[]{:S(2)}) collective-permute-start(bf16[4,96,768]{2,1,0:T(8,128)(2,1)S(1)} %copy-done.20), channel_id=1, source_target_pairs={{0,4},{4,0},{8,12},{12,8},{16,20},{20,16},{24,28},{28,24},{1,5},{5... | collective-permute-start | bytes 1769480 | tf_op jit(solution)/shard_map/ppermute | solution.py:412
  104.3 21.2 %collective-permute-start.18 = (bf16[192,768]{1,0:T(8,128)(2,1)}, bf16[192,768]{1,0:T(8,128)(2,1)}, u32[]{:S(2)}, u32[]{:S(2)}) collective-permute-start(bf16[192,768]{1,0:T(8,128)(2,1)} %get-tuple-element.110), channel_id=1, source_target_pairs={{0,1},{1,0},{2,3},{3,2},{4,5},{5,4},{6,7},{7,6},{8,9},{9,8},{10,11... | collective-permute-start | bytes 884744 | tf_op jit(solution)/shard_map/ppermute | solution.py:412
  108.4 19.4 %all-to-all-start.2 = ((bf16[8,96,128]{2,1,0:T(8,128)(2,1)}), bf16[8,96,128]{2,1,0:T(8,128)(2,1)S(1)}, u32[]{:S(2)}, u32[]{:S(2)}) async-start(bf16[8,96,128]{2,1,0:T(8,128)(2,1)} %get-tuple-element.122), calls=%async_computation.2 | async-start | bytes 393216 | tf_op jit(solution)/shard_map/all_to_all | solution.py:1185
  112.0 25.3 %collective-permute-start.25 = (bf16[4,96,768]{2,1,0:T(8,128)(2,1)S(1)}, bf16[4,96,768]{2,1,0:T(8,128)(2,1)S(1)}, u32[]{:S(2)}, u32[]{:S(2)}) collective-permute-start(bf16[4,96,768]{2,1,0:T(8,128)(2,1)S(1)} %copy-done.18), channel_id=1, source_target_pairs={{0,4},{4,0},{8,12},{12,8},{16,20},{20,16},{24,28},{28,24},{1,5},{5... | collective-permute-start | bytes 1769480 | tf_op jit(solution)/shard_map/ppermute | solution.py:412
  124.3 13.7 %collective-permute-start.26 = (bf16[4,32,768]{2,1,0:T(8,128)(2,1)S(1)}, bf16[4,32,768]{2,1,0:T(8,128)(2,1)S(1)}, u32[]{:S(2)}, u32[]{:S(2)}) collective-permute-start(bf16[4,32,768]{2,1,0:T(8,128)(2,1)S(1)} %copy-done.23), channel_id=1, source_target_pairs={{0,4},{4,0},{8,12},{12,8},{16,20},{20,16},{24,28},{28,24},{1,5},{5... | collective-permute-start | bytes 589832 | tf_op jit(solution)/shard_map/ppermute | solution.py:412
  126.5 15.9 %collective-permute-start.19 = (bf16[192,768]{1,0:T(8,128)(2,1)S(1)}, bf16[192,768]{1,0:T(8,128)(2,1)S(1)}, u32[]{:S(2)}, u32[]{:S(2)}) collective-permute-start(bf16[192,768]{1,0:T(8,128)(2,1)S(1)} %add_convert_fusion.4), channel_id=1, source_target_pairs={{0,2},{1,3},{2,0},{3,1},{4,6},{5,7},{6,4},{7,5},{8,10},{9,11},{10,... | collective-permute-start | bytes 884744 | tf_op jit(solution)/shard_map/ppermute | solution.py:412
  133.7 20.4 %all-to-all-start.3 = ((bf16[8,304,128]{2,1,0:T(8,128)(2,1)}), bf16[8,304,128]{2,1,0:T(8,128)(2,1)S(1)}, u32[]{:S(2)}, u32[]{:S(2)}) async-start(bf16[8,304,128]{2,1,0:T(8,128)(2,1)} %shard_map.224), calls=%async_computation.3 | async-start | bytes 1245184 | tf_op jit(solution)/shard_map/all_to_all | solution.py:1213
  141.0 19.7 %collective-permute-start.28 = (bf16[2,128,768]{2,1,0:T(8,128)(2,1)}, bf16[2,128,768]{2,1,0:T(8,128)(2,1)S(1)}, u32[]{:S(2)}, u32[]{:S(2)}) collective-permute-start(bf16[2,128,768]{2,1,0:T(8,128)(2,1)} %get-tuple-element.142), channel_id=1, source_target_pairs={{0,8},{4,12},{8,0},{12,4},{16,24},{20,28},{24,16},{28,20},{1,9},{5... | collective-permute-start | bytes 1179656 | tf_op jit(solution)/shard_map/ppermute | solution.py:412
  144.4 13.4 %collective-permute-start.27 = (bf16[96,768]{1,0:T(8,128)(2,1)}, bf16[96,768]{1,0:T(8,128)(2,1)S(1)}, u32[]{:S(2)}, u32[]{:S(2)}) collective-permute-start(bf16[96,768]{1,0:T(8,128)(2,1)} %shard_map.227), channel_id=1, source_target_pairs={{0,16},{4,20},{8,24},{12,28},{16,0},{20,4},{24,8},{28,12},{1,17},{... | collective-permute-start | bytes 442376 | tf_op jit(solution)/shard_map/ppermute | solution.py:412
  163.5 12.6 %collective-permute-start.32 = (bf16[4,432,128]{2,1,0:T(8,128)(2,1)S(1)}, bf16[4,432,128]{2,1,0:T(8,128)(2,1)S(1)}, u32[]{:S(2)}, u32[]{:S(2)}) collective-permute-start(bf16[4,432,128]{2,1,0:T(8,128)(2,1)S(1)} %copy-done.22), channel_id=1, source_target_pairs={{0,4},{4,0},{8,12},{12,8},{16,20},{20,16},{24,28},{28,24},{1,5},{5... | collective-permute-start | bytes 1327112 | tf_op jit(solution)/shard_map/ppermute | solution.py:412
  165.2 26.6 %collective-permute-start.30 = (bf16[192,768]{1,0:T(8,128)(2,1)S(1)}, bf16[192,768]{1,0:T(8,128)(2,1)S(1)}, u32[]{:S(2)}, u32[]{:S(2)}) collective-permute-start(bf16[192,768]{1,0:T(8,128)(2,1)S(1)} %add_convert_fusion.1), channel_id=1, source_target_pairs={{0,2},{1,3},{2,0},{3,1},{4,6},{5,7},{6,4},{7,5},{8,10},{9,11},{10,... | collective-permute-start | bytes 884744 | tf_op jit(solution)/shard_map/ppermute | solution.py:412
  167.9 13.9 %collective-permute-start.36 = (bf16[128,768]{1,0:T(8,128)(2,1)}, bf16[128,768]{1,0:T(8,128)(2,1)S(1)}, u32[]{:S(2)}, u32[]{:S(2)}) collective-permute-start(bf16[128,768]{1,0:T(8,128)(2,1)} %shard_map.230), channel_id=1, source_target_pairs={{0,16},{4,20},{8,24},{12,28},{16,0},{20,4},{24,8},{28,12},{1,17},{... | collective-permute-start | bytes 589832 | tf_op jit(solution)/shard_map/ppermute | solution.py:412
  (44 other events, 323.1 us)

commit v3 on v2

--- a/solution.py
+++ b/solution.py
@@ -640,16 +640,19 @@
     short_cot,
     gathered,
     mid_ref,
-    normed_ref,
     squared_ref,
-    grad_up_ref,
     grad_out_ref,
     keep,
     send,
+    up_keep,
+    up_send,
     scratch,
     attended,
     up,
     down,
+    blocks,
+    normed_ref,
+    grad_up_ref,
 ):
     seqs = long_in.shape[0]
     shard = gathered.shape[1] // 2
@@ -680,6 +683,10 @@
     grad_up_ref[...] = (grad_squared * 2.0 * relu).astype(BF16)
     scratch[...] = dot(grad_up_ref[...], up[...], NT).astype(BF16)
     split_halves(place, scratch, keep, send)
+    term = dot(normed_ref[...], grad_up_ref[...], TN).astype(BF16)
+    for s in range(8):
+        blocks[s] = term[s * shard : (s + 1) * shard]
+    split_y(place, blocks, up_keep, up_send)
 
 
 def split_halves(place, whole, keep, send):
@@ -703,16 +710,8 @@
         send[z] = blocks[2 * z + 1 - y]
 
 
-def up_term_body(place, normed, grad_up, keep, send, blocks):
-    rows = blocks.shape[1]
-    term = dot(normed[...], grad_up[...], TN).astype(BF16)
-    for s in range(8):
-        blocks[s] = term[s * rows : (s + 1) * rows]
-    split_y(place, blocks, keep, send)
-
-
 def down_term_body(
-    place, squared, grad_out, gathered, keep, send, f_keep, f_send, scratch, down, blocks
+    place, squared, grad_out, gathered, near, own, across, f_keep, f_send, scratch, down, blocks
 ):
     rows = gathered.shape[1] // 2
     for s in range(8):
@@ -720,9 +719,24 @@
     term = dot(grad_out[...], squared[...], TN).astype(BF16)
     for s in range(8):
         blocks[s] = term[s * rows : (s + 1) * rows]
-    split_y(place, blocks, keep, send)
+    z = place[0] // 2
+    for i, target in ((0, own), (1, near.at[0]), (2, across), (3, near.at[1])):
+        for y in range(2):
+            target[y] = blocks[2 * jnp.bitwise_xor(z, i) + y]
     scratch[...] = dot(squared[...], down[...], NT).astype(BF16)
     split_halves(place, scratch, f_keep, f_send)
+
+
+def down_across_body(across, near, out):
+    out[...] = (across[...].astype(F32) + near[1].astype(F32)).astype(BF16)
+
+
+def down_y_body(place, own, near, across, keep, send):
+    y = place[0] % 2
+    for target, block in ((keep, y), (send, 1 - y)):
+        target[...] = (
+            own[block].astype(F32) + near[0, block].astype(F32) + across[block].astype(F32)
+        ).astype(BF16)
 
 
 def middle_body(
@@ -883,7 +897,9 @@
             grad_mixed[2, at, lanes] = came[j, :rows, HEAD_DIM:]
 
 
-def proj_term_body(place, came, normed, keep, send, grad_mixed, blocks):
+def project_back_body(
+    place, came, normed, weight, keep_p, send_p, keep, send, taps, scratch, grad_mixed, blocks
+):
     place_grad_mixed(came, grad_mixed)
     shard = normed.shape[1] // 8
     terms = [dot(normed[...], grad_mixed[c], TN).astype(BF16) for c in range(3)]
@@ -894,11 +910,7 @@
         blocks[s, 3 * shard :, :] = fold(
             jnp.concatenate([terms[c][at, LANES:] for c in range(3)], axis=0)
         )
-    split_y(place, blocks, keep, send)
-
-
-def project_back_body(place, came, weight, keep, send, taps, scratch, grad_mixed):
-    place_grad_mixed(came, grad_mixed)
+    split_y(place, blocks, keep_p, send_p)
     rows = (came.shape[1] - 16) * 2 // 3
     total = came[0, rows + rows // 2 :, :].astype(F32)
     for j in range(1, 6):
@@ -993,14 +1005,14 @@
 
 
 def ffn_grad_body(
-    up_own, up_near, up_across, own, near, across, up, gain, up_grad, down_grad, out_grad, gain_grad
+    own, near, across, down_keep, down_came, up, gain, up_grad, down_grad, out_grad, gain_grad
 ):
     rows = up.shape[0]
-    raw = up_own[...].astype(F32) + up_near[0].astype(F32) + up_across[...].astype(F32)
     total = own[...].astype(F32) + near[0].astype(F32) + across[...].astype(F32)
+    raw = total[:rows]
     gain_grad[...] = jnp.sum(raw * up[...].astype(F32), axis=1, keepdims=True).T
     up_grad[...] = raw * gain[...].astype(F32).reshape(1, rows).T
-    down_grad[...] = total[:rows]
+    down_grad[...] = down_keep[...].astype(F32) + down_came[...].astype(F32)
     wide = total[rows : rows + 16]
     narrow = total[rows + 16 :]
     out = jnp.concatenate(
@@ -1124,16 +1136,16 @@
     half = add_low(keep, exchange(send, "head", 1))
     own = add_low(half, exchange(half, "head", 2))
     other = exchange(own, "head", 1)
-    mid, normed_ffn, squared, grad_up, grad_out, keep, send = in_vmem(
+    mid, squared, grad_out, keep, send, up_keep, up_send = in_vmem(
         functools.partial(feed_body, long_rows),
         [
             ((tokens, width), F32, "far"),
-            ((tokens, width), BF16, "far"),
-            ((tokens, hidden), BF16, "far"),
             ((tokens, hidden), BF16, "far"),
             ((tokens, width), BF16, "far"),
             ((tokens // 2, width), BF16),
             ((tokens // 2, width), BF16),
+            ((4, shard, hidden), BF16, "far"),
+            ((4, shard, hidden), BF16, "far"),
         ],
         (place, long_lengths, short_lengths),
         (own, other)
@@ -1143,23 +1155,21 @@
             ((tokens, width), F32),
             ((width, hidden), BF16),
             ((width, hidden), BF16),
+            ((8, shard, hidden), BF16),
+            ((tokens, width), BF16),
+            ((tokens, hidden), BF16),
         ],
         limit_mib=32,
     )
     half = add_low(keep, exchange(send, "head", 1))
-    up_keep, up_send = in_vmem(
-        up_term_body,
-        [((4, shard, hidden), BF16, "far")] * 2,
+    up_came = exchange(up_send, "seq", 1)
+    down_near, down_own, down_across, f_keep, f_send = in_vmem(
+        down_term_body,
+        [((2, 2, shard, hidden), BF16, "far")]
+        + [((2, shard, hidden), BF16, "far")] * 2
+        + [((tokens // 2, width), BF16, "far")] * 2,
         (place,),
-        far(after(normed_ffn, half), grad_up),
-        scratch=[((8, shard, hidden), BF16)],
-    )
-    up_came = exchange(up_send, "seq", 1)
-    down_keep, down_send, f_keep, f_send = in_vmem(
-        down_term_body,
-        [((4, shard, hidden), BF16, "far")] * 2 + [((tokens // 2, width), BF16, "far")] * 2,
-        (place,),
-        far(after(squared, up_send), grad_out, ffn_full),
+        far(after(squared, half), grad_out, ffn_full),
         scratch=[
             ((tokens, width), BF16),
             ((width, hidden), BF16),
@@ -1167,7 +1177,8 @@
         ],
         fence=True,
     )
-    own = add_low(half, after(exchange(half, "head", 2), down_send))
+    down_near = exchange(down_near, "seq", 2)
+    own = add_low(half, after(exchange(half, "head", 2), f_send))
     other = exchange(own, "head", 1)
     grad_mid, send, out_keep, out_send = in_vmem(
         middle_body,
@@ -1180,21 +1191,19 @@
         (place,),
         (own, other) + far(mid, grad_out, out_full, att),
         scratch=[((tokens, width), F32), ((tokens, width), BF16), ((8, 32, hidden), BF16)],
+    )
+    grad_came = lax.all_to_all(send, "seq", 0, 0, tiled=True)
+    out_came = exchange(out_send, "seq", 1)
+    (down_across,) = in_vmem(
+        down_across_body,
+        [((2, shard, hidden), BF16, "far")],
+        (),
+        far(after(down_across, send, up_came), down_near),
         fence=True,
     )
-    grad_came = lax.all_to_all(send, "seq", 0, 0, tiled=True)
-    down_came = exchange(after(down_send, send), "seq", 1)
-    out_came = exchange(out_send, "seq", 1)
-    up_near, up_own, up_across = in_vmem(
-        near_body,
-        [((2, shard, hidden), BF16, "far")] + [((shard, hidden), BF16, "far")] * 2,
-        (place,),
-        far(up_keep, after(up_came, grad_mid)),
-        fence=True,
-    )
-    up_near = exchange(up_near, "seq", 2)
-    grad_came = after(grad_came, up_own)
-    f_half = add_low(f_keep, exchange(f_send, "head", 1))
+    grad_came = after(grad_came, down_across)
+    down_across = exchange(down_across, "seq", 4)
+    f_half = add_low(f_keep, exchange(after(f_send, send), "head", 1))
     f_own = add_low(f_half, exchange(f_half, "head", 2))
     f_other = exchange(f_own, "head", 1)
     long_output, short_output = in_vmem(
@@ -1209,47 +1218,51 @@
         [((8, chunk, LANES), BF16)],
         (place, long_lengths, short_lengths),
         far(mixed, q_all, kv_all, att_t, log_row) + (grad_came,),
-    )
-    mixed_came = lax.all_to_all(after(send, up_near), "seq", 0, 0, tiled=True)
+        fence=True,
+    )
+    mixed_came = lax.all_to_all(send, "seq", 0, 0, tiled=True)
+    down_keep, down_send = in_vmem(
+        down_y_body,
+        [((shard, hidden), BF16, "far")] * 2,
+        (place,),
+        far(after(down_own, send), down_near, down_across),
+    )
+    down_came = exchange(down_send, "seq", 1)
     near, ffn_own, across = in_vmem(
         near_body,
         [((2, shard + 32, hidden), BF16, "far")] + [((shard + 32, hidden), BF16, "far")] * 2,
         (place,),
-        far(down_keep, after(down_came, send), out_keep, out_came),
+        far(up_keep, after(up_came, send), out_keep, out_came),
         fence=True,
     )
     near = exchange(near, "seq", 2)
-    (up_across,) = in_vmem(
-        across_body, [((shard, hidden), BF16, "far")], (), far(after(up_across, across), up_near)
-    )
-    up_across = exchange(up_across, "seq", 4)
-    mixed_came = after(mixed_came, long_output, ffn_own)
-    proj_keep, proj_send = in_vmem(
-        proj_term_body,
-        [((4, packed_rows, LANES), BF16, "far"), ((4, packed_rows, LANES), BF16, "far")],
-        (place,),
-        (mixed_came,) + far(normed),
-        scratch=[((3, tokens, local), BF16), ((8, packed_rows, LANES), BF16)],
-    )
-    proj_came = exchange(proj_send, "seq", 1)
-    keep, send, taps_grad = in_vmem(
+    mixed_came = after(mixed_came, long_output, ffn_own, down_send)
+    proj_keep, proj_send, keep, send, taps_grad = in_vmem(
         project_back_body,
         [
+            ((4, packed_rows, LANES), BF16, "far"),
+            ((4, packed_rows, LANES), BF16),
             ((tokens // 2, width), BF16),
             ((tokens // 2, width), BF16),
             (conv_taps.shape, F32),
         ],
         (place,),
-        (after(mixed_came, proj_send, up_across, near),) + far(proj_full),
-        scratch=[((tokens, width), BF16), ((3, tokens, local), BF16)],
+        (mixed_came,) + far(normed, proj_full),
+        scratch=[
+            ((tokens, width), BF16),
+            ((3, tokens, local), BF16),
+            ((8, packed_rows, LANES), BF16),
+        ],
         fence=True,
     )
+    proj_came = exchange(proj_send, "seq", 1)
+    send = after(send, near)
     half = add_low(keep, exchange(send, "head", 1))
     (across,) = in_vmem(
         across_body, [((shard + 32, hidden), BF16, "far")], (), far(after(across, send), near)
     )
     across = exchange(across, "seq", 4)
-    own = add_low(half, exchange(half, "head", 2))
+    own = add_low(half, after(exchange(half, "head", 2), proj_came))
     other = exchange(own, "head", 1)
     proj_blocks = in_vmem(
         scatter_z_body,
@@ -1267,7 +1280,7 @@
             ((1, shard), F32),
         ],
         (),
-        far(after(up_own, proj_blocks[0]), up_near, up_across, ffn_own, near, across, up_weight)
+        far(after(ffn_own, proj_blocks[0]), near, across, down_keep, down_came, up_weight)
         + (feed_gain,),
     )
     proj_blocks[3] = after(proj_blocks[3], up_grad)
@@ -1285,8 +1298,8 @@
         scratch=[((tokens, width), F32)],
     )
     gains = jnp.concatenate([attention_part, feed_part], axis=0)
-    gains = gains + exchange(gains, "head", 1)
-    gains = gains + after(exchange(gains, "head", 2), long_input_grad)
+    across_x = exchange(gains, "head", 2) + exchange(gains, "head", 3)
+    gains = (gains + exchange(gains, "head", 1)) + after(across_x, long_input_grad)
 
     return (
         short_output,

time: 199 us -> 190 us (0.955)
  Pallas kernels: 62.1 us -> 57.8 us
  waiting for transfers between devices: 74.2 us -> 71.2 us
    ppermute x39 -> x40, waiting for transfers between devices: 67.5 us -> 61.3 us  [exchange(): return lax.ppermute(array, axis, [(i, i ^ mask) for i in range(size)])]
    pallas_call x22 -> x20, Pallas kernels: 62.1 us -> 57.8 us  [in_vmem(): pl.pallas_call(body, out_shape=[pltpu.HBM(*out[:2]) if len(out) == 3 else...]
    all_to_all x1, waiting for transfers between devices: 5.14 us -> 8.23 us  [pair_shards(): mixed_came = lax.all_to_all(send, 'seq', 0, 0, tiled=True)]
    ppermute x39 -> x40, starting transfers between devices: 40.7 us -> 41.2 us  [exchange(): return lax.ppermute(array, axis, [(i, i ^ mask) for i in range(size)])]
  transfers between devices with their start and end apart: 43 -> 44, of which waited for: 22 -> 22; matrix products, arithmetic and copies ran while one was open for 1% -> 0% of each run, Pallas kernels for 26% -> 26%
where the time goes in v3:
time: 190 us; the launch traced here: 189 us
  waiting for transfers between devices  71.2 us (37%)
  Pallas kernels  57.8 us (30%)
  starting transfers between devices  55.4 us (29%)
  local copies, waits for them, and re-layouts  3.39 us (2%)
    ppermute x40, waiting for transfers between devices, exchange(): return lax.ppermute(array, axis, [(i, i ^ mask) for i in range(size)])  61.3 us
    pallas_call x20, Pallas kernels, in_vmem(): pl.pallas_call(body, out_shape=[pltpu.HBM(*out[:2]) if len(out) == 3 else...  57.8 us
    ppermute x40, starting transfers between devices, exchange(): return lax.ppermute(array, axis, [(i, i ^ mask) for i in range(size)])  41.2 us
    all_to_all x1, waiting for transfers between devices, pair_shards(): mixed_came = lax.all_to_all(send, 'seq', 0, 0, tiled=True)  8.23 us
  transfers between devices with their start and end apart: 44, of which 22 were waited for; matrix products, arithmetic and copies ran while one was open for 0% of the time, Pallas kernels for 26%

profile of v3, /device:TPU:0, one launch (start us, length us, event | category | flops | bytes accessed | tf_op | source)
XLA Modules:
  0.0 189.4 jit_solution(5390073695077666861)
XLA Ops:
  2.3 5.1 %collective-permute-start.5 = (bf16[448,128]{1,0:T(8,128)(2,1)S(1)}, bf16[448,128]{1,0:T(8,128)(2,1)S(1)}, u32[]{:S(2)}, u32[]{:S(2)}) collective-permute-start(bf16[448,128]{1,0:T(8,128)(2,1)S(1)} %shard_map.212.refs_0_), channel_id=1, source_target_pairs={{0,24},{4,28},{8,16},{12,20},{16,8},{20,12},{24,0},{28,4},{1,25},{... | collective-permute-start | bytes 344072 | tf_op jit(solution)/shard_map/ppermute | solution.py:412
  13.2 3.9 %collective-permute-done.3.refs_4_ = bf16[448,128]{1,0:T(8,128)(2,1)S(1)} collective-permute-done((bf16[448,128]{1,0:T(8,128)(2,1)S(1)}, bf16[448,128]{1,0:T(8,128)(2,1)S(1)}, u32[]{:S(2)}, u32[]{:S(2)}) %collective-permute-start.3) | collective-permute-done | bytes 114720 | tf_op jit(solution)/shard_map/ppermute | solution.py:412
  25.6 3.1 %shard_map.213 = (bf16[8,304,128]{2,1,0:T(8,128)(2,1)}, bf16[384,768]{1,0:T(8,128)(2,1)}, bf16[3,768,192]{2,1,0:T(8,128)(2,1)}, f32[1,768]{1,0:T(1,128)}) custom-call(s32[2]{0:T(128)S(1)} %pad_add_fusion.place, bf16[448,128]{1,0:T(8,128)(2,1)S(1)} %shard_map.212.refs_0_, bf16[448,128]{1,0:T(8,128)(2,1)S(1)} %collective-permute-done.refs_1_, ...), custom_call_target="tpu_custom_call" | custom-call | flops 99999997952 | tf_op jit(solution)/shard_map/pallas_call | solution.py:373
  28.7 3.7 %all-to-all-start = ((bf16[8,304,128]{2,1,0:T(8,128)(2,1)}), bf16[8,304,128]{2,1,0:T(8,128)(2,1)S(1)}, u32[]{:S(2)}, u32[]{:S(2)}) async-start(bf16[8,304,128]{2,1,0:T(8,128)(2,1)} %get-tuple-element.86), calls=%async_computation | async-start | bytes 1245184 | tf_op jit(solution)/shard_map/all_to_all | solution.py:1096
  32.4 6.1 %collective-permute-done.9.refs_4_ = bf16[224,768]{1,0:T(8,128)(2,1)S(1)} collective-permute-done((bf16[224,768]{1,0:T(8,128)(2,1)S(1)}, bf16[224,768]{1,0:T(8,128)(2,1)S(1)}, u32[]{:S(2)}, u32[]{:S(2)}) %collective-permute-start.9) | collective-permute-done | bytes 344096 | tf_op jit(solution)/shard_map/ppermute | solution.py:412
  40.7 14.5 %collective-permute-done.12.refs_6_ = bf16[224,768]{1,0:T(8,128)(2,1)S(1)} collective-permute-done((bf16[224,768]{1,0:T(8,128)(2,1)S(1)}, bf16[224,768]{1,0:T(8,128)(2,1)S(1)}, u32[]{:S(2)}, u32[]{:S(2)}) %collective-permute-start.12) | collective-permute-done | bytes 344096 | tf_op jit(solution)/shard_map/ppermute | solution.py:412
  56.7 4.5 %shard_map.214 = (bf16[8,96,128]{2,1,0:T(8,128)(2,1)}, bf16[1536,64]{1,0:T(8,128)(2,1)}, bf16[1536,128]{1,0:T(8,128)(2,1)}, f32[64,1536]{1,0:T(8,128)}, f32[1,1536]{1,0:T(1,128)}, /*index=5*/bf16[8,304,128]{2,1,0:T(8,128)(2,1)}) custom-call(s32[2]{0:T(128)S(1)} %pad_add_fusion.place, s32[2]{0:T(128)S(1)} %copy-done.5, s32[2]{0:T(128)S(1)} %copy-done.6, ...), custom_call_target="tpu_custom_call" | custom-call | flops 99999997952 | tf_op jit(solution)/shard_map/pallas_call | solution.py:373
  61.3 3.4 %all-to-all-start.1 = ((bf16[8,96,128]{2,1,0:T(8,128)(2,1)}), bf16[8,96,128]{2,1,0:T(8,128)(2,1)S(1)}, u32[]{:S(2)}, u32[]{:S(2)}) async-start(bf16[8,96,128]{2,1,0:T(8,128)(2,1)} %get-tuple-element.87), calls=%async_computation.1 | async-start | bytes 393216 | tf_op jit(solution)/shard_map/all_to_all | solution.py:1117
  64.8 2.9 %collective-permute-done.13.refs_7_ = bf16[224,768]{1,0:T(8,128)(2,1)} collective-permute-done((bf16[224,768]{1,0:T(8,128)(2,1)S(1)}, bf16[224,768]{1,0:T(8,128)(2,1)}, u32[]{:S(2)}, u32[]{:S(2)}) %collective-permute-start.13) | collective-permute-done | bytes 344096 | tf_op jit(solution)/shard_map/ppermute | solution.py:412
  67.7 3.5 %shard_map.216 = (bf16[8,192,768]{2,1,0:T(8,128)(2,1)}, bf16[768,192]{1,0:T(8,128)(2,1)}) custom-call(s32[2]{0:T(128)S(1)} %pad_add_fusion.place, bf16[224,768]{1,0:T(8,128)(2,1)} %copy-done, bf16[224,768]{1,0:T(8,128)(2,1)} %copy-done.11, bf16[224,768]{1,0:T(8,128)(2,1)} %copy-done.10, bf16[224,768]{1,0:T(8,128)(2,1)} %copy-done.14, ...), custom_call_target="tpu_custom_call" | custom-call | tf_op jit(solution)/shard_map/pallas_call | solution.py:373
  77.9 7.6 %collective-permute-done.15 = bf16[192,768]{1,0:T(8,128)(2,1)S(1)} collective-permute-done((bf16[192,768]{1,0:T(8,128)(2,1)S(1)}, bf16[192,768]{1,0:T(8,128)(2,1)S(1)}, u32[]{:S(2)}, u32[]{:S(2)}) %collective-permute-start.15) | collective-permute-done | bytes 294944 | tf_op jit(solution)/shard_map/ppermute | solution.py:412
  87.2 6.2 %shard_map.218 = (f32[384,768]{1,0:T(8,128)}, bf16[384,768]{1,0:T(8,128)(2,1)}, bf16[384,768]{1,0:T(8,128)(2,1)}, bf16[192,768]{1,0:T(8,128)(2,1)S(1)}, bf16[192...) custom-call(s32[2]{0:T(128)S(1)} %pad_add_fusion.place, s32[2]{0:T(128)S(1)} %copy-done.5, ...), custom_call_target="tpu_custom_call" | custom-call | tf_op jit(solution)/shard_map/pallas_call | solution.py:373
  96.6 4.4 %shard_map.219 = (bf16[2,2,96,768]{3,2,1,0:T(8,128)(2,1)}, bf16[2,96,768]{2,1,0:T(8,128)(2,1)}, bf16[2,96,768]{2,1,0:T(8,128)(2,1)}, bf16[192,768]{1,0:T(8,128)(2,1)}, bf16[192,768]{1,0:T(8,128)(2,1)}) custom-call(s32[2]{0:T(128)S(1)} %pad_add_fusion.place, bf16[384,768]{1,0:T(8,128)(2,1)} %get-tuple-element.100.squared, ...), custom_call_target="tpu_custom_call" | custom-call | flops 99999997952 | tf_op jit(solution)/shard_map/pallas_call | solution.py:373
  101.2 3.0 %collective-permute-done.18 = bf16[192,768]{1,0:T(8,128)(2,1)S(1)} collective-permute-done((bf16[192,768]{1,0:T(8,128)(2,1)S(1)}, bf16[192,768]{1,0:T(8,128)(2,1)S(1)}, u32[]{:S(2)}, u32[]{:S(2)}) %collective-permute-start.18) | collective-permute-done | bytes 294944 | tf_op jit(solution)/shard_map/ppermute | solution.py:412
  105.9 3.6 %shard_map.220 = (f32[384,768]{1,0:T(8,128)}, bf16[8,96,128]{2,1,0:T(8,128)(2,1)}, bf16[4,32,768]{2,1,0:T(8,128)(2,1)}, bf16[4,32,768]{2,1,0:T(8,128)(2,1)}) custom-call(s32[2]{0:T(128)S(1)} %pad_add_fusion.place, bf16[192,768]{1,0:T(8,128)(2,1)S(1)} %add_convert_fusion.4.own, bf16[192,768]{1,0:T(8,128)(2,1)S(1)} %collective-permute-done.19.other, ...), custom_call_target="tpu_custom_call" | custom-call | tf_op jit(solution)/shard_map/pallas_call | solution.py:373
  109.5 3.6 %all-to-all-start.2 = ((bf16[8,96,128]{2,1,0:T(8,128)(2,1)}), bf16[8,96,128]{2,1,0:T(8,128)(2,1)S(1)}, u32[]{:S(2)}, u32[]{:S(2)}) async-start(bf16[8,96,128]{2,1,0:T(8,128)(2,1)} %get-tuple-element.107), calls=%async_computation.2 | async-start | bytes 393216 | tf_op jit(solution)/shard_map/all_to_all | solution.py:1195
  121.7 5.9 %shard_map.223 = bf16[8,304,128]{2,1,0:T(8,128)(2,1)} custom-call(s32[2]{0:T(128)S(1)} %pad_add_fusion.place, s32[2]{0:T(128)S(1)} %copy-done.5, s32[2]{0:T(128)S(1)} %copy-done.6, bf16[8,304,128]{2,1,0:T(8,128)(2,1)} %get-tuple-element.111.came, bf16[1536,64]{1,0:T(8,128)(2,1)} %get-tuple-element.112.q_all, bf16[1536,128]{1,0:T(8,128)(2,1)} %get-tuple-element.113.kv_all, ...), custom_call_target="tpu_custom_call" | custom-call | flops 99999997952 | tf_op jit(solution)/shard_map/pallas_call | solution.py:373
  127.6 3.5 %all-to-all-start.3 = ((bf16[8,304,128]{2,1,0:T(8,128)(2,1)}), bf16[8,304,128]{2,1,0:T(8,128)(2,1)S(1)}, u32[]{:S(2)}, u32[]{:S(2)}) async-start(bf16[8,304,128]{2,1,0:T(8,128)(2,1)} %shard_map.223), calls=%async_computation.3 | async-start | bytes 1245184 | tf_op jit(solution)/shard_map/all_to_all | solution.py:1223
  139.9 8.2 %all-to-all-done.3.came = bf16[8,304,128]{2,1,0:T(8,128)(2,1)S(1)} async-done(((bf16[8,304,128]{2,1,0:T(8,128)(2,1)}), bf16[8,304,128]{2,1,0:T(8,128)(2,1)S(1)}, u32[]{:S(2)}, u32[]{:S(2)}) %all-to-all-start.3) | async-done | bytes 622624 | tf_op jit(solution)/shard_map/all_to_all | solution.py:1223
  148.1 4.0 %shard_map.226 = (bf16[4,432,128]{2,1,0:T(8,128)(2,1)}, bf16[4,432,128]{2,1,0:T(8,128)(2,1)S(1)}, bf16[192,768]{1,0:T(8,128)(2,1)S(1)}, bf16[192,768]{1,0:T(8,128)(2,1)S(1)}, f32[9,24]{1,0:T(8,128)}) custom-call(s32[2]{0:T(128)S(1)} %pad_add_fusion.place, bf16[8,304,128]{2,1,0:T(8,128)(2,1)S(1)} %all-to-all-done.3.came, ...), custom_call_target="tpu_custom_call" | custom-call | flops 99999997952 | tf_op jit(solution)/shard_map/pallas_call | solution.py:373
  160.2 5.6 %collective-permute-done.30.refs_1_ = bf16[4,432,128]{2,1,0:T(8,128)(2,1)S(1)} collective-permute-done((bf16[4,432,128]{2,1,0:T(8,128)(2,1)S(1)}, bf16[4,432,128]{2,1,0:T(8,128)(2,1)S(1)}, u32[]{:S(2)}, u32[]{:S(2)}) %collective-permute-start.30) | collective-permute-done | bytes 442400 | tf_op jit(solution)/shard_map/ppermute | solution.py:412
  167.2 3.4 %collective-permute-start.34 = (bf16[432,128]{1,0:T(8,128)(2,1)S(1)}, bf16[432,128]{1,0:T(8,128)(2,1)S(1)}, u32[]{:S(2)}, u32[]{:S(2)}) collective-permute-start(bf16[432,128]{1,0:T(8,128)(2,1)S(1)} %get-tuple-element.143), channel_id=1, source_target_pairs={{0,24},{4,28},{8,16},{12,20},{16,8},{20,12},{24,0},{28,4},{1,25},{... | collective-permute-start | bytes 331784 | tf_op jit(solution)/shard_map/ppermute | solution.py:412
  175.0 4.0 %collective-permute-done.32.b1 = bf16[432,128]{1,0:T(8,128)(2,1)S(1)} collective-permute-done((bf16[432,128]{1,0:T(8,128)(2,1)S(1)}, bf16[432,128]{1,0:T(8,128)(2,1)S(1)}, u32[]{:S(2)}, u32[]{:S(2)}) %collective-permute-start.32) | collective-permute-done | bytes 110624 | tf_op jit(solution)/shard_map/ppermute | solution.py:412
  185.9 3.0 %shard_map.231 = (f32[2,128,768]{2,1,0:T(8,128)}, f32[2,64,768]{2,1,0:T(8,128)}) custom-call(s32[2]{0:T(128)S(1)} %pad_add_fusion.place, bf16[192,768]{1,0:T(8,128)(2,1)S(1)} %add_convert_fusion.own, bf16[192,768]{1,0:T(8,128)(2,1)S(1)} %collective-permute-done.31.other, f32[384,768]{1,0:T(8,128)} %get-tuple-element.151.grad_mid, ...), custom_call_target="tpu_custom_call" | custom-call | tf_op jit(solution)/shard_map/pallas_call | solution.py:373
  (139 shorter events, 71.8 us)
Async XLA Ops:
  7.4 11.2 %collective-permute-start.1 = (bf16[448,128]{1,0:T(8,128)(2,1)S(1)}, bf16[448,128]{1,0:T(8,128)(2,1)S(1)}, u32[]{:S(2)}, u32[]{:S(2)}) collective-permute-start(bf16[448,128]{1,0:T(8,128)(2,1)S(1)} %shard_map.212.refs_0_), channel_id=1, source_target_pairs={{0,8},{4,12},{8,0},{12,4},{16,24},{20,28},{24,16},{28,20},{1,9},{5... | collective-permute-start | bytes 344072 | tf_op jit(solution)/shard_map/ppermute | solution.py:412
  8.1 14.8 %collective-permute-start = (bf16[448,128]{1,0:T(8,128)(2,1)S(1)}, bf16[448,128]{1,0:T(8,128)(2,1)S(1)}, u32[]{:S(2)}, u32[]{:S(2)}) collective-permute-start(bf16[448,128]{1,0:T(8,128)(2,1)S(1)} %shard_map.212.refs_0_), channel_id=1, source_target_pairs={{0,4},{4,0},{8,12},{12,8},{16,20},{20,16},{24,28},{28,24},{1,5},{5... | collective-permute-start | bytes 344072 | tf_op jit(solution)/shard_map/ppermute | solution.py:412
  11.5 12.6 %collective-permute-start.6 = (bf16[448,128]{1,0:T(8,128)(2,1)S(1)}, bf16[448,128]{1,0:T(8,128)(2,1)S(1)}, u32[]{:S(2)}, u32[]{:S(2)}) collective-permute-start(bf16[448,128]{1,0:T(8,128)(2,1)S(1)} %collective-permute-done.5.refs_6_), channel_id=1, source_target_pairs={{0,4},{4,0},{8,12},{12,8},{16,20},{20,16},{24,28},{28,24},{1,5},{5... | collective-permute-start | bytes 344072 | tf_op jit(solution)/shard_map/ppermute | solution.py:412
  21.1 17.4 %collective-permute-start.9 = (bf16[224,768]{1,0:T(8,128)(2,1)S(1)}, bf16[224,768]{1,0:T(8,128)(2,1)S(1)}, u32[]{:S(2)}, u32[]{:S(2)}) collective-permute-start(bf16[224,768]{1,0:T(8,128)(2,1)S(1)} %shard_map.215.refs_0_), channel_id=1, source_target_pairs={{0,16},{4,20},{8,24},{12,28},{16,0},{20,4},{24,8},{28,12},{1,17},{... | collective-permute-start | bytes 1032200 | tf_op jit(solution)/shard_map/ppermute | solution.py:412
  22.9 17.4 %collective-permute-start.8 = (bf16[224,768]{1,0:T(8,128)(2,1)S(1)}, bf16[224,768]{1,0:T(8,128)(2,1)S(1)}, u32[]{:S(2)}, u32[]{:S(2)}) collective-permute-start(bf16[224,768]{1,0:T(8,128)(2,1)S(1)} %shard_map.215.refs_0_), channel_id=1, source_target_pairs={{0,8},{4,12},{8,0},{12,4},{16,24},{20,28},{24,16},{28,20},{1,9},{5... | collective-permute-start | bytes 1032200 | tf_op jit(solution)/shard_map/ppermute | solution.py:412
  24.1 14.4 %collective-permute-start.7 = (bf16[224,768]{1,0:T(8,128)(2,1)S(1)}, bf16[224,768]{1,0:T(8,128)(2,1)S(1)}, u32[]{:S(2)}, u32[]{:S(2)}) collective-permute-start(bf16[224,768]{1,0:T(8,128)(2,1)S(1)} %shard_map.215.refs_0_), channel_id=1, source_target_pairs={{0,4},{4,0},{8,12},{12,8},{16,20},{20,16},{24,28},{28,24},{1,5},{5... | collective-permute-start | bytes 1032200 | tf_op jit(solution)/shard_map/ppermute | solution.py:412
  28.7 28.0 %all-to-all-start = ((bf16[8,304,128]{2,1,0:T(8,128)(2,1)}), bf16[8,304,128]{2,1,0:T(8,128)(2,1)S(1)}, u32[]{:S(2)}, u32[]{:S(2)}) async-start(bf16[8,304,128]{2,1,0:T(8,128)(2,1)} %get-tuple-element.86), calls=%async_computation | async-start | bytes 1245184 | tf_op jit(solution)/shard_map/all_to_all | solution.py:1096
  38.5 16.7 %collective-permute-start.12 = (bf16[224,768]{1,0:T(8,128)(2,1)S(1)}, bf16[224,768]{1,0:T(8,128)(2,1)S(1)}, u32[]{:S(2)}, u32[]{:S(2)}) collective-permute-start(bf16[224,768]{1,0:T(8,128)(2,1)S(1)} %collective-permute-done.9.refs_4_), channel_id=1, source_target_pairs={{0,8},{4,12},{8,0},{12,4},{16,24},{20,28},{24,16},{28,20},{1,9},{5... | collective-permute-start | bytes 1032200 | tf_op jit(solution)/shard_map/ppermute | solution.py:412
  38.6 26.2 %collective-permute-start.11 = (bf16[224,768]{1,0:T(8,128)(2,1)S(1)}, bf16[224,768]{1,0:T(8,128)(2,1)S(1)}, u32[]{:S(2)}, u32[]{:S(2)}) collective-permute-start(bf16[224,768]{1,0:T(8,128)(2,1)S(1)} %collective-permute-done.9.refs_4_), channel_id=1, source_target_pairs={{0,4},{4,0},{8,12},{12,8},{16,20},{20,16},{24,28},{28,24},{1,5},{5... | collective-permute-start | bytes 1032200 | tf_op jit(solution)/shard_map/ppermute | solution.py:412
  40.2 24.5 %collective-permute-start.10 = (bf16[224,768]{1,0:T(8,128)(2,1)S(1)}, bf16[224,768]{1,0:T(8,128)(2,1)S(1)}, u32[]{:S(2)}, u32[]{:S(2)}) collective-permute-start(bf16[224,768]{1,0:T(8,128)(2,1)S(1)} %collective-permute-done.8.refs_2_), channel_id=1, source_target_pairs={{0,4},{4,0},{8,12},{12,8},{16,20},{20,16},{24,28},{28,24},{1,5},{5... | collective-permute-start | bytes 1032200 | tf_op jit(solution)/shard_map/ppermute | solution.py:412
  55.2 12.4 %collective-permute-start.13 = (bf16[224,768]{1,0:T(8,128)(2,1)S(1)}, bf16[224,768]{1,0:T(8,128)(2,1)}, u32[]{:S(2)}, u32[]{:S(2)}) collective-permute-start(bf16[224,768]{1,0:T(8,128)(2,1)S(1)} %collective-permute-done.12.refs_6_), channel_id=1, source_target_pairs={{0,4},{4,0},{8,12},{12,8},{16,20},{20,16},{24,28},{28,24},{1,5},{5... | collective-permute-start | bytes 1032200 | tf_op jit(solution)/shard_map/ppermute | solution.py:412
  61.3 11.4 %all-to-all-start.1 = ((bf16[8,96,128]{2,1,0:T(8,128)(2,1)}), bf16[8,96,128]{2,1,0:T(8,128)(2,1)S(1)}, u32[]{:S(2)}, u32[]{:S(2)}) async-start(bf16[8,96,128]{2,1,0:T(8,128)(2,1)} %get-tuple-element.87), calls=%async_computation.1 | async-start | bytes 393216 | tf_op jit(solution)/shard_map/all_to_all | solution.py:1117
  93.6 21.3 %collective-permute-start.23 = (bf16[4,96,768]{2,1,0:T(8,128)(2,1)}, bf16[4,96,768]{2,1,0:T(8,128)(2,1)S(1)}, u32[]{:S(2)}, u32[]{:S(2)}) collective-permute-start(bf16[4,96,768]{2,1,0:T(8,128)(2,1)} %get-tuple-element.117), channel_id=1, source_target_pairs={{0,4},{4,0},{8,12},{12,8},{16,20},{20,16},{24,28},{28,24},{1,5},{5... | collective-permute-start | bytes 1769480 | tf_op jit(solution)/shard_map/ppermute | solution.py:412
  101.0 15.8 %collective-permute-start.24 = (bf16[2,2,96,768]{3,2,1,0:T(8,128)(2,1)}, bf16[2,2,96,768]{3,2,1,0:T(8,128)(2,1)S(1)}, u32[]{:S(2)}, u32[]{:S(2)}) collective-permute-start(bf16[2,2,96,768]{3,2,1,0:T(8,128)(2,1)} %get-tuple-element.119), channel_id=1, source_target_pairs={{0,8},{4,12},{8,0},{12,4},{16,24},{20,28},{24,16},{28,20},{1,9},{5... | collective-permute-start | bytes 1769480 | tf_op jit(solution)/shard_map/ppermute | solution.py:412
  109.5 12.2 %all-to-all-start.2 = ((bf16[8,96,128]{2,1,0:T(8,128)(2,1)}), bf16[8,96,128]{2,1,0:T(8,128)(2,1)S(1)}, u32[]{:S(2)}, u32[]{:S(2)}) async-start(bf16[8,96,128]{2,1,0:T(8,128)(2,1)} %get-tuple-element.107), calls=%async_computation.2 | async-start | bytes 393216 | tf_op jit(solution)/shard_map/all_to_all | solution.py:1195
  113.1 18.2 %collective-permute-start.25 = (bf16[4,32,768]{2,1,0:T(8,128)(2,1)}, bf16[4,32,768]{2,1,0:T(8,128)(2,1)}, u32[]{:S(2)}, u32[]{:S(2)}) collective-permute-start(bf16[4,32,768]{2,1,0:T(8,128)(2,1)} %get-tuple-element.124), channel_id=1, source_target_pairs={{0,4},{4,0},{8,12},{12,8},{16,20},{20,16},{24,28},{28,24},{1,5},{5... | collective-permute-start | bytes 589832 | tf_op jit(solution)/shard_map/ppermute | solution.py:412
  119.6 16.0 %collective-permute-start.26 = (bf16[2,96,768]{2,1,0:T(8,128)(2,1)}, bf16[2,96,768]{2,1,0:T(8,128)(2,1)}, u32[]{:S(2)}, u32[]{:S(2)}) collective-permute-start(bf16[2,96,768]{2,1,0:T(8,128)(2,1)} %shard_map.222), channel_id=1, source_target_pairs={{0,16},{4,20},{8,24},{12,28},{16,0},{20,4},{24,8},{28,12},{1,17},{... | collective-permute-start | bytes 884744 | tf_op jit(solution)/shard_map/ppermute | solution.py:412
  127.6 20.5 %all-to-all-start.3 = ((bf16[8,304,128]{2,1,0:T(8,128)(2,1)}), bf16[8,304,128]{2,1,0:T(8,128)(2,1)S(1)}, u32[]{:S(2)}, u32[]{:S(2)}) async-start(bf16[8,304,128]{2,1,0:T(8,128)(2,1)} %shard_map.223), calls=%async_computation.3 | async-start | bytes 1245184 | tf_op jit(solution)/shard_map/all_to_all | solution.py:1223
  133.7 19.2 %collective-permute-start.27 = (bf16[2,128,768]{2,1,0:T(8,128)(2,1)}, bf16[2,128,768]{2,1,0:T(8,128)(2,1)S(1)}, u32[]{:S(2)}, u32[]{:S(2)}) collective-permute-start(bf16[2,128,768]{2,1,0:T(8,128)(2,1)} %get-tuple-element.134), channel_id=1, source_target_pairs={{0,8},{4,12},{8,0},{12,4},{16,24},{20,28},{24,16},{28,20},{1,9},{5... | collective-permute-start | bytes 1179656 | tf_op jit(solution)/shard_map/ppermute | solution.py:412
  152.9 13.0 %collective-permute-start.30 = (bf16[4,432,128]{2,1,0:T(8,128)(2,1)S(1)}, bf16[4,432,128]{2,1,0:T(8,128)(2,1)S(1)}, u32[]{:S(2)}, u32[]{:S(2)}) collective-permute-start(bf16[4,432,128]{2,1,0:T(8,128)(2,1)S(1)} %get-tuple-element.136), channel_id=1, source_target_pairs={{0,4},{4,0},{8,12},{12,8},{16,20},{20,16},{24,28},{28,24},{1,5},{5... | collective-permute-start | bytes 1327112 | tf_op jit(solution)/shard_map/ppermute | solution.py:412
  154.6 11.3 %collective-permute-start.29 = (bf16[192,768]{1,0:T(8,128)(2,1)S(1)}, bf16[192,768]{1,0:T(8,128)(2,1)S(1)}, u32[]{:S(2)}, u32[]{:S(2)}) collective-permute-start(bf16[192,768]{1,0:T(8,128)(2,1)S(1)} %add_convert_fusion.1), channel_id=1, source_target_pairs={{0,2},{1,3},{2,0},{3,1},{4,6},{5,7},{6,4},{7,5},{8,10},{9,11},{10,... | collective-permute-start | bytes 884744 | tf_op jit(solution)/shard_map/ppermute | solution.py:412
  156.1 14.4 %collective-permute-start.36 = (bf16[96,768]{1,0:T(8,128)(2,1)S(1)}, bf16[96,768]{1,0:T(8,128)(2,1)S(1)}, u32[]{:S(2)}, u32[]{:S(2)}) collective-permute-start(bf16[96,768]{1,0:T(8,128)(2,1)S(1)} %copy-done.20), channel_id=1, source_target_pairs={{0,4},{4,0},{8,12},{12,8},{16,20},{20,16},{24,28},{28,24},{1,5},{5... | collective-permute-start | bytes 442376 | tf_op jit(solution)/shard_map/ppermute | solution.py:412
  158.5 13.2 %collective-permute-start.35 = (bf16[128,768]{1,0:T(8,128)(2,1)}, bf16[128,768]{1,0:T(8,128)(2,1)S(1)}, u32[]{:S(2)}, u32[]{:S(2)}) collective-permute-start(bf16[128,768]{1,0:T(8,128)(2,1)} %shard_map.228), channel_id=1, source_target_pairs={{0,16},{4,20},{8,24},{12,28},{16,0},{20,4},{24,8},{28,12},{1,17},{... | collective-permute-start | bytes 589832 | tf_op jit(solution)/shard_map/ppermute | solution.py:412
  166.0 19.9 %collective-permute-start.31 = (bf16[192,768]{1,0:T(8,128)(2,1)S(1)}, bf16[192,768]{1,0:T(8,128)(2,1)S(1)}, u32[]{:S(2)}, u32[]{:S(2)}) collective-permute-start(bf16[192,768]{1,0:T(8,128)(2,1)S(1)} %add_convert_fusion.own), channel_id=1, source_target_pairs={{0,1},{1,0},{2,3},{3,2},{4,5},{5,4},{6,7},{7,6},{8,9},{9,8},{10,11... | collective-permute-start | bytes 884744 | tf_op jit(solution)/shard_map/ppermute | solution.py:412
  (41 other events, 327.7 us)

commit v4 on v3

--- a/solution.py
+++ b/solution.py
@@ -477,16 +477,19 @@
 
 
 def place_ffn_body(place, *refs):
-    whole, out = refs[8:]
+    up, down, out, out_now = refs[8:]
     rows = out.shape[0] // 8
     for i in range(8):
         owner = jnp.bitwise_xor(place[0], i)
         part = refs[i]
-        whole[owner] = part[: 2 * rows, :]
+        first = pl.ds(pl.multiple_of(owner * rows, rows), rows)
+        up[first, :] = part[:rows, :]
+        down[first, :] = part[rows : 2 * rows, :]
         for g in range(rows // 16):
             at = pl.ds(pl.multiple_of(owner * rows + 16 * g, 16), 16)
             out[at, :LANES] = part[2 * rows : 2 * rows + 16, LANES * g : LANES * g + LANES]
             out[at, LANES:] = part[2 * rows + 16 :, LANES * g : LANES * g + HEAD_DIM]
+    out_now[...] = out[...]
 
 
 def project_body(place, *refs):
@@ -638,7 +641,8 @@
     short_in,
     long_cot,
     short_cot,
-    gathered,
+    up,
+    down,
     mid_ref,
     squared_ref,
     grad_out_ref,
@@ -648,17 +652,12 @@
     up_send,
     scratch,
     attended,
-    up,
-    down,
     blocks,
     normed_ref,
     grad_up_ref,
 ):
     seqs = long_in.shape[0]
-    shard = gathered.shape[1] // 2
-    for s in range(8):
-        up[s * shard : (s + 1) * shard, :] = gathered[s, :shard, :]
-        down[s * shard : (s + 1) * shard, :] = gathered[s, shard:, :]
+    shard = up.shape[0] // 8
     rows = long_rows + short_in.shape[1]
     join_halves(place, attended, own, other)
     for b in range(seqs):
@@ -711,11 +710,9 @@
 
 
 def down_term_body(
-    place, squared, grad_out, gathered, near, own, across, f_keep, f_send, scratch, down, blocks
+    place, squared, grad_out, down, near, own, across, f_keep, f_send, scratch, blocks
 ):
-    rows = gathered.shape[1] // 2
-    for s in range(8):
-        down[s * rows : (s + 1) * rows, :] = gathered[s, rows:, :]
+    rows = blocks.shape[1]
     term = dot(grad_out[...], squared[...], TN).astype(BF16)
     for s in range(8):
         blocks[s] = term[s * rows : (s + 1) * rows]
@@ -1064,18 +1061,19 @@
         pack_proj_body,
         [((packed_rows + 16, LANES), BF16)],
         (),
-        far(proj_weight) + (attention_gain,),
+        far(proj_weight, attention_gain),
     )
     (ffn_packed,) = in_vmem(
         pack_ffn_body,
         [((2 * shard + 32, hidden), BF16)],
         (),
-        far(up_weight, down_t, out_weight) + (feed_gain,),
+        far(up_weight, down_t, out_weight, feed_gain),
     )
     proj_z = [proj_packed] + [exchange(proj_packed, "seq", mask) for mask in (2, 4, 6)]
-    proj_parts = [proj_packed, exchange(proj_packed, "seq", 1)]
-    for piece in proj_z[1:]:
-        proj_parts += [piece, exchange(piece, "seq", 1)]
+    proj_parts = [proj_packed, exchange(after(proj_packed, ffn_packed), "seq", 1)]
+    proj_parts += [proj_z[1], exchange(proj_z[1], "seq", 1)]
+    proj_parts += [proj_z[2], exchange(proj_z[2], "seq", 1)]
+    proj_parts += [proj_z[3], exchange(proj_z[3], "seq", 1)]
     ffn_0 = after(ffn_packed, *proj_z)
     ffn_1 = exchange(ffn_0, "seq", 1)
     ffn_2 = exchange(ffn_0, "seq", 2)
@@ -1095,11 +1093,11 @@
     )
     came = lax.all_to_all(send, "seq", 0, 0, tiled=True)
     across_z = marker(ffn_4, ffn_1, send)
-    ffn_2, ffn_4 = after(ffn_2, across_z), after(ffn_4, across_z)
+    ffn_2 = after(ffn_2, across_z)
+    ffn_4 = after(ffn_4, across_z)
     ffn_6 = exchange(ffn_4, "seq", 2)
     ffn_3 = exchange(ffn_2, "seq", 1)
     ffn_5 = exchange(ffn_4, "seq", 1)
-    ffn_7 = exchange(ffn_6, "seq", 1)
     att_send, q_all, kv_all, att_t, log_row, mixed = in_vmem(
         functools.partial(attend_body, long_rows, seqs),
         [
@@ -1115,9 +1113,11 @@
         fence=True,
     )
     att_0 = lax.all_to_all(att_send, "seq", 0, 0, tiled=True)
-    ffn_full, out_full = in_vmem(
+    ffn_7 = exchange(ffn_6, "seq", 1)
+    up_full, down_full, out_full, out_now = in_vmem(
         place_ffn_body,
-        [((8, 2 * shard, hidden), BF16, "far"), ((width, local), BF16, "far")],
+        [((width, hidden), BF16, "far")] * 2
+        + [((width, local), BF16, "far"), ((width, local), BF16)],
         (place,),
         far(after(ffn_packed, att_send), ffn_1, ffn_2, ffn_3, ffn_4, ffn_5, ffn_6, ffn_7),
     )
@@ -1130,8 +1130,9 @@
             ((tokens // 2, width), BF16),
         ],
         (place,),
-        (att_0,) + far(out_full),
+        (att_0, out_now),
         scratch=[((tokens, width), BF16)],
+        fence=True,
     )
     half = add_low(keep, exchange(send, "head", 1))
     own = add_low(half, exchange(half, "head", 2))
@@ -1149,12 +1150,10 @@
         ],
         (place, long_lengths, short_lengths),
         (own, other)
-        + far(long_input, short_input, long_cotangent, short_cotangent, ffn_full),
+        + far(long_input, short_input, long_cotangent, short_cotangent, up_full, down_full),
         scratch=[
             ((tokens, width), BF16),
             ((tokens, width), F32),
-            ((width, hidden), BF16),
-            ((width, hidden), BF16),
             ((8, shard, hidden), BF16),
             ((tokens, width), BF16),
             ((tokens, hidden), BF16),
@@ -1169,10 +1168,9 @@
         + [((2, shard, hidden), BF16, "far")] * 2
         + [((tokens // 2, width), BF16, "far")] * 2,
         (place,),
-        far(after(squared, half), grad_out, ffn_full),
+        far(after(squared, half), grad_out, down_full),
         scratch=[
             ((tokens, width), BF16),
-            ((width, hidden), BF16),
             ((8, shard, hidden), BF16),
         ],
         fence=True,
@@ -1221,13 +1219,6 @@
         fence=True,
     )
     mixed_came = lax.all_to_all(send, "seq", 0, 0, tiled=True)
-    down_keep, down_send = in_vmem(
-        down_y_body,
-        [((shard, hidden), BF16, "far")] * 2,
-        (place,),
-        far(after(down_own, send), down_near, down_across),
-    )
-    down_came = exchange(down_send, "seq", 1)
     near, ffn_own, across = in_vmem(
         near_body,
         [((2, shard + 32, hidden), BF16, "far")] + [((shard + 32, hidden), BF16, "far")] * 2,
@@ -1236,7 +1227,14 @@
         fence=True,
     )
     near = exchange(near, "seq", 2)
-    mixed_came = after(mixed_came, long_output, ffn_own, down_send)
+    down_keep, down_send = in_vmem(
+        down_y_body,
+        [((shard, hidden), BF16, "far")] * 2,
+        (place,),
+        far(after(down_own, ffn_own), down_near, down_across),
+    )
+    down_came = exchange(down_send, "seq", 1)
+    mixed_came = after(mixed_came, long_output, down_send)
     proj_keep, proj_send, keep, send, taps_grad = in_vmem(
         project_back_body,
         [
@@ -1256,7 +1254,6 @@
         fence=True,
     )
     proj_came = exchange(proj_send, "seq", 1)
-    send = after(send, near)
     half = add_low(keep, exchange(send, "head", 1))
     (across,) = in_vmem(
         across_body, [((shard + 32, hidden), BF16, "far")], (), far(after(across, send), near)
@@ -1269,6 +1266,7 @@
         [((packed_rows, LANES), BF16)] * 4,
         (place,),
         far(proj_keep) + (proj_came,),
+        fence=True,
     )
     proj_blocks = [proj_blocks[0]] + [exchange(proj_blocks[i], "seq", 2 * i) for i in (1, 2, 3)]
     up_grad, down_grad, out_grad, feed_part = in_vmem(
@@ -1298,8 +1296,8 @@
         scratch=[((tokens, width), F32)],
     )
     gains = jnp.concatenate([attention_part, feed_part], axis=0)
-    across_x = exchange(gains, "head", 2) + exchange(gains, "head", 3)
-    gains = (gains + exchange(gains, "head", 1)) + after(across_x, long_input_grad)
+    gains = gains + exchange(gains, "head", 1)
+    gains = gains + after(exchange(gains, "head", 2), long_input_grad)
 
     return (
         short_output,

time: 190 us -> 184 us (0.968)
  waiting for transfers between devices: 71.2 us -> 64.9 us
    ppermute x40 -> x39, waiting for transfers between devices: 61.3 us -> 55.3 us  [exchange(): return lax.ppermute(array, axis, [(i, i ^ mask) for i in range(size)])]
    ppermute x40 -> x39, starting transfers between devices: 41.2 us -> 41.1 us  [exchange(): return lax.ppermute(array, axis, [(i, i ^ mask) for i in range(size)])]
  transfers between devices with their start and end apart: 44 -> 43, of which waited for: 22 -> 20; matrix products, arithmetic and copies ran while one was open for 0% -> 0% of each run, Pallas kernels for 26% -> 26%
where the time goes in v4:
time: 184 us; the launch traced here: 183 us
  waiting for transfers between devices  64.9 us (35%)
  starting transfers between devices  57 us (31%)
  Pallas kernels  56.7 us (31%)
  local copies, waits for them, and re-layouts  2.83 us (2%)
    pallas_call x20, Pallas kernels, in_vmem(): pl.pallas_call(body, out_shape=[pltpu.HBM(*out[:2]) if len(out) == 3 else...  56.7 us
    ppermute x39, waiting for transfers between devices, exchange(): return lax.ppermute(array, axis, [(i, i ^ mask) for i in range(size)])  55.3 us
    ppermute x39, starting transfers between devices, exchange(): return lax.ppermute(array, axis, [(i, i ^ mask) for i in range(size)])  41.1 us
    all_to_all x1, waiting for transfers between devices, pair_shards(): mixed_came = lax.all_to_all(send, 'seq', 0, 0, tiled=True)  8.22 us
    all_to_all x1, starting transfers between devices, pair_shards(): came = lax.all_to_all(send, 'seq', 0, 0, tiled=True)  5.45 us
  transfers between devices with their start and end apart: 43, of which 20 were waited for; matrix products, arithmetic and copies ran while one was open for 0% of the time, Pallas kernels for 26%

profile of v4, /device:TPU:0, one launch (start us, length us, event | category | flops | bytes accessed | tf_op | source)
XLA Modules:
  0.0 183.2 jit_solution(350259910339964283)
XLA Ops:
  1.7 5.1 %collective-permute-start.5 = (bf16[448,128]{1,0:T(8,128)(2,1)S(1)}, bf16[448,128]{1,0:T(8,128)(2,1)S(1)}, u32[]{:S(2)}, u32[]{:S(2)}) collective-permute-start(bf16[448,128]{1,0:T(8,128)(2,1)S(1)} %shard_map.212.refs_0_), channel_id=1, source_target_pairs={{0,24},{4,28},{8,16},{12,20},{16,8},{20,12},{24,0},{28,4},{1,25},{... | collective-permute-start | bytes 344072 | tf_op jit(solution)/shard_map/ppermute | solution.py:412
  12.6 3.9 %collective-permute-done.3.refs_4_ = bf16[448,128]{1,0:T(8,128)(2,1)S(1)} collective-permute-done((bf16[448,128]{1,0:T(8,128)(2,1)S(1)}, bf16[448,128]{1,0:T(8,128)(2,1)S(1)}, u32[]{:S(2)}, u32[]{:S(2)}) %collective-permute-start.3) | collective-permute-done | bytes 114720 | tf_op jit(solution)/shard_map/ppermute | solution.py:412
  24.1 3.0 %shard_map.214 = (bf16[8,304,128]{2,1,0:T(8,128)(2,1)}, bf16[384,768]{1,0:T(8,128)(2,1)}, bf16[3,768,192]{2,1,0:T(8,128)(2,1)}, f32[1,768]{1,0:T(1,128)}) custom-call(s32[2]{0:T(128)S(1)} %pad_add_fusion.place, bf16[448,128]{1,0:T(8,128)(2,1)S(1)} %shard_map.212.refs_0_, bf16[448,128]{1,0:T(8,128)(2,1)S(1)} %collective-permute-done.refs_1_, ...), custom_call_target="tpu_custom_call" | custom-call | flops 99999997952 | tf_op jit(solution)/shard_map/pallas_call | solution.py:373
  27.2 5.4 %all-to-all-start = ((bf16[8,304,128]{2,1,0:T(8,128)(2,1)}), bf16[8,304,128]{2,1,0:T(8,128)(2,1)S(1)}, u32[]{:S(2)}, u32[]{:S(2)}) async-start(bf16[8,304,128]{2,1,0:T(8,128)(2,1)} %get-tuple-element.89), calls=%async_computation | async-start | bytes 1245184 | tf_op jit(solution)/shard_map/all_to_all | solution.py:1094
  32.6 2.8 %collective-permute-done.9.refs_4_ = bf16[224,768]{1,0:T(8,128)(2,1)S(1)} collective-permute-done((bf16[224,768]{1,0:T(8,128)(2,1)S(1)}, bf16[224,768]{1,0:T(8,128)(2,1)S(1)}, u32[]{:S(2)}, u32[]{:S(2)}) %collective-permute-start.9) | collective-permute-done | bytes 344096 | tf_op jit(solution)/shard_map/ppermute | solution.py:412
  37.8 14.9 %collective-permute-done.12.refs_6_ = bf16[224,768]{1,0:T(8,128)(2,1)S(1)} collective-permute-done((bf16[224,768]{1,0:T(8,128)(2,1)S(1)}, bf16[224,768]{1,0:T(8,128)(2,1)S(1)}, u32[]{:S(2)}, u32[]{:S(2)}) %collective-permute-start.12) | collective-permute-done | bytes 344096 | tf_op jit(solution)/shard_map/ppermute | solution.py:412
  54.2 4.5 %shard_map.215 = (bf16[8,96,128]{2,1,0:T(8,128)(2,1)}, bf16[1536,64]{1,0:T(8,128)(2,1)}, bf16[1536,128]{1,0:T(8,128)(2,1)}, f32[64,1536]{1,0:T(8,128)}, f32[1,1536]{1,0:T(1,128)}, /*index=5*/bf16[8,304,128]{2,1,0:T(8,128)(2,1)}) custom-call(s32[2]{0:T(128)S(1)} %pad_add_fusion.place, s32[2]{0:T(128)S(1)} %copy-done.3, s32[2]{0:T(128)S(1)} %copy-done.4, ...), custom_call_target="tpu_custom_call" | custom-call | flops 99999997952 | tf_op jit(solution)/shard_map/pallas_call | solution.py:373
  58.8 3.4 %all-to-all-start.1 = ((bf16[8,96,128]{2,1,0:T(8,128)(2,1)}), bf16[8,96,128]{2,1,0:T(8,128)(2,1)S(1)}, u32[]{:S(2)}, u32[]{:S(2)}) async-start(bf16[8,96,128]{2,1,0:T(8,128)(2,1)} %get-tuple-element.90), calls=%async_computation.1 | async-start | bytes 393216 | tf_op jit(solution)/shard_map/all_to_all | solution.py:1115
  62.2 2.8 %collective-permute-done.13.refs_7_ = bf16[224,768]{1,0:T(8,128)(2,1)} collective-permute-done((bf16[224,768]{1,0:T(8,128)(2,1)S(1)}, bf16[224,768]{1,0:T(8,128)(2,1)}, u32[]{:S(2)}, u32[]{:S(2)}) %collective-permute-start.13) | collective-permute-done | bytes 344096 | tf_op jit(solution)/shard_map/ppermute | solution.py:412
  65.1 3.4 %shard_map.216 = (bf16[768,768]{1,0:T(8,128)(2,1)}, bf16[768,768]{1,0:T(8,128)(2,1)}, bf16[768,192]{1,0:T(8,128)(2,1)}, bf16[768,192]{1,0:T(8,128)(2,1)S(1)}) custom-call(s32[2]{0:T(128)S(1)} %pad_add_fusion.place, bf16[224,768]{1,0:T(8,128)(2,1)} %copy-done, bf16[224,768]{1,0:T(8,128)(2,1)} %copy-done.9, bf16[224,768]{1,0:T(8,128)(2,1)} %copy-done.8, ...), custom_call_target="tpu_custom_call" | custom-call | tf_op jit(solution)/shard_map/pallas_call | solution.py:373
  74.6 7.6 %collective-permute-done.15 = bf16[192,768]{1,0:T(8,128)(2,1)S(1)} collective-permute-done((bf16[192,768]{1,0:T(8,128)(2,1)S(1)}, bf16[192,768]{1,0:T(8,128)(2,1)S(1)}, u32[]{:S(2)}, u32[]{:S(2)}) %collective-permute-start.15) | collective-permute-done | bytes 294944 | tf_op jit(solution)/shard_map/ppermute | solution.py:412
  83.9 6.1 %shard_map.218 = (f32[384,768]{1,0:T(8,128)}, bf16[384,768]{1,0:T(8,128)(2,1)}, bf16[384,768]{1,0:T(8,128)(2,1)}, bf16[192,768]{1,0:T(8,128)(2,1)S(1)}, bf16[192...) custom-call(s32[2]{0:T(128)S(1)} %pad_add_fusion.place, s32[2]{0:T(128)S(1)} %copy-done.3, ...), custom_call_target="tpu_custom_call" | custom-call | tf_op jit(solution)/shard_map/pallas_call | solution.py:373
  93.2 4.0 %shard_map.219 = (bf16[2,2,96,768]{3,2,1,0:T(8,128)(2,1)}, bf16[2,96,768]{2,1,0:T(8,128)(2,1)}, bf16[2,96,768]{2,1,0:T(8,128)(2,1)}, bf16[192,768]{1,0:T(8,128)(2,1)}, bf16[192,768]{1,0:T(8,128)(2,1)}) custom-call(s32[2]{0:T(128)S(1)} %pad_add_fusion.place, bf16[384,768]{1,0:T(8,128)(2,1)} %get-tuple-element.105.squared, ...), custom_call_target="tpu_custom_call" | custom-call | flops 99999997952 | tf_op jit(solution)/shard_map/pallas_call | solution.py:373
  97.4 3.4 %collective-permute-done.18 = bf16[192,768]{1,0:T(8,128)(2,1)S(1)} collective-permute-done((bf16[192,768]{1,0:T(8,128)(2,1)S(1)}, bf16[192,768]{1,0:T(8,128)(2,1)S(1)}, u32[]{:S(2)}, u32[]{:S(2)}) %collective-permute-start.18) | collective-permute-done | bytes 294944 | tf_op jit(solution)/shard_map/ppermute | solution.py:412
  102.5 3.5 %shard_map.220 = (f32[384,768]{1,0:T(8,128)}, bf16[8,96,128]{2,1,0:T(8,128)(2,1)}, bf16[4,32,768]{2,1,0:T(8,128)(2,1)}, bf16[4,32,768]{2,1,0:T(8,128)(2,1)}) custom-call(s32[2]{0:T(128)S(1)} %pad_add_fusion.place, bf16[192,768]{1,0:T(8,128)(2,1)S(1)} %add_convert_fusion.4.own, bf16[192,768]{1,0:T(8,128)(2,1)S(1)} %collective-permute-done.19.other, ...), custom_call_target="tpu_custom_call" | custom-call | tf_op jit(solution)/shard_map/pallas_call | solution.py:373
  106.1 3.6 %all-to-all-start.2 = ((bf16[8,96,128]{2,1,0:T(8,128)(2,1)}), bf16[8,96,128]{2,1,0:T(8,128)(2,1)S(1)}, u32[]{:S(2)}, u32[]{:S(2)}) async-start(bf16[8,96,128]{2,1,0:T(8,128)(2,1)} %get-tuple-element.112), calls=%async_computation.2 | async-start | bytes 393216 | tf_op jit(solution)/shard_map/all_to_all | solution.py:1193
  118.2 5.9 %shard_map.223 = bf16[8,304,128]{2,1,0:T(8,128)(2,1)} custom-call(s32[2]{0:T(128)S(1)} %pad_add_fusion.place, s32[2]{0:T(128)S(1)} %copy-done.3, s32[2]{0:T(128)S(1)} %copy-done.4, bf16[8,304,128]{2,1,0:T(8,128)(2,1)} %get-tuple-element.116.came, bf16[1536,64]{1,0:T(8,128)(2,1)} %get-tuple-element.117.q_all, bf16[1536,128]{1,0:T(8,128)(2,1)} %get-tuple-element.118.kv_all, ...), custom_call_target="tpu_custom_call" | custom-call | flops 99999997952 | tf_op jit(solution)/shard_map/pallas_call | solution.py:373
  124.2 3.5 %all-to-all-start.3 = ((bf16[8,304,128]{2,1,0:T(8,128)(2,1)}), bf16[8,304,128]{2,1,0:T(8,128)(2,1)S(1)}, u32[]{:S(2)}, u32[]{:S(2)}) async-start(bf16[8,304,128]{2,1,0:T(8,128)(2,1)} %shard_map.223), calls=%async_computation.3 | async-start | bytes 1245184 | tf_op jit(solution)/shard_map/all_to_all | solution.py:1221
  127.9 2.3 %shard_map.224 = (bf16[2,128,768]{2,1,0:T(8,128)(2,1)}, bf16[128,768]{1,0:T(8,128)(2,1)}, bf16[128,768]{1,0:T(8,128)(2,1)}) custom-call(s32[2]{0:T(128)S(1)} %pad_add_fusion.place, bf16[4,96,768]{2,1,0:T(8,128)(2,1)} %get-tuple-element.127.refs_0_, bf16[4,96,768]{2,1,0:T(8,128)(2,1)} %copy-done.16, bf16[4,32,768]{2,1,0:T(8,128)(2,1)} %get-tuple-element.129.refs_2_, ...), custom_call_target="tpu_custom_call" | custom-call | flops 99999997952 | tf_op jit(solution)/shard_map/pallas_call | solution.py:373
  136.5 8.2 %all-to-all-done.3.came = bf16[8,304,128]{2,1,0:T(8,128)(2,1)S(1)} async-done(((bf16[8,304,128]{2,1,0:T(8,128)(2,1)}), bf16[8,304,128]{2,1,0:T(8,128)(2,1)S(1)}, u32[]{:S(2)}, u32[]{:S(2)}) %all-to-all-start.3) | async-done | bytes 622624 | tf_op jit(solution)/shard_map/all_to_all | solution.py:1221
  144.7 4.0 %shard_map.226 = (bf16[4,432,128]{2,1,0:T(8,128)(2,1)}, bf16[4,432,128]{2,1,0:T(8,128)(2,1)S(1)}, bf16[192,768]{1,0:T(8,128)(2,1)S(1)}, bf16[192,768]{1,0:T(8,128)(2,1)S(1)}, f32[9,24]{1,0:T(8,128)}) custom-call(s32[2]{0:T(128)S(1)} %pad_add_fusion.place, bf16[8,304,128]{2,1,0:T(8,128)(2,1)S(1)} %all-to-all-done.3.came, ...), custom_call_target="tpu_custom_call" | custom-call | flops 99999997952 | tf_op jit(solution)/shard_map/pallas_call | solution.py:373
  155.4 6.2 %collective-permute-done.29.refs_1_ = bf16[4,432,128]{2,1,0:T(8,128)(2,1)S(1)} collective-permute-done((bf16[4,432,128]{2,1,0:T(8,128)(2,1)S(1)}, bf16[4,432,128]{2,1,0:T(8,128)(2,1)S(1)}, u32[]{:S(2)}, u32[]{:S(2)}) %collective-permute-start.29) | collective-permute-done | bytes 442400 | tf_op jit(solution)/shard_map/ppermute | solution.py:412
  162.8 3.2 %collective-permute-start.33 = (bf16[432,128]{1,0:T(8,128)(2,1)S(1)}, bf16[432,128]{1,0:T(8,128)(2,1)S(1)}, u32[]{:S(2)}, u32[]{:S(2)}) collective-permute-start(bf16[432,128]{1,0:T(8,128)(2,1)S(1)} %get-tuple-element.146), channel_id=1, source_target_pairs={{0,24},{4,28},{8,16},{12,20},{16,8},{20,12},{24,0},{28,4},{1,25},{... | collective-permute-start | bytes 331784 | tf_op jit(solution)/shard_map/ppermute | solution.py:412
  179.7 3.0 %shard_map.231 = (f32[2,128,768]{2,1,0:T(8,128)}, f32[2,64,768]{2,1,0:T(8,128)}) custom-call(s32[2]{0:T(128)S(1)} %pad_add_fusion.place, bf16[192,768]{1,0:T(8,128)(2,1)S(1)} %add_convert_fusion.own, bf16[192,768]{1,0:T(8,128)(2,1)S(1)} %collective-permute-done.30.other, f32[384,768]{1,0:T(8,128)} %get-tuple-element.155.grad_mid, ...), custom_call_target="tpu_custom_call" | custom-call | tf_op jit(solution)/shard_map/pallas_call | solution.py:373
  (133 shorter events, 68.4 us)
Async XLA Ops:
  6.8 11.2 %collective-permute-start.1 = (bf16[448,128]{1,0:T(8,128)(2,1)S(1)}, bf16[448,128]{1,0:T(8,128)(2,1)S(1)}, u32[]{:S(2)}, u32[]{:S(2)}) collective-permute-start(bf16[448,128]{1,0:T(8,128)(2,1)S(1)} %shard_map.212.refs_0_), channel_id=1, source_target_pairs={{0,8},{4,12},{8,0},{12,4},{16,24},{20,28},{24,16},{28,20},{1,9},{5... | collective-permute-start | bytes 344072 | tf_op jit(solution)/shard_map/ppermute | solution.py:412
  8.6 11.7 %collective-permute-start = (bf16[448,128]{1,0:T(8,128)(2,1)S(1)}, bf16[448,128]{1,0:T(8,128)(2,1)S(1)}, u32[]{:S(2)}, u32[]{:S(2)}) collective-permute-start(bf16[448,128]{1,0:T(8,128)(2,1)S(1)} %shard_map.212.refs_0_), channel_id=1, source_target_pairs={{0,4},{4,0},{8,12},{12,8},{16,20},{20,16},{24,28},{28,24},{1,5},{5... | collective-permute-start | bytes 344072 | tf_op jit(solution)/shard_map/ppermute | solution.py:412
  10.8 10.7 %collective-permute-start.6 = (bf16[448,128]{1,0:T(8,128)(2,1)S(1)}, bf16[448,128]{1,0:T(8,128)(2,1)S(1)}, u32[]{:S(2)}, u32[]{:S(2)}) collective-permute-start(bf16[448,128]{1,0:T(8,128)(2,1)S(1)} %collective-permute-done.5.refs_6_), channel_id=1, source_target_pairs={{0,4},{4,0},{8,12},{12,8},{16,20},{20,16},{24,28},{28,24},{1,5},{5... | collective-permute-start | bytes 344072 | tf_op jit(solution)/shard_map/ppermute | solution.py:412
  18.6 16.8 %collective-permute-start.9 = (bf16[224,768]{1,0:T(8,128)(2,1)S(1)}, bf16[224,768]{1,0:T(8,128)(2,1)S(1)}, u32[]{:S(2)}, u32[]{:S(2)}) collective-permute-start(bf16[224,768]{1,0:T(8,128)(2,1)S(1)} %shard_map.213.refs_0_), channel_id=1, source_target_pairs={{0,16},{4,20},{8,24},{12,28},{16,0},{20,4},{24,8},{28,12},{1,17},{... | collective-permute-start | bytes 1032200 | tf_op jit(solution)/shard_map/ppermute | solution.py:412
  20.3 17.4 %collective-permute-start.8 = (bf16[224,768]{1,0:T(8,128)(2,1)S(1)}, bf16[224,768]{1,0:T(8,128)(2,1)S(1)}, u32[]{:S(2)}, u32[]{:S(2)}) collective-permute-start(bf16[224,768]{1,0:T(8,128)(2,1)S(1)} %shard_map.213.refs_0_), channel_id=1, source_target_pairs={{0,8},{4,12},{8,0},{12,4},{16,24},{20,28},{24,16},{28,20},{1,9},{5... | collective-permute-start | bytes 1032200 | tf_op jit(solution)/shard_map/ppermute | solution.py:412
  21.6 13.8 %collective-permute-start.7 = (bf16[224,768]{1,0:T(8,128)(2,1)S(1)}, bf16[224,768]{1,0:T(8,128)(2,1)S(1)}, u32[]{:S(2)}, u32[]{:S(2)}) collective-permute-start(bf16[224,768]{1,0:T(8,128)(2,1)S(1)} %shard_map.213.refs_0_), channel_id=1, source_target_pairs={{0,4},{4,0},{8,12},{12,8},{16,20},{20,16},{24,28},{28,24},{1,5},{5... | collective-permute-start | bytes 1032200 | tf_op jit(solution)/shard_map/ppermute | solution.py:412
  27.2 27.0 %all-to-all-start = ((bf16[8,304,128]{2,1,0:T(8,128)(2,1)}), bf16[8,304,128]{2,1,0:T(8,128)(2,1)S(1)}, u32[]{:S(2)}, u32[]{:S(2)}) async-start(bf16[8,304,128]{2,1,0:T(8,128)(2,1)} %get-tuple-element.89), calls=%async_computation | async-start | bytes 1245184 | tf_op jit(solution)/shard_map/all_to_all | solution.py:1094
  35.4 17.3 %collective-permute-start.12 = (bf16[224,768]{1,0:T(8,128)(2,1)S(1)}, bf16[224,768]{1,0:T(8,128)(2,1)S(1)}, u32[]{:S(2)}, u32[]{:S(2)}) collective-permute-start(bf16[224,768]{1,0:T(8,128)(2,1)S(1)} %collective-permute-done.9.refs_4_), channel_id=1, source_target_pairs={{0,8},{4,12},{8,0},{12,4},{16,24},{20,28},{24,16},{28,20},{1,9},{5... | collective-permute-start | bytes 1032200 | tf_op jit(solution)/shard_map/ppermute | solution.py:412
  35.5 26.8 %collective-permute-start.11 = (bf16[224,768]{1,0:T(8,128)(2,1)S(1)}, bf16[224,768]{1,0:T(8,128)(2,1)S(1)}, u32[]{:S(2)}, u32[]{:S(2)}) collective-permute-start(bf16[224,768]{1,0:T(8,128)(2,1)S(1)} %collective-permute-done.9.refs_4_), channel_id=1, source_target_pairs={{0,4},{4,0},{8,12},{12,8},{16,20},{20,16},{24,28},{28,24},{1,5},{5... | collective-permute-start | bytes 1032200 | tf_op jit(solution)/shard_map/ppermute | solution.py:412
  37.7 24.5 %collective-permute-start.10 = (bf16[224,768]{1,0:T(8,128)(2,1)S(1)}, bf16[224,768]{1,0:T(8,128)(2,1)S(1)}, u32[]{:S(2)}, u32[]{:S(2)}) collective-permute-start(bf16[224,768]{1,0:T(8,128)(2,1)S(1)} %collective-permute-done.8.refs_2_), channel_id=1, source_target_pairs={{0,4},{4,0},{8,12},{12,8},{16,20},{20,16},{24,28},{28,24},{1,5},{5... | collective-permute-start | bytes 1032200 | tf_op jit(solution)/shard_map/ppermute | solution.py:412
  52.7 12.4 %collective-permute-start.13 = (bf16[224,768]{1,0:T(8,128)(2,1)S(1)}, bf16[224,768]{1,0:T(8,128)(2,1)}, u32[]{:S(2)}, u32[]{:S(2)}) collective-permute-start(bf16[224,768]{1,0:T(8,128)(2,1)S(1)} %collective-permute-done.12.refs_6_), channel_id=1, source_target_pairs={{0,4},{4,0},{8,12},{12,8},{16,20},{20,16},{24,28},{28,24},{1,5},{5... | collective-permute-start | bytes 1032200 | tf_op jit(solution)/shard_map/ppermute | solution.py:412
  58.8 11.1 %all-to-all-start.1 = ((bf16[8,96,128]{2,1,0:T(8,128)(2,1)}), bf16[8,96,128]{2,1,0:T(8,128)(2,1)S(1)}, u32[]{:S(2)}, u32[]{:S(2)}) async-start(bf16[8,96,128]{2,1,0:T(8,128)(2,1)} %get-tuple-element.90), calls=%async_computation.1 | async-start | bytes 393216 | tf_op jit(solution)/shard_map/all_to_all | solution.py:1115
  90.2 21.2 %collective-permute-start.23 = (bf16[4,96,768]{2,1,0:T(8,128)(2,1)}, bf16[4,96,768]{2,1,0:T(8,128)(2,1)S(1)}, u32[]{:S(2)}, u32[]{:S(2)}) collective-permute-start(bf16[4,96,768]{2,1,0:T(8,128)(2,1)} %get-tuple-element.122), channel_id=1, source_target_pairs={{0,4},{4,0},{8,12},{12,8},{16,20},{20,16},{24,28},{28,24},{1,5},{5... | collective-permute-start | bytes 1769480 | tf_op jit(solution)/shard_map/ppermute | solution.py:412
  97.2 15.5 %collective-permute-start.24 = (bf16[2,2,96,768]{3,2,1,0:T(8,128)(2,1)}, bf16[2,2,96,768]{3,2,1,0:T(8,128)(2,1)S(1)}, u32[]{:S(2)}, u32[]{:S(2)}) collective-permute-start(bf16[2,2,96,768]{3,2,1,0:T(8,128)(2,1)} %get-tuple-element.124), channel_id=1, source_target_pairs={{0,8},{4,12},{8,0},{12,4},{16,24},{20,28},{24,16},{28,20},{1,9},{5... | collective-permute-start | bytes 1769480 | tf_op jit(solution)/shard_map/ppermute | solution.py:412
  106.1 12.2 %all-to-all-start.2 = ((bf16[8,96,128]{2,1,0:T(8,128)(2,1)}), bf16[8,96,128]{2,1,0:T(8,128)(2,1)S(1)}, u32[]{:S(2)}, u32[]{:S(2)}) async-start(bf16[8,96,128]{2,1,0:T(8,128)(2,1)} %get-tuple-element.112), calls=%async_computation.2 | async-start | bytes 393216 | tf_op jit(solution)/shard_map/all_to_all | solution.py:1193
  109.6 18.2 %collective-permute-start.25 = (bf16[4,32,768]{2,1,0:T(8,128)(2,1)}, bf16[4,32,768]{2,1,0:T(8,128)(2,1)}, u32[]{:S(2)}, u32[]{:S(2)}) collective-permute-start(bf16[4,32,768]{2,1,0:T(8,128)(2,1)} %get-tuple-element.130), channel_id=1, source_target_pairs={{0,4},{4,0},{8,12},{12,8},{16,20},{20,16},{24,28},{28,24},{1,5},{5... | collective-permute-start | bytes 589832 | tf_op jit(solution)/shard_map/ppermute | solution.py:412
  115.5 16.7 %collective-permute-start.26 = (bf16[2,96,768]{2,1,0:T(8,128)(2,1)}, bf16[2,96,768]{2,1,0:T(8,128)(2,1)}, u32[]{:S(2)}, u32[]{:S(2)}) collective-permute-start(bf16[2,96,768]{2,1,0:T(8,128)(2,1)} %shard_map.222), channel_id=1, source_target_pairs={{0,16},{4,20},{8,24},{12,28},{16,0},{20,4},{24,8},{28,12},{1,17},{... | collective-permute-start | bytes 884744 | tf_op jit(solution)/shard_map/ppermute | solution.py:412
  116.7 11.0 %collective-permute-start.21 = (bf16[192,768]{1,0:T(8,128)(2,1)S(1)}, bf16[192,768]{1,0:T(8,128)(2,1)S(1)}, u32[]{:S(2)}, u32[]{:S(2)}) collective-permute-start(bf16[192,768]{1,0:T(8,128)(2,1)S(1)} %add_convert_fusion.3), channel_id=1, source_target_pairs={{0,2},{1,3},{2,0},{3,1},{4,6},{5,7},{6,4},{7,5},{8,10},{9,11},{10,... | collective-permute-start | bytes 884744 | tf_op jit(solution)/shard_map/ppermute | solution.py:412
  124.2 20.5 %all-to-all-start.3 = ((bf16[8,304,128]{2,1,0:T(8,128)(2,1)}), bf16[8,304,128]{2,1,0:T(8,128)(2,1)S(1)}, u32[]{:S(2)}, u32[]{:S(2)}) async-start(bf16[8,304,128]{2,1,0:T(8,128)(2,1)} %shard_map.223), calls=%async_computation.3 | async-start | bytes 1245184 | tf_op jit(solution)/shard_map/all_to_all | solution.py:1221
  130.2 20.5 %collective-permute-start.34 = (bf16[2,128,768]{2,1,0:T(8,128)(2,1)}, bf16[2,128,768]{2,1,0:T(8,128)(2,1)S(1)}, u32[]{:S(2)}, u32[]{:S(2)}) collective-permute-start(bf16[2,128,768]{2,1,0:T(8,128)(2,1)} %get-tuple-element.148), channel_id=1, source_target_pairs={{0,8},{4,12},{8,0},{12,4},{16,24},{20,28},{24,16},{28,20},{1,9},{5... | collective-permute-start | bytes 1179656 | tf_op jit(solution)/shard_map/ppermute | solution.py:412
  148.7 13.0 %collective-permute-start.29 = (bf16[4,432,128]{2,1,0:T(8,128)(2,1)S(1)}, bf16[4,432,128]{2,1,0:T(8,128)(2,1)S(1)}, u32[]{:S(2)}, u32[]{:S(2)}) collective-permute-start(bf16[4,432,128]{2,1,0:T(8,128)(2,1)S(1)} %get-tuple-element.139), channel_id=1, source_target_pairs={{0,4},{4,0},{8,12},{12,8},{16,20},{20,16},{24,28},{28,24},{1,5},{5... | collective-permute-start | bytes 1327112 | tf_op jit(solution)/shard_map/ppermute | solution.py:412
  150.1 15.9 %collective-permute-start.36 = (bf16[96,768]{1,0:T(8,128)(2,1)S(1)}, bf16[96,768]{1,0:T(8,128)(2,1)S(1)}, u32[]{:S(2)}, u32[]{:S(2)}) collective-permute-start(bf16[96,768]{1,0:T(8,128)(2,1)S(1)} %copy-done.18), channel_id=1, source_target_pairs={{0,4},{4,0},{8,12},{12,8},{16,20},{20,16},{24,28},{28,24},{1,5},{5... | collective-permute-start | bytes 442376 | tf_op jit(solution)/shard_map/ppermute | solution.py:412
  153.3 14.0 %collective-permute-start.35 = (bf16[128,768]{1,0:T(8,128)(2,1)}, bf16[128,768]{1,0:T(8,128)(2,1)S(1)}, u32[]{:S(2)}, u32[]{:S(2)}) collective-permute-start(bf16[128,768]{1,0:T(8,128)(2,1)} %shard_map.228), channel_id=1, source_target_pairs={{0,16},{4,20},{8,24},{12,28},{16,0},{20,4},{24,8},{28,12},{1,17},{... | collective-permute-start | bytes 589832 | tf_op jit(solution)/shard_map/ppermute | solution.py:412
  153.9 22.7 %collective-permute-start.28 = (bf16[192,768]{1,0:T(8,128)(2,1)S(1)}, bf16[192,768]{1,0:T(8,128)(2,1)S(1)}, u32[]{:S(2)}, u32[]{:S(2)}) collective-permute-start(bf16[192,768]{1,0:T(8,128)(2,1)S(1)} %add_convert_fusion.1), channel_id=1, source_target_pairs={{0,2},{1,3},{2,0},{3,1},{4,6},{5,7},{6,4},{7,5},{8,10},{9,11},{10,... | collective-permute-start | bytes 884744 | tf_op jit(solution)/shard_map/ppermute | solution.py:412
  (38 other events, 303.2 us)

commit v5 on v4

--- a/solution.py
+++ b/solution.py
@@ -648,16 +648,12 @@
     grad_out_ref,
     keep,
     send,
-    up_keep,
-    up_send,
+    normed_ref,
+    grad_up_ref,
     scratch,
     attended,
-    blocks,
-    normed_ref,
-    grad_up_ref,
 ):
     seqs = long_in.shape[0]
-    shard = up.shape[0] // 8
     rows = long_rows + short_in.shape[1]
     join_halves(place, attended, own, other)
     for b in range(seqs):
@@ -682,10 +678,6 @@
     grad_up_ref[...] = (grad_squared * 2.0 * relu).astype(BF16)
     scratch[...] = dot(grad_up_ref[...], up[...], NT).astype(BF16)
     split_halves(place, scratch, keep, send)
-    term = dot(normed_ref[...], grad_up_ref[...], TN).astype(BF16)
-    for s in range(8):
-        blocks[s] = term[s * shard : (s + 1) * shard]
-    split_y(place, blocks, up_keep, up_send)
 
 
 def split_halves(place, whole, keep, send):
@@ -710,9 +702,27 @@
 
 
 def down_term_body(
-    place, squared, grad_out, down, near, own, across, f_keep, f_send, scratch, blocks
+    place,
+    squared,
+    grad_out,
+    down,
+    normed,
+    grad_up,
+    near,
+    own,
+    across,
+    f_keep,
+    f_send,
+    up_keep,
+    up_send,
+    scratch,
+    blocks,
 ):
     rows = blocks.shape[1]
+    term = dot(normed[...], grad_up[...], TN).astype(BF16)
+    for s in range(8):
+        blocks[s] = term[s * rows : (s + 1) * rows]
+    split_y(place, blocks, up_keep, up_send)
     term = dot(grad_out[...], squared[...], TN).astype(BF16)
     for s in range(8):
         blocks[s] = term[s * rows : (s + 1) * rows]
@@ -842,16 +852,12 @@
             (grad_q, q_mixed, taps_q, terms_q),
             (grad_kv, kv_mixed, taps_kv, terms_kv),
         ):
+            grad_mixed = 0.0
             for m in range(3):
-                back = mixed if m == 0 else shift_back(mixed, m)
-                terms[m] = terms[m] + jnp.sum(grad_conv * back, axis=0, keepdims=True)
-            pair.append(
-                (
-                    taps[0] * grad_conv
-                    + taps[1] * shift_ahead(grad_conv, 1)
-                    + taps[2] * shift_ahead(grad_conv, 2)
-                ).astype(BF16)
-            )
+                ahead = grad_conv if m == 0 else shift_ahead(grad_conv, m)
+                terms[m] = terms[m] + jnp.sum(ahead * mixed, axis=0, keepdims=True)
+                grad_mixed = grad_mixed + taps[m] * ahead
+            pair.append(grad_mixed.astype(BF16))
         results.append(pair)
         first += count
     table = jnp.concatenate(
@@ -1137,7 +1143,7 @@
     half = add_low(keep, exchange(send, "head", 1))
     own = add_low(half, exchange(half, "head", 2))
     other = exchange(own, "head", 1)
-    mid, squared, grad_out, keep, send, up_keep, up_send = in_vmem(
+    mid, squared, grad_out, keep, send, normed_ffn, grad_up = in_vmem(
         functools.partial(feed_body, long_rows),
         [
             ((tokens, width), F32, "far"),
@@ -1145,8 +1151,8 @@
             ((tokens, width), BF16, "far"),
             ((tokens // 2, width), BF16),
             ((tokens // 2, width), BF16),
-            ((4, shard, hidden), BF16, "far"),
-            ((4, shard, hidden), BF16, "far"),
+            ((tokens, width), BF16, "far"),
+            ((tokens, hidden), BF16, "far"),
         ],
         (place, long_lengths, short_lengths),
         (own, other)
@@ -1154,28 +1160,27 @@
         scratch=[
             ((tokens, width), BF16),
             ((tokens, width), F32),
-            ((8, shard, hidden), BF16),
-            ((tokens, width), BF16),
-            ((tokens, hidden), BF16),
         ],
         limit_mib=32,
     )
     half = add_low(keep, exchange(send, "head", 1))
-    up_came = exchange(up_send, "seq", 1)
-    down_near, down_own, down_across, f_keep, f_send = in_vmem(
+    down_near, down_own, down_across, f_keep, f_send, up_keep, up_send = in_vmem(
         down_term_body,
         [((2, 2, shard, hidden), BF16, "far")]
         + [((2, shard, hidden), BF16, "far")] * 2
-        + [((tokens // 2, width), BF16, "far")] * 2,
+        + [((tokens // 2, width), BF16, "far")] * 2
+        + [((4, shard, hidden), BF16, "far")] * 2,
         (place,),
-        far(after(squared, half), grad_out, down_full),
+        far(after(squared, half), grad_out, down_full, normed_ffn, grad_up),
         scratch=[
             ((tokens, width), BF16),
             ((8, shard, hidden), BF16),
         ],
+        limit_mib=32,
         fence=True,
     )
     down_near = exchange(down_near, "seq", 2)
+    up_came = exchange(up_send, "seq", 1)
     own = add_low(half, after(exchange(half, "head", 2), f_send))
     other = exchange(own, "head", 1)
     grad_mid, send, out_keep, out_send = in_vmem(
@@ -1256,7 +1261,7 @@
     proj_came = exchange(proj_send, "seq", 1)
     half = add_low(keep, exchange(send, "head", 1))
     (across,) = in_vmem(
-        across_body, [((shard + 32, hidden), BF16, "far")], (), far(after(across, send), near)
+        across_body, [((shard + 32, hidden), BF16, "far")], (), far(across, near)
     )
     across = exchange(across, "seq", 4)
     own = add_low(half, after(exchange(half, "head", 2), proj_came))

time: 184 us -> 183 us (level)
  starting transfers between devices: 57 us -> 54.2 us
  waiting for transfers between devices: 64.9 us -> 66.9 us
    ppermute x39, waiting for transfers between devices: 55.3 us -> 58.8 us  [exchange(): return lax.ppermute(array, axis, [(i, i ^ mask) for i in range(size)])]
    ppermute x39, starting transfers between devices: 41.1 us -> 37.6 us  [exchange(): return lax.ppermute(array, axis, [(i, i ^ mask) for i in range(size)])]
  transfers between devices with their start and end apart: 43 -> 43, of which waited for: 20 -> 21; matrix products, arithmetic and copies ran while one was open for 0% -> 0% of each run, Pallas kernels for 26% -> 27%
where the time goes in v5:
time: 183 us; the launch traced here: 182 us
  waiting for transfers between devices  66.9 us (37%)
  Pallas kernels  56.5 us (31%)
  starting transfers between devices  54.2 us (30%)
  local copies, waits for them, and re-layouts  2.82 us (2%)
    ppermute x39, waiting for transfers between devices, exchange(): return lax.ppermute(array, axis, [(i, i ^ mask) for i in range(size)])  58.8 us
    pallas_call x20, Pallas kernels, in_vmem(): pl.pallas_call(body, out_shape=[pltpu.HBM(*out[:2]) if len(out) == 3 else...  56.5 us
    ppermute x39, starting transfers between devices, exchange(): return lax.ppermute(array, axis, [(i, i ^ mask) for i in range(size)])  37.6 us
    all_to_all x1, waiting for transfers between devices, pair_shards(): mixed_came = lax.all_to_all(send, 'seq', 0, 0, tiled=True)  6.65 us
    all_to_all x1, starting transfers between devices, pair_shards(): came = lax.all_to_all(send, 'seq', 0, 0, tiled=True)  5.45 us
    all_to_all x1, starting transfers between devices, pair_shards(): mixed_came = lax.all_to_all(send, 'seq', 0, 0, tiled=True)  4.19 us
  transfers between devices with their start and end apart: 43, of which 21 were waited for; matrix products, arithmetic and copies ran while one was open for 0% of the time, Pallas kernels for 27%

profile of v5, /device:TPU:0, one launch (start us, length us, event | category | flops | bytes accessed | tf_op | source)
XLA Modules:
  0.0 182.0 jit_solution(2161165027328712056)
XLA Ops:
  1.7 5.1 %collective-permute-start.5 = (bf16[448,128]{1,0:T(8,128)(2,1)S(1)}, bf16[448,128]{1,0:T(8,128)(2,1)S(1)}, u32[]{:S(2)}, u32[]{:S(2)}) collective-permute-start(bf16[448,128]{1,0:T(8,128)(2,1)S(1)} %shard_map.212.refs_0_), channel_id=1, source_target_pairs={{0,24},{4,28},{8,16},{12,20},{16,8},{20,12},{24,0},{28,4},{1,25},{... | collective-permute-start | bytes 344072 | tf_op jit(solution)/shard_map/ppermute | solution.py:412
  12.6 3.9 %collective-permute-done.3.refs_4_ = bf16[448,128]{1,0:T(8,128)(2,1)S(1)} collective-permute-done((bf16[448,128]{1,0:T(8,128)(2,1)S(1)}, bf16[448,128]{1,0:T(8,128)(2,1)S(1)}, u32[]{:S(2)}, u32[]{:S(2)}) %collective-permute-start.3) | collective-permute-done | bytes 114720 | tf_op jit(solution)/shard_map/ppermute | solution.py:412
  24.1 3.0 %shard_map.214 = (bf16[8,304,128]{2,1,0:T(8,128)(2,1)}, bf16[384,768]{1,0:T(8,128)(2,1)}, bf16[3,768,192]{2,1,0:T(8,128)(2,1)}, f32[1,768]{1,0:T(1,128)}) custom-call(s32[2]{0:T(128)S(1)} %pad_add_fusion.place, bf16[448,128]{1,0:T(8,128)(2,1)S(1)} %shard_map.212.refs_0_, bf16[448,128]{1,0:T(8,128)(2,1)S(1)} %collective-permute-done.refs_1_, ...), custom_call_target="tpu_custom_call" | custom-call | flops 99999997952 | tf_op jit(solution)/shard_map/pallas_call | solution.py:373
  27.2 5.4 %all-to-all-start = ((bf16[8,304,128]{2,1,0:T(8,128)(2,1)}), bf16[8,304,128]{2,1,0:T(8,128)(2,1)S(1)}, u32[]{:S(2)}, u32[]{:S(2)}) async-start(bf16[8,304,128]{2,1,0:T(8,128)(2,1)} %get-tuple-element.90), calls=%async_computation | async-start | bytes 1245184 | tf_op jit(solution)/shard_map/all_to_all | solution.py:1100
  32.6 2.8 %collective-permute-done.9.refs_4_ = bf16[224,768]{1,0:T(8,128)(2,1)S(1)} collective-permute-done((bf16[224,768]{1,0:T(8,128)(2,1)S(1)}, bf16[224,768]{1,0:T(8,128)(2,1)S(1)}, u32[]{:S(2)}, u32[]{:S(2)}) %collective-permute-start.9) | collective-permute-done | bytes 344096 | tf_op jit(solution)/shard_map/ppermute | solution.py:412
  37.8 14.9 %collective-permute-done.12.refs_6_ = bf16[224,768]{1,0:T(8,128)(2,1)S(1)} collective-permute-done((bf16[224,768]{1,0:T(8,128)(2,1)S(1)}, bf16[224,768]{1,0:T(8,128)(2,1)S(1)}, u32[]{:S(2)}, u32[]{:S(2)}) %collective-permute-start.12) | collective-permute-done | bytes 344096 | tf_op jit(solution)/shard_map/ppermute | solution.py:412
  54.2 4.5 %shard_map.215 = (bf16[8,96,128]{2,1,0:T(8,128)(2,1)}, bf16[1536,64]{1,0:T(8,128)(2,1)}, bf16[1536,128]{1,0:T(8,128)(2,1)}, f32[64,1536]{1,0:T(8,128)}, f32[1,1536]{1,0:T(1,128)}, /*index=5*/bf16[8,304,128]{2,1,0:T(8,128)(2,1)}) custom-call(s32[2]{0:T(128)S(1)} %pad_add_fusion.place, s32[2]{0:T(128)S(1)} %copy-done.3, s32[2]{0:T(128)S(1)} %copy-done.4, ...), custom_call_target="tpu_custom_call" | custom-call | flops 99999997952 | tf_op jit(solution)/shard_map/pallas_call | solution.py:373
  58.8 3.4 %all-to-all-start.1 = ((bf16[8,96,128]{2,1,0:T(8,128)(2,1)}), bf16[8,96,128]{2,1,0:T(8,128)(2,1)S(1)}, u32[]{:S(2)}, u32[]{:S(2)}) async-start(bf16[8,96,128]{2,1,0:T(8,128)(2,1)} %get-tuple-element.91), calls=%async_computation.1 | async-start | bytes 393216 | tf_op jit(solution)/shard_map/all_to_all | solution.py:1121
  62.2 2.8 %collective-permute-done.13.refs_7_ = bf16[224,768]{1,0:T(8,128)(2,1)} collective-permute-done((bf16[224,768]{1,0:T(8,128)(2,1)S(1)}, bf16[224,768]{1,0:T(8,128)(2,1)}, u32[]{:S(2)}, u32[]{:S(2)}) %collective-permute-start.13) | collective-permute-done | bytes 344096 | tf_op jit(solution)/shard_map/ppermute | solution.py:412
  65.1 3.3 %shard_map.216 = (bf16[768,768]{1,0:T(8,128)(2,1)}, bf16[768,768]{1,0:T(8,128)(2,1)}, bf16[768,192]{1,0:T(8,128)(2,1)}, bf16[768,192]{1,0:T(8,128)(2,1)S(1)}) custom-call(s32[2]{0:T(128)S(1)} %pad_add_fusion.place, bf16[224,768]{1,0:T(8,128)(2,1)} %copy-done, bf16[224,768]{1,0:T(8,128)(2,1)} %copy-done.9, bf16[224,768]{1,0:T(8,128)(2,1)} %copy-done.8, ...), custom_call_target="tpu_custom_call" | custom-call | tf_op jit(solution)/shard_map/pallas_call | solution.py:373
  74.6 7.6 %collective-permute-done.15 = bf16[192,768]{1,0:T(8,128)(2,1)S(1)} collective-permute-done((bf16[192,768]{1,0:T(8,128)(2,1)S(1)}, bf16[192,768]{1,0:T(8,128)(2,1)S(1)}, u32[]{:S(2)}, u32[]{:S(2)}) %collective-permute-start.15) | collective-permute-done | bytes 294944 | tf_op jit(solution)/shard_map/ppermute | solution.py:412
  83.9 4.6 %shard_map.218 = (f32[384,768]{1,0:T(8,128)}, bf16[384,768]{1,0:T(8,128)(2,1)}, bf16[384,768]{1,0:T(8,128)(2,1)}, bf16[192,768]{1,0:T(8,128)(2,1)S(1)}, bf16[192...) custom-call(s32[2]{0:T(128)S(1)} %pad_add_fusion.place, s32[2]{0:T(128)S(1)} %copy-done.3, ...), custom_call_target="tpu_custom_call" | custom-call | tf_op jit(solution)/shard_map/pallas_call | solution.py:373
  91.7 5.4 %shard_map.219 = (bf16[2,2,96,768]{3,2,1,0:T(8,128)(2,1)}, bf16[2,96,768]{2,1,0:T(8,128)(2,1)}, bf16[2,96,768]{2,1,0:T(8,128)(2,1)}, bf16[192,768]{1,0:T(8,128)(...) custom-call(s32[2]{0:T(128)S(1)} %pad_add_fusion.place, ...), custom_call_target="tpu_custom_call" | custom-call | flops 99999997952 | tf_op jit(solution)/shard_map/pallas_call | solution.py:373
  101.0 3.5 %shard_map.220 = (f32[384,768]{1,0:T(8,128)}, bf16[8,96,128]{2,1,0:T(8,128)(2,1)}, bf16[4,32,768]{2,1,0:T(8,128)(2,1)}, bf16[4,32,768]{2,1,0:T(8,128)(2,1)}) custom-call(s32[2]{0:T(128)S(1)} %pad_add_fusion.place, bf16[192,768]{1,0:T(8,128)(2,1)S(1)} %add_convert_fusion.4.own, bf16[192,768]{1,0:T(8,128)(2,1)S(1)} %collective-permute-done.19.other, ...), custom_call_target="tpu_custom_call" | custom-call | tf_op jit(solution)/shard_map/pallas_call | solution.py:373
  104.5 3.6 %all-to-all-start.2 = ((bf16[8,96,128]{2,1,0:T(8,128)(2,1)}), bf16[8,96,128]{2,1,0:T(8,128)(2,1)S(1)}, u32[]{:S(2)}, u32[]{:S(2)}) async-start(bf16[8,96,128]{2,1,0:T(8,128)(2,1)} %get-tuple-element.115), calls=%async_computation.2 | async-start | bytes 393216 | tf_op jit(solution)/shard_map/all_to_all | solution.py:1198
  109.9 4.3 %collective-permute-done.23.refs_1_ = bf16[4,96,768]{2,1,0:T(8,128)(2,1)S(1)} collective-permute-done((bf16[4,96,768]{2,1,0:T(8,128)(2,1)}, bf16[4,96,768]{2,1,0:T(8,128)(2,1)S(1)}, u32[]{:S(2)}, u32[]{:S(2)}) %collective-permute-start.23) | collective-permute-done | bytes 589856 | tf_op jit(solution)/shard_map/ppermute | solution.py:412
  118.5 5.8 %shard_map.223 = bf16[8,304,128]{2,1,0:T(8,128)(2,1)} custom-call(s32[2]{0:T(128)S(1)} %pad_add_fusion.place, s32[2]{0:T(128)S(1)} %copy-done.3, s32[2]{0:T(128)S(1)} %copy-done.4, bf16[8,304,128]{2,1,0:T(8,128)(2,1)} %get-tuple-element.119.came, bf16[1536,64]{1,0:T(8,128)(2,1)} %get-tuple-element.120.q_all, bf16[1536,128]{1,0:T(8,128)(2,1)} %get-tuple-element.121.kv_all, ...), custom_call_target="tpu_custom_call" | custom-call | flops 99999997952 | tf_op jit(solution)/shard_map/pallas_call | solution.py:373
  124.3 4.2 %all-to-all-start.3 = ((bf16[8,304,128]{2,1,0:T(8,128)(2,1)}), bf16[8,304,128]{2,1,0:T(8,128)(2,1)S(1)}, u32[]{:S(2)}, u32[]{:S(2)}) async-start(bf16[8,304,128]{2,1,0:T(8,128)(2,1)} %shard_map.223), calls=%async_computation.3 | async-start | bytes 1245184 | tf_op jit(solution)/shard_map/all_to_all | solution.py:1226
  128.7 2.3 %shard_map.224 = (bf16[2,128,768]{2,1,0:T(8,128)(2,1)}, bf16[128,768]{1,0:T(8,128)(2,1)}, bf16[128,768]{1,0:T(8,128)(2,1)}) custom-call(s32[2]{0:T(128)S(1)} %pad_add_fusion.place, bf16[4,96,768]{2,1,0:T(8,128)(2,1)} %get-tuple-element.130.refs_0_, bf16[4,96,768]{2,1,0:T(8,128)(2,1)} %copy-done.16, bf16[4,32,768]{2,1,0:T(8,128)(2,1)} %get-tuple-element.132.refs_2_, ...), custom_call_target="tpu_custom_call" | custom-call | flops 99999997952 | tf_op jit(solution)/shard_map/pallas_call | solution.py:373
  137.3 6.7 %all-to-all-done.3.came = bf16[8,304,128]{2,1,0:T(8,128)(2,1)S(1)} async-done(((bf16[8,304,128]{2,1,0:T(8,128)(2,1)}), bf16[8,304,128]{2,1,0:T(8,128)(2,1)S(1)}, u32[]{:S(2)}, u32[]{:S(2)}) %all-to-all-start.3) | async-done | bytes 622624 | tf_op jit(solution)/shard_map/all_to_all | solution.py:1226
  144.0 4.0 %shard_map.226 = (bf16[4,432,128]{2,1,0:T(8,128)(2,1)}, bf16[4,432,128]{2,1,0:T(8,128)(2,1)S(1)}, bf16[192,768]{1,0:T(8,128)(2,1)S(1)}, bf16[192,768]{1,0:T(8,128)(2,1)S(1)}, f32[9,24]{1,0:T(8,128)}) custom-call(s32[2]{0:T(128)S(1)} %pad_add_fusion.place, bf16[8,304,128]{2,1,0:T(8,128)(2,1)S(1)} %all-to-all-done.3.came, ...), custom_call_target="tpu_custom_call" | custom-call | flops 99999997952 | tf_op jit(solution)/shard_map/pallas_call | solution.py:373
  154.0 7.0 %collective-permute-done.29.refs_1_ = bf16[4,432,128]{2,1,0:T(8,128)(2,1)S(1)} collective-permute-done((bf16[4,432,128]{2,1,0:T(8,128)(2,1)S(1)}, bf16[4,432,128]{2,1,0:T(8,128)(2,1)S(1)}, u32[]{:S(2)}, u32[]{:S(2)}) %collective-permute-start.29) | collective-permute-done | bytes 442400 | tf_op jit(solution)/shard_map/ppermute | solution.py:412
  162.2 2.4 %collective-permute-start.33 = (bf16[432,128]{1,0:T(8,128)(2,1)S(1)}, bf16[432,128]{1,0:T(8,128)(2,1)S(1)}, u32[]{:S(2)}, u32[]{:S(2)}) collective-permute-start(bf16[432,128]{1,0:T(8,128)(2,1)S(1)} %get-tuple-element.149), channel_id=1, source_target_pairs={{0,24},{4,28},{8,16},{12,20},{16,8},{20,12},{24,0},{28,4},{1,25},{... | collective-permute-start | bytes 331784 | tf_op jit(solution)/shard_map/ppermute | solution.py:412
  178.5 3.0 %shard_map.231 = (f32[2,128,768]{2,1,0:T(8,128)}, f32[2,64,768]{2,1,0:T(8,128)}) custom-call(s32[2]{0:T(128)S(1)} %pad_add_fusion.place, bf16[192,768]{1,0:T(8,128)(2,1)S(1)} %add_convert_fusion.own, bf16[192,768]{1,0:T(8,128)(2,1)S(1)} %collective-permute-done.30.other, f32[384,768]{1,0:T(8,128)} %get-tuple-element.157.grad_mid, ...), custom_call_target="tpu_custom_call" | custom-call | tf_op jit(solution)/shard_map/pallas_call | solution.py:373
  (133 shorter events, 67.6 us)
Async XLA Ops:
  6.8 11.2 %collective-permute-start.1 = (bf16[448,128]{1,0:T(8,128)(2,1)S(1)}, bf16[448,128]{1,0:T(8,128)(2,1)S(1)}, u32[]{:S(2)}, u32[]{:S(2)}) collective-permute-start(bf16[448,128]{1,0:T(8,128)(2,1)S(1)} %shard_map.212.refs_0_), channel_id=1, source_target_pairs={{0,8},{4,12},{8,0},{12,4},{16,24},{20,28},{24,16},{28,20},{1,9},{5... | collective-permute-start | bytes 344072 | tf_op jit(solution)/shard_map/ppermute | solution.py:412
  8.6 11.7 %collective-permute-start = (bf16[448,128]{1,0:T(8,128)(2,1)S(1)}, bf16[448,128]{1,0:T(8,128)(2,1)S(1)}, u32[]{:S(2)}, u32[]{:S(2)}) collective-permute-start(bf16[448,128]{1,0:T(8,128)(2,1)S(1)} %shard_map.212.refs_0_), channel_id=1, source_target_pairs={{0,4},{4,0},{8,12},{12,8},{16,20},{20,16},{24,28},{28,24},{1,5},{5... | collective-permute-start | bytes 344072 | tf_op jit(solution)/shard_map/ppermute | solution.py:412
  10.8 10.7 %collective-permute-start.6 = (bf16[448,128]{1,0:T(8,128)(2,1)S(1)}, bf16[448,128]{1,0:T(8,128)(2,1)S(1)}, u32[]{:S(2)}, u32[]{:S(2)}) collective-permute-start(bf16[448,128]{1,0:T(8,128)(2,1)S(1)} %collective-permute-done.5.refs_6_), channel_id=1, source_target_pairs={{0,4},{4,0},{8,12},{12,8},{16,20},{20,16},{24,28},{28,24},{1,5},{5... | collective-permute-start | bytes 344072 | tf_op jit(solution)/shard_map/ppermute | solution.py:412
  18.6 16.8 %collective-permute-start.9 = (bf16[224,768]{1,0:T(8,128)(2,1)S(1)}, bf16[224,768]{1,0:T(8,128)(2,1)S(1)}, u32[]{:S(2)}, u32[]{:S(2)}) collective-permute-start(bf16[224,768]{1,0:T(8,128)(2,1)S(1)} %shard_map.213.refs_0_), channel_id=1, source_target_pairs={{0,16},{4,20},{8,24},{12,28},{16,0},{20,4},{24,8},{28,12},{1,17},{... | collective-permute-start | bytes 1032200 | tf_op jit(solution)/shard_map/ppermute | solution.py:412
  20.3 17.4 %collective-permute-start.8 = (bf16[224,768]{1,0:T(8,128)(2,1)S(1)}, bf16[224,768]{1,0:T(8,128)(2,1)S(1)}, u32[]{:S(2)}, u32[]{:S(2)}) collective-permute-start(bf16[224,768]{1,0:T(8,128)(2,1)S(1)} %shard_map.213.refs_0_), channel_id=1, source_target_pairs={{0,8},{4,12},{8,0},{12,4},{16,24},{20,28},{24,16},{28,20},{1,9},{5... | collective-permute-start | bytes 1032200 | tf_op jit(solution)/shard_map/ppermute | solution.py:412
  21.6 13.8 %collective-permute-start.7 = (bf16[224,768]{1,0:T(8,128)(2,1)S(1)}, bf16[224,768]{1,0:T(8,128)(2,1)S(1)}, u32[]{:S(2)}, u32[]{:S(2)}) collective-permute-start(bf16[224,768]{1,0:T(8,128)(2,1)S(1)} %shard_map.213.refs_0_), channel_id=1, source_target_pairs={{0,4},{4,0},{8,12},{12,8},{16,20},{20,16},{24,28},{28,24},{1,5},{5... | collective-permute-start | bytes 1032200 | tf_op jit(solution)/shard_map/ppermute | solution.py:412
  27.2 27.0 %all-to-all-start = ((bf16[8,304,128]{2,1,0:T(8,128)(2,1)}), bf16[8,304,128]{2,1,0:T(8,128)(2,1)S(1)}, u32[]{:S(2)}, u32[]{:S(2)}) async-start(bf16[8,304,128]{2,1,0:T(8,128)(2,1)} %get-tuple-element.90), calls=%async_computation | async-start | bytes 1245184 | tf_op jit(solution)/shard_map/all_to_all | solution.py:1100
  35.4 17.3 %collective-permute-start.12 = (bf16[224,768]{1,0:T(8,128)(2,1)S(1)}, bf16[224,768]{1,0:T(8,128)(2,1)S(1)}, u32[]{:S(2)}, u32[]{:S(2)}) collective-permute-start(bf16[224,768]{1,0:T(8,128)(2,1)S(1)} %collective-permute-done.9.refs_4_), channel_id=1, source_target_pairs={{0,8},{4,12},{8,0},{12,4},{16,24},{20,28},{24,16},{28,20},{1,9},{5... | collective-permute-start | bytes 1032200 | tf_op jit(solution)/shard_map/ppermute | solution.py:412
  35.5 26.8 %collective-permute-start.11 = (bf16[224,768]{1,0:T(8,128)(2,1)S(1)}, bf16[224,768]{1,0:T(8,128)(2,1)S(1)}, u32[]{:S(2)}, u32[]{:S(2)}) collective-permute-start(bf16[224,768]{1,0:T(8,128)(2,1)S(1)} %collective-permute-done.9.refs_4_), channel_id=1, source_target_pairs={{0,4},{4,0},{8,12},{12,8},{16,20},{20,16},{24,28},{28,24},{1,5},{5... | collective-permute-start | bytes 1032200 | tf_op jit(solution)/shard_map/ppermute | solution.py:412
  37.7 24.5 %collective-permute-start.10 = (bf16[224,768]{1,0:T(8,128)(2,1)S(1)}, bf16[224,768]{1,0:T(8,128)(2,1)S(1)}, u32[]{:S(2)}, u32[]{:S(2)}) collective-permute-start(bf16[224,768]{1,0:T(8,128)(2,1)S(1)} %collective-permute-done.8.refs_2_), channel_id=1, source_target_pairs={{0,4},{4,0},{8,12},{12,8},{16,20},{20,16},{24,28},{28,24},{1,5},{5... | collective-permute-start | bytes 1032200 | tf_op jit(solution)/shard_map/ppermute | solution.py:412
  52.7 12.4 %collective-permute-start.13 = (bf16[224,768]{1,0:T(8,128)(2,1)S(1)}, bf16[224,768]{1,0:T(8,128)(2,1)}, u32[]{:S(2)}, u32[]{:S(2)}) collective-permute-start(bf16[224,768]{1,0:T(8,128)(2,1)S(1)} %collective-permute-done.12.refs_6_), channel_id=1, source_target_pairs={{0,4},{4,0},{8,12},{12,8},{16,20},{20,16},{24,28},{28,24},{1,5},{5... | collective-permute-start | bytes 1032200 | tf_op jit(solution)/shard_map/ppermute | solution.py:412
  58.8 11.1 %all-to-all-start.1 = ((bf16[8,96,128]{2,1,0:T(8,128)(2,1)}), bf16[8,96,128]{2,1,0:T(8,128)(2,1)S(1)}, u32[]{:S(2)}, u32[]{:S(2)}) async-start(bf16[8,96,128]{2,1,0:T(8,128)(2,1)} %get-tuple-element.91), calls=%async_computation.1 | async-start | bytes 393216 | tf_op jit(solution)/shard_map/all_to_all | solution.py:1121
  97.1 17.2 %collective-permute-start.23 = (bf16[4,96,768]{2,1,0:T(8,128)(2,1)}, bf16[4,96,768]{2,1,0:T(8,128)(2,1)S(1)}, u32[]{:S(2)}, u32[]{:S(2)}) collective-permute-start(bf16[4,96,768]{2,1,0:T(8,128)(2,1)} %get-tuple-element.125), channel_id=1, source_target_pairs={{0,4},{4,0},{8,12},{12,8},{16,20},{20,16},{24,28},{28,24},{1,5},{5... | collective-permute-start | bytes 1769480 | tf_op jit(solution)/shard_map/ppermute | solution.py:412
  98.0 17.5 %collective-permute-start.24 = (bf16[2,2,96,768]{3,2,1,0:T(8,128)(2,1)}, bf16[2,2,96,768]{3,2,1,0:T(8,128)(2,1)S(1)}, u32[]{:S(2)}, u32[]{:S(2)}) collective-permute-start(bf16[2,2,96,768]{3,2,1,0:T(8,128)(2,1)} %get-tuple-element.127), channel_id=1, source_target_pairs={{0,8},{4,12},{8,0},{12,4},{16,24},{20,28},{24,16},{28,20},{1,9},{5... | collective-permute-start | bytes 1769480 | tf_op jit(solution)/shard_map/ppermute | solution.py:412
  104.5 14.0 %all-to-all-start.2 = ((bf16[8,96,128]{2,1,0:T(8,128)(2,1)}), bf16[8,96,128]{2,1,0:T(8,128)(2,1)S(1)}, u32[]{:S(2)}, u32[]{:S(2)}) async-start(bf16[8,96,128]{2,1,0:T(8,128)(2,1)} %get-tuple-element.115), calls=%async_computation.2 | async-start | bytes 393216 | tf_op jit(solution)/shard_map/all_to_all | solution.py:1198
  108.1 20.5 %collective-permute-start.25 = (bf16[4,32,768]{2,1,0:T(8,128)(2,1)}, bf16[4,32,768]{2,1,0:T(8,128)(2,1)}, u32[]{:S(2)}, u32[]{:S(2)}) collective-permute-start(bf16[4,32,768]{2,1,0:T(8,128)(2,1)} %get-tuple-element.133), channel_id=1, source_target_pairs={{0,4},{4,0},{8,12},{12,8},{16,20},{20,16},{24,28},{28,24},{1,5},{5... | collective-permute-start | bytes 589832 | tf_op jit(solution)/shard_map/ppermute | solution.py:412
  118.3 14.7 %collective-permute-start.26 = (bf16[2,96,768]{2,1,0:T(8,128)(2,1)}, bf16[2,96,768]{2,1,0:T(8,128)(2,1)}, u32[]{:S(2)}, u32[]{:S(2)}) collective-permute-start(bf16[2,96,768]{2,1,0:T(8,128)(2,1)} %shard_map.222), channel_id=1, source_target_pairs={{0,16},{4,20},{8,24},{12,28},{16,0},{20,4},{24,8},{28,12},{1,17},{... | collective-permute-start | bytes 884744 | tf_op jit(solution)/shard_map/ppermute | solution.py:412
  118.4 10.1 %collective-permute-start.21 = (bf16[192,768]{1,0:T(8,128)(2,1)S(1)}, bf16[192,768]{1,0:T(8,128)(2,1)S(1)}, u32[]{:S(2)}, u32[]{:S(2)}) collective-permute-start(bf16[192,768]{1,0:T(8,128)(2,1)S(1)} %add_convert_fusion.3), channel_id=1, source_target_pairs={{0,2},{1,3},{2,0},{3,1},{4,6},{5,7},{6,4},{7,5},{8,10},{9,11},{10,... | collective-permute-start | bytes 884744 | tf_op jit(solution)/shard_map/ppermute | solution.py:412
  124.3 19.7 %all-to-all-start.3 = ((bf16[8,304,128]{2,1,0:T(8,128)(2,1)}), bf16[8,304,128]{2,1,0:T(8,128)(2,1)S(1)}, u32[]{:S(2)}, u32[]{:S(2)}) async-start(bf16[8,304,128]{2,1,0:T(8,128)(2,1)} %shard_map.223), calls=%async_computation.3 | async-start | bytes 1245184 | tf_op jit(solution)/shard_map/all_to_all | solution.py:1226
  131.0 19.0 %collective-permute-start.34 = (bf16[2,128,768]{2,1,0:T(8,128)(2,1)}, bf16[2,128,768]{2,1,0:T(8,128)(2,1)S(1)}, u32[]{:S(2)}, u32[]{:S(2)}) collective-permute-start(bf16[2,128,768]{2,1,0:T(8,128)(2,1)} %get-tuple-element.151), channel_id=1, source_target_pairs={{0,8},{4,12},{8,0},{12,4},{16,24},{20,28},{24,16},{28,20},{1,9},{5... | collective-permute-start | bytes 1179656 | tf_op jit(solution)/shard_map/ppermute | solution.py:412
  148.0 13.0 %collective-permute-start.29 = (bf16[4,432,128]{2,1,0:T(8,128)(2,1)S(1)}, bf16[4,432,128]{2,1,0:T(8,128)(2,1)S(1)}, u32[]{:S(2)}, u32[]{:S(2)}) collective-permute-start(bf16[4,432,128]{2,1,0:T(8,128)(2,1)S(1)} %get-tuple-element.142), channel_id=1, source_target_pairs={{0,4},{4,0},{8,12},{12,8},{16,20},{20,16},{24,28},{28,24},{1,5},{5... | collective-permute-start | bytes 1327112 | tf_op jit(solution)/shard_map/ppermute | solution.py:412
  148.7 15.9 %collective-permute-start.36 = (bf16[96,768]{1,0:T(8,128)(2,1)S(1)}, bf16[96,768]{1,0:T(8,128)(2,1)S(1)}, u32[]{:S(2)}, u32[]{:S(2)}) collective-permute-start(bf16[96,768]{1,0:T(8,128)(2,1)S(1)} %copy-done.18), channel_id=1, source_target_pairs={{0,4},{4,0},{8,12},{12,8},{16,20},{20,16},{24,28},{28,24},{1,5},{5... | collective-permute-start | bytes 442376 | tf_op jit(solution)/shard_map/ppermute | solution.py:412
  152.6 14.0 %collective-permute-start.35 = (bf16[128,768]{1,0:T(8,128)(2,1)}, bf16[128,768]{1,0:T(8,128)(2,1)S(1)}, u32[]{:S(2)}, u32[]{:S(2)}) collective-permute-start(bf16[128,768]{1,0:T(8,128)(2,1)} %shard_map.228), channel_id=1, source_target_pairs={{0,16},{4,20},{8,24},{12,28},{16,0},{20,4},{24,8},{28,12},{1,17},{... | collective-permute-start | bytes 589832 | tf_op jit(solution)/shard_map/ppermute | solution.py:412
  152.7 23.2 %collective-permute-start.28 = (bf16[192,768]{1,0:T(8,128)(2,1)S(1)}, bf16[192,768]{1,0:T(8,128)(2,1)S(1)}, u32[]{:S(2)}, u32[]{:S(2)}) collective-permute-start(bf16[192,768]{1,0:T(8,128)(2,1)S(1)} %add_convert_fusion.1), channel_id=1, source_target_pairs={{0,2},{1,3},{2,0},{3,1},{4,6},{5,7},{6,4},{7,5},{8,10},{9,11},{10,... | collective-permute-start | bytes 884744 | tf_op jit(solution)/shard_map/ppermute | solution.py:412
  (38 other events, 305.8 us)

commit v6 on v5

--- a/solution.py
+++ b/solution.py
@@ -464,20 +464,29 @@
         store(16, LANES * g, jnp.concatenate([tail, jnp.zeros_like(tail)], axis=1))
 
 
-def pack_ffn_body(up, down, out, gain, packed):
+def pack_out_body(out, packed):
+    def store(row, lane, value):
+        packed[row : row + 16, lane : lane + LANES] = value
+
+    narrow_pack(out[...].astype(F32).T.astype(BF16), store)
+
+
+def pack_ffn_body(up, down, out, out_x, gain, packed):
     rows = up.shape[0]
     gain_column = gain[...].astype(F32).reshape(1, rows).T
     packed[:rows, :] = (up[...].astype(F32) * gain_column).astype(BF16)
     packed[rows : 2 * rows, :] = down[...]
-
-    def store(row, lane, value):
-        packed[2 * rows + row : 2 * rows + row + 16, lane : lane + LANES] = value
-
-    narrow_pack(out[...].astype(F32).T.astype(BF16), store)
+    packed[2 * rows : 2 * rows + 16, :] = out[:16, :]
+    packed[2 * rows + 16 : 2 * rows + 32, :] = out_x[:16, :]
+    for g in range(rows // 16):
+        lanes = slice(LANES * g, LANES * g + HEAD_DIM)
+        packed[2 * rows + 32 :, LANES * g : LANES * (g + 1)] = jnp.concatenate(
+            [out[16:, lanes], out_x[16:, lanes]], axis=1
+        )
 
 
 def place_ffn_body(place, *refs):
-    up, down, out, out_now = refs[8:]
+    up, down, out, out_now, out_x = refs[8:]
     rows = out.shape[0] // 8
     for i in range(8):
         owner = jnp.bitwise_xor(place[0], i)
@@ -487,8 +496,12 @@
         down[first, :] = part[rows : 2 * rows, :]
         for g in range(rows // 16):
             at = pl.ds(pl.multiple_of(owner * rows + 16 * g, 16), 16)
-            out[at, :LANES] = part[2 * rows : 2 * rows + 16, LANES * g : LANES * g + LANES]
-            out[at, LANES:] = part[2 * rows + 16 :, LANES * g : LANES * g + HEAD_DIM]
+            lanes = slice(LANES * g, LANES * (g + 1))
+            narrow = part[2 * rows + 32 :, lanes]
+            out[at, :LANES] = part[2 * rows : 2 * rows + 16, lanes]
+            out[at, LANES:] = narrow[:, :HEAD_DIM]
+            out_x[at, :LANES] = part[2 * rows + 16 : 2 * rows + 32, lanes]
+            out_x[at, LANES:] = narrow[:, HEAD_DIM:]
     out_now[...] = out[...]
 
 
@@ -624,10 +637,10 @@
     return jnp.concatenate(columns, axis=1)
 
 
-def out_proj_body(place, came, out, att, keep, send, scratch):
+def out_proj_body(came, came_x, out, out_x, att, part):
     att[...] = pair_rows(came, 2)
-    scratch[...] = dot(att[...], out[...], NT).astype(BF16)
-    split_halves(place, scratch, keep, send)
+    total = dot(att[...], out[...], NT)
+    part[...] = (total + dot(pair_rows(came_x, 2), out_x[...], NT)).astype(BF16)
 
 
 def feed_body(
@@ -655,7 +668,7 @@
 ):
     seqs = long_in.shape[0]
     rows = long_rows + short_in.shape[1]
-    join_halves(place, attended, own, other)
+    attended[...] = own[...].astype(F32) + other[...].astype(F32)
     for b in range(seqs):
         at = slice(b * rows, (b + 1) * rows)
         residual = jnp.concatenate([long_in[b], short_in[b]], axis=0).astype(F32)
@@ -1069,11 +1082,13 @@
         (),
         far(proj_weight, attention_gain),
     )
+    (out_packed,) = in_vmem(pack_out_body, [((32, hidden), BF16)], (), far(out_weight))
+    out_packed_x = exchange(out_packed, "head", 2)
     (ffn_packed,) = in_vmem(
         pack_ffn_body,
-        [((2 * shard + 32, hidden), BF16)],
+        [((2 * shard + 48, hidden), BF16)],
         (),
-        far(up_weight, down_t, out_weight, feed_gain),
+        far(up_weight, down_t) + (out_packed, out_packed_x) + far(feed_gain),
     )
     proj_z = [proj_packed] + [exchange(proj_packed, "seq", mask) for mask in (2, 4, 6)]
     proj_parts = [proj_packed, exchange(after(proj_packed, ffn_packed), "seq", 1)]
@@ -1120,28 +1135,22 @@
     )
     att_0 = lax.all_to_all(att_send, "seq", 0, 0, tiled=True)
     ffn_7 = exchange(ffn_6, "seq", 1)
-    up_full, down_full, out_full, out_now = in_vmem(
+    up_full, down_full, out_full, out_now, out_x = in_vmem(
         place_ffn_body,
         [((width, hidden), BF16, "far")] * 2
-        + [((width, local), BF16, "far"), ((width, local), BF16)],
+        + [((width, local), BF16, "far"), ((width, local), BF16), ((width, local), BF16)],
         (place,),
         far(after(ffn_packed, att_send), ffn_1, ffn_2, ffn_3, ffn_4, ffn_5, ffn_6, ffn_7),
     )
     att_0 = after(att_0, out_full)
-    att, keep, send = in_vmem(
+    att_x = exchange(att_0, "head", 2)
+    att, own = in_vmem(
         out_proj_body,
-        [
-            ((tokens, local), BF16, "far"),
-            ((tokens // 2, width), BF16),
-            ((tokens // 2, width), BF16),
-        ],
-        (place,),
-        (att_0, out_now),
-        scratch=[((tokens, width), BF16)],
+        [((tokens, local), BF16, "far"), ((tokens, width), BF16)],
+        (),
+        (att_0, att_x, out_now, out_x),
         fence=True,
     )
-    half = add_low(keep, exchange(send, "head", 1))
-    own = add_low(half, exchange(half, "head", 2))
     other = exchange(own, "head", 1)
     mid, squared, grad_out, keep, send, normed_ffn, grad_up = in_vmem(
         functools.partial(feed_body, long_rows),

time: 183 us -> 182 us (level)
  waiting for transfers between devices: 66.9 us -> 56.1 us
  starting transfers between devices: 54.2 us -> 63.2 us
    ppermute x39, waiting for transfers between devices: 58.8 us -> 50.2 us  [exchange(): return lax.ppermute(array, axis, [(i, i ^ mask) for i in range(size)])]
    ppermute x39, starting transfers between devices: 37.6 us -> 45.1 us  [exchange(): return lax.ppermute(array, axis, [(i, i ^ mask) for i in range(size)])]
    pallas_call x20 -> x21, Pallas kernels: 56.5 us -> 57.1 us  [in_vmem(): pl.pallas_call(body, out_shape=[pltpu.HBM(*out[:2]) if len(out) == 3 else...]
  transfers between devices with their start and end apart: 43 -> 43, of which waited for: 21 -> 17; matrix products, arithmetic and copies ran while one was open for 0% -> 0% of each run, Pallas kernels for 27% -> 28%
where the time goes in v6:
time: 182 us; the launch traced here: 181 us
  starting transfers between devices  63.2 us (35%)
  Pallas kernels  57.1 us (31%)
  waiting for transfers between devices  56.1 us (31%)
  local copies, waits for them, and re-layouts  2.82 us (2%)
    pallas_call x21, Pallas kernels, in_vmem(): pl.pallas_call(body, out_shape=[pltpu.HBM(*out[:2]) if len(out) == 3 else...  57.1 us
    ppermute x39, waiting for transfers between devices, exchange(): return lax.ppermute(array, axis, [(i, i ^ mask) for i in range(size)])  50.2 us
    ppermute x39, starting transfers between devices, exchange(): return lax.ppermute(array, axis, [(i, i ^ mask) for i in range(size)])  45.1 us
    all_to_all x1, starting transfers between devices, pair_shards(): came = lax.all_to_all(send, 'seq', 0, 0, tiled=True)  7.02 us
    all_to_all x1, waiting for transfers between devices, pair_shards(): mixed_came = lax.all_to_all(send, 'seq', 0, 0, tiled=True)  5.88 us
    all_to_all x1, starting transfers between devices, pair_shards(): grad_came = lax.all_to_all(send, 'seq', 0, 0, tiled=True)  4.12 us
  transfers between devices with their start and end apart: 43, of which 17 were waited for; matrix products, arithmetic and copies ran while one was open for 0% of the time, Pallas kernels for 28%

profile of v6, /device:TPU:0, one launch (start us, length us, event | category | flops | bytes accessed | tf_op | source)
XLA Modules:
  0.0 180.8 jit_solution(13959680143154519533)
XLA Ops:
  1.7 5.1 %collective-permute-start.6 = (bf16[448,128]{1,0:T(8,128)(2,1)S(1)}, bf16[448,128]{1,0:T(8,128)(2,1)S(1)}, u32[]{:S(2)}, u32[]{:S(2)}) collective-permute-start(bf16[448,128]{1,0:T(8,128)(2,1)S(1)} %shard_map.212.refs_0_), channel_id=1, source_target_pairs={{0,24},{4,28},{8,16},{12,20},{16,8},{20,12},{24,0},{28,4},{1,25},{... | collective-permute-start | bytes 344072 | tf_op jit(solution)/shard_map/ppermute | solution.py:412
  10.0 2.5 %collective-permute-done.out_x = bf16[32,768]{1,0:T(8,128)(2,1)S(1)} collective-permute-done((bf16[32,768]{1,0:T(8,128)(2,1)S(1)}, bf16[32,768]{1,0:T(8,128)(2,1)S(1)}, u32[]{:S(2)}, u32[]{:S(2)}) %collective-permute-start) | collective-permute-done | bytes 49184 | tf_op jit(solution)/shard_map/ppermute | solution.py:412
  23.8 2.5 %collective-permute-done.3.refs_3_ = bf16[448,128]{1,0:T(8,128)(2,1)S(1)} collective-permute-done((bf16[448,128]{1,0:T(8,128)(2,1)S(1)}, bf16[448,128]{1,0:T(8,128)(2,1)S(1)}, u32[]{:S(2)}, u32[]{:S(2)}) %collective-permute-start.3) | collective-permute-done | bytes 114720 | tf_op jit(solution)/shard_map/ppermute | solution.py:412
  26.3 3.0 %shard_map.215 = (bf16[8,304,128]{2,1,0:T(8,128)(2,1)}, bf16[384,768]{1,0:T(8,128)(2,1)}, bf16[3,768,192]{2,1,0:T(8,128)(2,1)}, f32[1,768]{1,0:T(1,128)}) custom-call(s32[2]{0:T(128)S(1)} %pad_add_fusion.place, bf16[448,128]{1,0:T(8,128)(2,1)S(1)} %shard_map.212.refs_0_, bf16[448,128]{1,0:T(8,128)(2,1)S(1)} %collective-permute-done.1.refs_1_, ...), custom_call_target="tpu_custom_call" | custom-call | flops 99999997952 | tf_op jit(solution)/shard_map/pallas_call | solution.py:373
  29.3 7.0 %all-to-all-start = ((bf16[8,304,128]{2,1,0:T(8,128)(2,1)}), bf16[8,304,128]{2,1,0:T(8,128)(2,1)S(1)}, u32[]{:S(2)}, u32[]{:S(2)}) async-start(bf16[8,304,128]{2,1,0:T(8,128)(2,1)} %get-tuple-element.90), calls=%async_computation | async-start | bytes 1245184 | tf_op jit(solution)/shard_map/all_to_all | solution.py:1115
  40.5 13.8 %collective-permute-done.13.refs_6_ = bf16[240,768]{1,0:T(8,128)(2,1)S(1)} collective-permute-done((bf16[240,768]{1,0:T(8,128)(2,1)S(1)}, bf16[240,768]{1,0:T(8,128)(2,1)S(1)}, u32[]{:S(2)}, u32[]{:S(2)}) %collective-permute-start.13) | collective-permute-done | bytes 368672 | tf_op jit(solution)/shard_map/ppermute | solution.py:412
  55.9 4.5 %shard_map.216 = (bf16[8,96,128]{2,1,0:T(8,128)(2,1)}, bf16[1536,64]{1,0:T(8,128)(2,1)}, bf16[1536,128]{1,0:T(8,128)(2,1)}, f32[64,1536]{1,0:T(8,128)}, f32[1,1536]{1,0:T(1,128)}, /*index=5*/bf16[8,304,128]{2,1,0:T(8,128)(2,1)}) custom-call(s32[2]{0:T(128)S(1)} %pad_add_fusion.place, s32[2]{0:T(128)S(1)} %copy-done.3, s32[2]{0:T(128)S(1)} %copy-done.4, ...), custom_call_target="tpu_custom_call" | custom-call | flops 99999997952 | tf_op jit(solution)/shard_map/pallas_call | solution.py:373
  60.4 3.4 %all-to-all-start.1 = ((bf16[8,96,128]{2,1,0:T(8,128)(2,1)}), bf16[8,96,128]{2,1,0:T(8,128)(2,1)S(1)}, u32[]{:S(2)}, u32[]{:S(2)}) async-start(bf16[8,96,128]{2,1,0:T(8,128)(2,1)} %get-tuple-element.91), calls=%async_computation.1 | async-start | bytes 393216 | tf_op jit(solution)/shard_map/all_to_all | solution.py:1136
  63.9 6.0 %collective-permute-done.14.refs_7_ = bf16[240,768]{1,0:T(8,128)(2,1)} collective-permute-done((bf16[240,768]{1,0:T(8,128)(2,1)S(1)}, bf16[240,768]{1,0:T(8,128)(2,1)}, u32[]{:S(2)}, u32[]{:S(2)}) %collective-permute-start.14) | collective-permute-done | bytes 368672 | tf_op jit(solution)/shard_map/ppermute | solution.py:412
  69.9 3.6 %shard_map.217 = (bf16[768,768]{1,0:T(8,128)(2,1)}, bf16[768,768]{1,0:T(8,128)(2,1)}, bf16[768,192]{1,0:T(8,128)(2,1)}, bf16[768,192]{1,0:T(8,128)(2,1)S(1)}, bf16[768,192]{1,0:T(8,128)(2,1)S(1)}) custom-call(s32[2]{0:T(128)S(1)} %pad_add_fusion.place, bf16[240,768]{1,0:T(8,128)(2,1)} %copy-done, bf16[240,768]{1,0:T(8,128)(2,1)} %copy-done.9, ...), custom_call_target="tpu_custom_call" | custom-call | tf_op jit(solution)/shard_map/pallas_call | solution.py:373
  75.0 4.2 %collective-permute-done.15.came_x = bf16[8,96,128]{2,1,0:T(8,128)(2,1)S(1)} collective-permute-done((bf16[8,96,128]{2,1,0:T(8,128)(2,1)S(1)}, bf16[8,96,128]{2,1,0:T(8,128)(2,1)S(1)}, u32[]{:S(2)}, u32[]{:S(2)}) %collective-permute-start.15) | collective-permute-done | bytes 196640 | tf_op jit(solution)/shard_map/ppermute | solution.py:412
  82.3 4.5 %shard_map.219 = (f32[384,768]{1,0:T(8,128)}, bf16[384,768]{1,0:T(8,128)(2,1)}, bf16[384,768]{1,0:T(8,128)(2,1)}, bf16[192,768]{1,0:T(8,128)(2,1)S(1)}, bf16[192...) custom-call(s32[2]{0:T(128)S(1)} %pad_add_fusion.place, s32[2]{0:T(128)S(1)} %copy-done.3, ...), custom_call_target="tpu_custom_call" | custom-call | tf_op jit(solution)/shard_map/pallas_call | solution.py:373
  90.0 5.4 %shard_map.220 = (bf16[2,2,96,768]{3,2,1,0:T(8,128)(2,1)}, bf16[2,96,768]{2,1,0:T(8,128)(2,1)}, bf16[2,96,768]{2,1,0:T(8,128)(2,1)}, bf16[192,768]{1,0:T(8,128)(...) custom-call(s32[2]{0:T(128)S(1)} %pad_add_fusion.place, ...), custom_call_target="tpu_custom_call" | custom-call | flops 99999997952 | tf_op jit(solution)/shard_map/pallas_call | solution.py:373
  99.3 3.5 %shard_map.221 = (f32[384,768]{1,0:T(8,128)}, bf16[8,96,128]{2,1,0:T(8,128)(2,1)}, bf16[4,32,768]{2,1,0:T(8,128)(2,1)}, bf16[4,32,768]{2,1,0:T(8,128)(2,1)}) custom-call(s32[2]{0:T(128)S(1)} %pad_add_fusion.place, bf16[192,768]{1,0:T(8,128)(2,1)S(1)} %add_convert_fusion.4.own, bf16[192,768]{1,0:T(8,128)(2,1)S(1)} %collective-permute-done.19.other, ...), custom_call_target="tpu_custom_call" | custom-call | tf_op jit(solution)/shard_map/pallas_call | solution.py:373
  102.9 4.1 %all-to-all-start.2 = ((bf16[8,96,128]{2,1,0:T(8,128)(2,1)}), bf16[8,96,128]{2,1,0:T(8,128)(2,1)S(1)}, u32[]{:S(2)}, u32[]{:S(2)}) async-start(bf16[8,96,128]{2,1,0:T(8,128)(2,1)} %get-tuple-element.115), calls=%async_computation.2 | async-start | bytes 393216 | tf_op jit(solution)/shard_map/all_to_all | solution.py:1207
  109.0 3.2 %collective-permute-done.23.refs_1_ = bf16[4,96,768]{2,1,0:T(8,128)(2,1)S(1)} collective-permute-done((bf16[4,96,768]{2,1,0:T(8,128)(2,1)}, bf16[4,96,768]{2,1,0:T(8,128)(2,1)S(1)}, u32[]{:S(2)}, u32[]{:S(2)}) %collective-permute-start.23) | collective-permute-done | bytes 589856 | tf_op jit(solution)/shard_map/ppermute | solution.py:412
  115.0 2.5 %collective-permute-start.26 = (bf16[2,96,768]{2,1,0:T(8,128)(2,1)}, bf16[2,96,768]{2,1,0:T(8,128)(2,1)}, u32[]{:S(2)}, u32[]{:S(2)}) collective-permute-start(bf16[2,96,768]{2,1,0:T(8,128)(2,1)} %shard_map.223), channel_id=1, source_target_pairs={{0,16},{4,20},{8,24},{12,28},{16,0},{20,4},{24,8},{28,12},{1,17},{... | collective-permute-start | bytes 884744 | tf_op jit(solution)/shard_map/ppermute | solution.py:412
  117.6 5.8 %shard_map.224 = bf16[8,304,128]{2,1,0:T(8,128)(2,1)} custom-call(s32[2]{0:T(128)S(1)} %pad_add_fusion.place, s32[2]{0:T(128)S(1)} %copy-done.3, s32[2]{0:T(128)S(1)} %copy-done.4, bf16[8,304,128]{2,1,0:T(8,128)(2,1)} %get-tuple-element.119.came, bf16[1536,64]{1,0:T(8,128)(2,1)} %get-tuple-element.120.q_all, bf16[1536,128]{1,0:T(8,128)(2,1)} %get-tuple-element.121.kv_all, ...), custom_call_target="tpu_custom_call" | custom-call | flops 99999997952 | tf_op jit(solution)/shard_map/pallas_call | solution.py:373
  123.4 3.6 %all-to-all-start.3 = ((bf16[8,304,128]{2,1,0:T(8,128)(2,1)}), bf16[8,304,128]{2,1,0:T(8,128)(2,1)S(1)}, u32[]{:S(2)}, u32[]{:S(2)}) async-start(bf16[8,304,128]{2,1,0:T(8,128)(2,1)} %shard_map.224), calls=%async_computation.3 | async-start | bytes 1245184 | tf_op jit(solution)/shard_map/all_to_all | solution.py:1235
  136.1 5.9 %all-to-all-done.3.came = bf16[8,304,128]{2,1,0:T(8,128)(2,1)S(1)} async-done(((bf16[8,304,128]{2,1,0:T(8,128)(2,1)}), bf16[8,304,128]{2,1,0:T(8,128)(2,1)S(1)}, u32[]{:S(2)}, u32[]{:S(2)}) %all-to-all-start.3) | async-done | bytes 622624 | tf_op jit(solution)/shard_map/all_to_all | solution.py:1235
  142.0 4.0 %shard_map.227 = (bf16[4,432,128]{2,1,0:T(8,128)(2,1)}, bf16[4,432,128]{2,1,0:T(8,128)(2,1)S(1)}, bf16[192,768]{1,0:T(8,128)(2,1)S(1)}, bf16[192,768]{1,0:T(8,128)(2,1)S(1)}, f32[9,24]{1,0:T(8,128)}) custom-call(s32[2]{0:T(128)S(1)} %pad_add_fusion.place, bf16[8,304,128]{2,1,0:T(8,128)(2,1)S(1)} %all-to-all-done.3.came, ...), custom_call_target="tpu_custom_call" | custom-call | flops 99999997952 | tf_op jit(solution)/shard_map/pallas_call | solution.py:373
  153.1 5.9 %collective-permute-done.29.refs_1_ = bf16[4,432,128]{2,1,0:T(8,128)(2,1)S(1)} collective-permute-done((bf16[4,432,128]{2,1,0:T(8,128)(2,1)S(1)}, bf16[4,432,128]{2,1,0:T(8,128)(2,1)S(1)}, u32[]{:S(2)}, u32[]{:S(2)}) %collective-permute-start.29) | collective-permute-done | bytes 442400 | tf_op jit(solution)/shard_map/ppermute | solution.py:412
  160.1 3.5 %collective-permute-start.33 = (bf16[432,128]{1,0:T(8,128)(2,1)S(1)}, bf16[432,128]{1,0:T(8,128)(2,1)S(1)}, u32[]{:S(2)}, u32[]{:S(2)}) collective-permute-start(bf16[432,128]{1,0:T(8,128)(2,1)S(1)} %get-tuple-element.149), channel_id=1, source_target_pairs={{0,24},{4,28},{8,16},{12,20},{16,8},{20,12},{24,0},{28,4},{1,25},{... | collective-permute-start | bytes 331784 | tf_op jit(solution)/shard_map/ppermute | solution.py:412
  177.2 3.0 %shard_map.232 = (f32[2,128,768]{2,1,0:T(8,128)}, f32[2,64,768]{2,1,0:T(8,128)}) custom-call(s32[2]{0:T(128)S(1)} %pad_add_fusion.place, bf16[192,768]{1,0:T(8,128)(2,1)S(1)} %add_convert_fusion.own, bf16[192,768]{1,0:T(8,128)(2,1)S(1)} %collective-permute-done.30.other, f32[384,768]{1,0:T(8,128)} %get-tuple-element.157.grad_mid, ...), custom_call_target="tpu_custom_call" | custom-call | tf_op jit(solution)/shard_map/pallas_call | solution.py:373
  (132 shorter events, 69.5 us)
Async XLA Ops:
  1.7 13.7 %collective-permute-start.6 = (bf16[448,128]{1,0:T(8,128)(2,1)S(1)}, bf16[448,128]{1,0:T(8,128)(2,1)S(1)}, u32[]{:S(2)}, u32[]{:S(2)}) collective-permute-start(bf16[448,128]{1,0:T(8,128)(2,1)S(1)} %shard_map.212.refs_0_), channel_id=1, source_target_pairs={{0,24},{4,28},{8,16},{12,20},{16,8},{20,12},{24,0},{28,4},{1,25},{... | collective-permute-start | bytes 344072 | tf_op jit(solution)/shard_map/ppermute | solution.py:412
  6.8 9.7 %collective-permute-start.4 = (bf16[448,128]{1,0:T(8,128)(2,1)S(1)}, bf16[448,128]{1,0:T(8,128)(2,1)S(1)}, u32[]{:S(2)}, u32[]{:S(2)}) collective-permute-start(bf16[448,128]{1,0:T(8,128)(2,1)S(1)} %shard_map.212.refs_0_), channel_id=1, source_target_pairs={{0,16},{4,20},{8,24},{12,28},{16,0},{20,4},{24,8},{28,12},{1,17},{... | collective-permute-start | bytes 344072 | tf_op jit(solution)/shard_map/ppermute | solution.py:412
  6.8 11.2 %collective-permute-start.2 = (bf16[448,128]{1,0:T(8,128)(2,1)S(1)}, bf16[448,128]{1,0:T(8,128)(2,1)S(1)}, u32[]{:S(2)}, u32[]{:S(2)}) collective-permute-start(bf16[448,128]{1,0:T(8,128)(2,1)S(1)} %shard_map.212.refs_0_), channel_id=1, source_target_pairs={{0,8},{4,12},{8,0},{12,4},{16,24},{20,28},{24,16},{28,20},{1,9},{5... | collective-permute-start | bytes 344072 | tf_op jit(solution)/shard_map/ppermute | solution.py:412
  18.6 17.8 %collective-permute-start.10 = (bf16[240,768]{1,0:T(8,128)(2,1)S(1)}, bf16[240,768]{1,0:T(8,128)(2,1)S(1)}, u32[]{:S(2)}, u32[]{:S(2)}) collective-permute-start(bf16[240,768]{1,0:T(8,128)(2,1)S(1)} %shard_map.214.refs_0_), channel_id=1, source_target_pairs={{0,16},{4,20},{8,24},{12,28},{16,0},{20,4},{24,8},{28,12},{1,17},{... | collective-permute-start | bytes 1105928 | tf_op jit(solution)/shard_map/ppermute | solution.py:412
  20.3 19.6 %collective-permute-start.9 = (bf16[240,768]{1,0:T(8,128)(2,1)S(1)}, bf16[240,768]{1,0:T(8,128)(2,1)S(1)}, u32[]{:S(2)}, u32[]{:S(2)}) collective-permute-start(bf16[240,768]{1,0:T(8,128)(2,1)S(1)} %shard_map.214.refs_0_), channel_id=1, source_target_pairs={{0,8},{4,12},{8,0},{12,4},{16,24},{20,28},{24,16},{28,20},{1,9},{5... | collective-permute-start | bytes 1105928 | tf_op jit(solution)/shard_map/ppermute | solution.py:412
  22.2 14.2 %collective-permute-start.8 = (bf16[240,768]{1,0:T(8,128)(2,1)S(1)}, bf16[240,768]{1,0:T(8,128)(2,1)S(1)}, u32[]{:S(2)}, u32[]{:S(2)}) collective-permute-start(bf16[240,768]{1,0:T(8,128)(2,1)S(1)} %shard_map.214.refs_0_), channel_id=1, source_target_pairs={{0,4},{4,0},{8,12},{12,8},{16,20},{20,16},{24,28},{28,24},{1,5},{5... | collective-permute-start | bytes 1105928 | tf_op jit(solution)/shard_map/ppermute | solution.py:412
  29.3 26.5 %all-to-all-start = ((bf16[8,304,128]{2,1,0:T(8,128)(2,1)}), bf16[8,304,128]{2,1,0:T(8,128)(2,1)S(1)}, u32[]{:S(2)}, u32[]{:S(2)}) async-start(bf16[8,304,128]{2,1,0:T(8,128)(2,1)} %get-tuple-element.90), calls=%async_computation | async-start | bytes 1245184 | tf_op jit(solution)/shard_map/all_to_all | solution.py:1115
  36.4 17.9 %collective-permute-start.13 = (bf16[240,768]{1,0:T(8,128)(2,1)S(1)}, bf16[240,768]{1,0:T(8,128)(2,1)S(1)}, u32[]{:S(2)}, u32[]{:S(2)}) collective-permute-start(bf16[240,768]{1,0:T(8,128)(2,1)S(1)} %collective-permute-done.10.refs_4_), channel_id=1, source_target_pairs={{0,8},{4,12},{8,0},{12,4},{16,24},{20,28},{24,16},{28,20},{1,9},{5... | collective-permute-start | bytes 1105928 | tf_op jit(solution)/shard_map/ppermute | solution.py:412
  38.5 25.4 %collective-permute-start.12 = (bf16[240,768]{1,0:T(8,128)(2,1)S(1)}, bf16[240,768]{1,0:T(8,128)(2,1)S(1)}, u32[]{:S(2)}, u32[]{:S(2)}) collective-permute-start(bf16[240,768]{1,0:T(8,128)(2,1)S(1)} %collective-permute-done.10.refs_4_), channel_id=1, source_target_pairs={{0,4},{4,0},{8,12},{12,8},{16,20},{20,16},{24,28},{28,24},{1,5},{5... | collective-permute-start | bytes 1105928 | tf_op jit(solution)/shard_map/ppermute | solution.py:412
  39.9 23.9 %collective-permute-start.11 = (bf16[240,768]{1,0:T(8,128)(2,1)S(1)}, bf16[240,768]{1,0:T(8,128)(2,1)S(1)}, u32[]{:S(2)}, u32[]{:S(2)}) collective-permute-start(bf16[240,768]{1,0:T(8,128)(2,1)S(1)} %collective-permute-done.9.refs_2_), channel_id=1, source_target_pairs={{0,4},{4,0},{8,12},{12,8},{16,20},{20,16},{24,28},{28,24},{1,5},{5... | collective-permute-start | bytes 1105928 | tf_op jit(solution)/shard_map/ppermute | solution.py:412
  54.3 15.6 %collective-permute-start.14 = (bf16[240,768]{1,0:T(8,128)(2,1)S(1)}, bf16[240,768]{1,0:T(8,128)(2,1)}, u32[]{:S(2)}, u32[]{:S(2)}) collective-permute-start(bf16[240,768]{1,0:T(8,128)(2,1)S(1)} %collective-permute-done.13.refs_6_), channel_id=1, source_target_pairs={{0,4},{4,0},{8,12},{12,8},{16,20},{20,16},{24,28},{28,24},{1,5},{5... | collective-permute-start | bytes 1105928 | tf_op jit(solution)/shard_map/ppermute | solution.py:412
  60.4 13.0 %all-to-all-start.1 = ((bf16[8,96,128]{2,1,0:T(8,128)(2,1)}), bf16[8,96,128]{2,1,0:T(8,128)(2,1)S(1)}, u32[]{:S(2)}, u32[]{:S(2)}) async-start(bf16[8,96,128]{2,1,0:T(8,128)(2,1)} %get-tuple-element.91), calls=%async_computation.1 | async-start | bytes 393216 | tf_op jit(solution)/shard_map/all_to_all | solution.py:1136
  95.4 16.8 %collective-permute-start.23 = (bf16[4,96,768]{2,1,0:T(8,128)(2,1)}, bf16[4,96,768]{2,1,0:T(8,128)(2,1)S(1)}, u32[]{:S(2)}, u32[]{:S(2)}) collective-permute-start(bf16[4,96,768]{2,1,0:T(8,128)(2,1)} %get-tuple-element.125), channel_id=1, source_target_pairs={{0,4},{4,0},{8,12},{12,8},{16,20},{20,16},{24,28},{28,24},{1,5},{5... | collective-permute-start | bytes 1769480 | tf_op jit(solution)/shard_map/ppermute | solution.py:412
  95.4 16.8 %collective-permute-start.24 = (bf16[2,2,96,768]{3,2,1,0:T(8,128)(2,1)}, bf16[2,2,96,768]{3,2,1,0:T(8,128)(2,1)S(1)}, u32[]{:S(2)}, u32[]{:S(2)}) collective-permute-start(bf16[2,2,96,768]{3,2,1,0:T(8,128)(2,1)} %get-tuple-element.127), channel_id=1, source_target_pairs={{0,8},{4,12},{8,0},{12,4},{16,24},{20,28},{24,16},{28,20},{1,9},{5... | collective-permute-start | bytes 1769480 | tf_op jit(solution)/shard_map/ppermute | solution.py:412
  102.9 14.8 %all-to-all-start.2 = ((bf16[8,96,128]{2,1,0:T(8,128)(2,1)}), bf16[8,96,128]{2,1,0:T(8,128)(2,1)S(1)}, u32[]{:S(2)}, u32[]{:S(2)}) async-start(bf16[8,96,128]{2,1,0:T(8,128)(2,1)} %get-tuple-element.115), calls=%async_computation.2 | async-start | bytes 393216 | tf_op jit(solution)/shard_map/all_to_all | solution.py:1207
  107.0 20.2 %collective-permute-start.25 = (bf16[4,32,768]{2,1,0:T(8,128)(2,1)}, bf16[4,32,768]{2,1,0:T(8,128)(2,1)}, u32[]{:S(2)}, u32[]{:S(2)}) collective-permute-start(bf16[4,32,768]{2,1,0:T(8,128)(2,1)} %get-tuple-element.133), channel_id=1, source_target_pairs={{0,4},{4,0},{8,12},{12,8},{16,20},{20,16},{24,28},{28,24},{1,5},{5... | collective-permute-start | bytes 589832 | tf_op jit(solution)/shard_map/ppermute | solution.py:412
  115.0 16.8 %collective-permute-start.26 = (bf16[2,96,768]{2,1,0:T(8,128)(2,1)}, bf16[2,96,768]{2,1,0:T(8,128)(2,1)}, u32[]{:S(2)}, u32[]{:S(2)}) collective-permute-start(bf16[2,96,768]{2,1,0:T(8,128)(2,1)} %shard_map.223), channel_id=1, source_target_pairs={{0,16},{4,20},{8,24},{12,28},{16,0},{20,4},{24,8},{28,12},{1,17},{... | collective-permute-start | bytes 884744 | tf_op jit(solution)/shard_map/ppermute | solution.py:412
  117.5 9.5 %collective-permute-start.21 = (bf16[192,768]{1,0:T(8,128)(2,1)S(1)}, bf16[192,768]{1,0:T(8,128)(2,1)S(1)}, u32[]{:S(2)}, u32[]{:S(2)}) collective-permute-start(bf16[192,768]{1,0:T(8,128)(2,1)S(1)} %add_convert_fusion.3), channel_id=1, source_target_pairs={{0,2},{1,3},{2,0},{3,1},{4,6},{5,7},{6,4},{7,5},{8,10},{9,11},{10,... | collective-permute-start | bytes 884744 | tf_op jit(solution)/shard_map/ppermute | solution.py:412
  123.4 18.6 %all-to-all-start.3 = ((bf16[8,304,128]{2,1,0:T(8,128)(2,1)}), bf16[8,304,128]{2,1,0:T(8,128)(2,1)S(1)}, u32[]{:S(2)}, u32[]{:S(2)}) async-start(bf16[8,304,128]{2,1,0:T(8,128)(2,1)} %shard_map.224), calls=%async_computation.3 | async-start | bytes 1245184 | tf_op jit(solution)/shard_map/all_to_all | solution.py:1235
  129.5 18.5 %collective-permute-start.34 = (bf16[2,128,768]{2,1,0:T(8,128)(2,1)}, bf16[2,128,768]{2,1,0:T(8,128)(2,1)S(1)}, u32[]{:S(2)}, u32[]{:S(2)}) collective-permute-start(bf16[2,128,768]{2,1,0:T(8,128)(2,1)} %get-tuple-element.151), channel_id=1, source_target_pairs={{0,8},{4,12},{8,0},{12,4},{16,24},{20,28},{24,16},{28,20},{1,9},{5... | collective-permute-start | bytes 1179656 | tf_op jit(solution)/shard_map/ppermute | solution.py:412
  146.0 13.0 %collective-permute-start.29 = (bf16[4,432,128]{2,1,0:T(8,128)(2,1)S(1)}, bf16[4,432,128]{2,1,0:T(8,128)(2,1)S(1)}, u32[]{:S(2)}, u32[]{:S(2)}) collective-permute-start(bf16[4,432,128]{2,1,0:T(8,128)(2,1)S(1)} %get-tuple-element.142), channel_id=1, source_target_pairs={{0,4},{4,0},{8,12},{12,8},{16,20},{20,16},{24,28},{28,24},{1,5},{5... | collective-permute-start | bytes 1327112 | tf_op jit(solution)/shard_map/ppermute | solution.py:412
  147.0 16.6 %collective-permute-start.36 = (bf16[96,768]{1,0:T(8,128)(2,1)S(1)}, bf16[96,768]{1,0:T(8,128)(2,1)S(1)}, u32[]{:S(2)}, u32[]{:S(2)}) collective-permute-start(bf16[96,768]{1,0:T(8,128)(2,1)S(1)} %copy-done.18), channel_id=1, source_target_pairs={{0,4},{4,0},{8,12},{12,8},{16,20},{20,16},{24,28},{28,24},{1,5},{5... | collective-permute-start | bytes 442376 | tf_op jit(solution)/shard_map/ppermute | solution.py:412
  150.6 14.0 %collective-permute-start.35 = (bf16[128,768]{1,0:T(8,128)(2,1)}, bf16[128,768]{1,0:T(8,128)(2,1)S(1)}, u32[]{:S(2)}, u32[]{:S(2)}) collective-permute-start(bf16[128,768]{1,0:T(8,128)(2,1)} %shard_map.229), channel_id=1, source_target_pairs={{0,16},{4,20},{8,24},{12,28},{16,0},{20,4},{24,8},{28,12},{1,17},{... | collective-permute-start | bytes 589832 | tf_op jit(solution)/shard_map/ppermute | solution.py:412
  151.3 22.8 %collective-permute-start.28 = (bf16[192,768]{1,0:T(8,128)(2,1)S(1)}, bf16[192,768]{1,0:T(8,128)(2,1)S(1)}, u32[]{:S(2)}, u32[]{:S(2)}) collective-permute-start(bf16[192,768]{1,0:T(8,128)(2,1)S(1)} %add_convert_fusion.1), channel_id=1, source_target_pairs={{0,2},{1,3},{2,0},{3,1},{4,6},{5,7},{6,4},{7,5},{8,10},{9,11},{10,... | collective-permute-start | bytes 884744 | tf_op jit(solution)/shard_map/ppermute | solution.py:412
  (38 other events, 305.3 us)

commit v7 on v6

--- a/solution.py
+++ b/solution.py
@@ -1096,7 +1096,7 @@
     proj_parts += [proj_z[2], exchange(proj_z[2], "seq", 1)]
     proj_parts += [proj_z[3], exchange(proj_z[3], "seq", 1)]
     ffn_0 = after(ffn_packed, *proj_z)
-    ffn_1 = exchange(ffn_0, "seq", 1)
+    ffn_1 = exchange(ffn_packed, "seq", 1)
     ffn_2 = exchange(ffn_0, "seq", 2)
     ffn_4 = exchange(ffn_0, "seq", 4)
     send, normed, proj_full, gain = in_vmem(

time: 182 us -> 181 us (level)
  starting transfers between devices: 63.2 us -> 60.1 us
  waiting for transfers between devices: 56.1 us -> 58.3 us
    ppermute x39, starting transfers between devices: 45.1 us -> 40.1 us  [exchange(): return lax.ppermute(array, axis, [(i, i ^ mask) for i in range(size)])]
    ppermute x39, waiting for transfers between devices: 50.2 us -> 52.2 us  [exchange(): return lax.ppermute(array, axis, [(i, i ^ mask) for i in range(size)])]
  transfers between devices with their start and end apart: 43 -> 43, of which waited for: 17 -> 18; matrix products, arithmetic and copies ran while one was open for 0% -> 0% of each run, Pallas kernels for 28% -> 28%
where the time goes in v7:
time: 181 us; the launch traced here: 180 us
  starting transfers between devices  60.1 us (33%)
  waiting for transfers between devices  58.3 us (32%)
  Pallas kernels  57.1 us (32%)
  local copies, waits for them, and re-layouts  2.82 us (2%)
    pallas_call x21, Pallas kernels, in_vmem(): pl.pallas_call(body, out_shape=[pltpu.HBM(*out[:2]) if len(out) == 3 else...  57.1 us
    ppermute x39, waiting for transfers between devices, exchange(): return lax.ppermute(array, axis, [(i, i ^ mask) for i in range(size)])  52.2 us
    ppermute x39, starting transfers between devices, exchange(): return lax.ppermute(array, axis, [(i, i ^ mask) for i in range(size)])  40.1 us
    all_to_all x1, starting transfers between devices, pair_shards(): came = lax.all_to_all(send, 'seq', 0, 0, tiled=True)  7.02 us
    all_to_all x1, waiting for transfers between devices, pair_shards(): mixed_came = lax.all_to_all(send, 'seq', 0, 0, tiled=True)  6.06 us
    all_to_all x1, starting transfers between devices, pair_shards(): mixed_came = lax.all_to_all(send, 'seq', 0, 0, tiled=True)  4.85 us
    all_to_all x1, starting transfers between devices, pair_shards(): att_0 = lax.all_to_all(att_send, 'seq', 0, 0, tiled=True)  4.53 us
  transfers between devices with their start and end apart: 43, of which 18 were waited for; matrix products, arithmetic and copies ran while one was open for 0% of the time, Pallas kernels for 28%

profile of v7, /device:TPU:0, one launch (start us, length us, event | category | flops | bytes accessed | tf_op | source)
XLA Modules:
  0.0 179.7 jit_solution(9878677157200304282)
XLA Ops:
  1.7 5.1 %collective-permute-start.6 = (bf16[448,128]{1,0:T(8,128)(2,1)S(1)}, bf16[448,128]{1,0:T(8,128)(2,1)S(1)}, u32[]{:S(2)}, u32[]{:S(2)}) collective-permute-start(bf16[448,128]{1,0:T(8,128)(2,1)S(1)} %shard_map.212.refs_0_), channel_id=1, source_target_pairs={{0,24},{4,28},{8,16},{12,20},{16,8},{20,12},{24,0},{28,4},{1,25},{... | collective-permute-start | bytes 344072 | tf_op jit(solution)/shard_map/ppermute | solution.py:412
  10.0 2.5 %collective-permute-done.out_x = bf16[32,768]{1,0:T(8,128)(2,1)S(1)} collective-permute-done((bf16[32,768]{1,0:T(8,128)(2,1)S(1)}, bf16[32,768]{1,0:T(8,128)(2,1)S(1)}, u32[]{:S(2)}, u32[]{:S(2)}) %collective-permute-start) | collective-permute-done | bytes 49184 | tf_op jit(solution)/shard_map/ppermute | solution.py:412
  26.3 3.0 %shard_map.215 = (bf16[8,304,128]{2,1,0:T(8,128)(2,1)}, bf16[384,768]{1,0:T(8,128)(2,1)}, bf16[3,768,192]{2,1,0:T(8,128)(2,1)}, f32[1,768]{1,0:T(1,128)}) custom-call(s32[2]{0:T(128)S(1)} %pad_add_fusion.place, bf16[448,128]{1,0:T(8,128)(2,1)S(1)} %shard_map.212.refs_0_, bf16[448,128]{1,0:T(8,128)(2,1)S(1)} %collective-permute-done.1.refs_1_, ...), custom_call_target="tpu_custom_call" | custom-call | flops 99999997952 | tf_op jit(solution)/shard_map/pallas_call | solution.py:373
  29.3 7.0 %all-to-all-start = ((bf16[8,304,128]{2,1,0:T(8,128)(2,1)}), bf16[8,304,128]{2,1,0:T(8,128)(2,1)S(1)}, u32[]{:S(2)}, u32[]{:S(2)}) async-start(bf16[8,304,128]{2,1,0:T(8,128)(2,1)} %get-tuple-element.90), calls=%async_computation | async-start | bytes 1245184 | tf_op jit(solution)/shard_map/all_to_all | solution.py:1115
  40.8 14.7 %collective-permute-done.13.refs_6_ = bf16[240,768]{1,0:T(8,128)(2,1)S(1)} collective-permute-done((bf16[240,768]{1,0:T(8,128)(2,1)S(1)}, bf16[240,768]{1,0:T(8,128)(2,1)S(1)}, u32[]{:S(2)}, u32[]{:S(2)}) %collective-permute-start.13) | collective-permute-done | bytes 368672 | tf_op jit(solution)/shard_map/ppermute | solution.py:412
  56.0 4.5 %shard_map.216 = (bf16[8,96,128]{2,1,0:T(8,128)(2,1)}, bf16[1536,64]{1,0:T(8,128)(2,1)}, bf16[1536,128]{1,0:T(8,128)(2,1)}, f32[64,1536]{1,0:T(8,128)}, f32[1,1536]{1,0:T(1,128)}, /*index=5*/bf16[8,304,128]{2,1,0:T(8,128)(2,1)}) custom-call(s32[2]{0:T(128)S(1)} %pad_add_fusion.place, s32[2]{0:T(128)S(1)} %copy-done.3, s32[2]{0:T(128)S(1)} %copy-done.4, ...), custom_call_target="tpu_custom_call" | custom-call | flops 99999997952 | tf_op jit(solution)/shard_map/pallas_call | solution.py:373
  60.6 4.5 %all-to-all-start.1 = ((bf16[8,96,128]{2,1,0:T(8,128)(2,1)}), bf16[8,96,128]{2,1,0:T(8,128)(2,1)S(1)}, u32[]{:S(2)}, u32[]{:S(2)}) async-start(bf16[8,96,128]{2,1,0:T(8,128)(2,1)} %get-tuple-element.91), calls=%async_computation.1 | async-start | bytes 393216 | tf_op jit(solution)/shard_map/all_to_all | solution.py:1136
  65.2 4.5 %collective-permute-done.14.refs_7_ = bf16[240,768]{1,0:T(8,128)(2,1)} collective-permute-done((bf16[240,768]{1,0:T(8,128)(2,1)S(1)}, bf16[240,768]{1,0:T(8,128)(2,1)}, u32[]{:S(2)}, u32[]{:S(2)}) %collective-permute-start.14) | collective-permute-done | bytes 368672 | tf_op jit(solution)/shard_map/ppermute | solution.py:412
  69.7 3.6 %shard_map.217 = (bf16[768,768]{1,0:T(8,128)(2,1)}, bf16[768,768]{1,0:T(8,128)(2,1)}, bf16[768,192]{1,0:T(8,128)(2,1)}, bf16[768,192]{1,0:T(8,128)(2,1)S(1)}, bf16[768,192]{1,0:T(8,128)(2,1)S(1)}) custom-call(s32[2]{0:T(128)S(1)} %pad_add_fusion.place, bf16[240,768]{1,0:T(8,128)(2,1)} %copy-done, bf16[240,768]{1,0:T(8,128)(2,1)} %copy-done.7, ...), custom_call_target="tpu_custom_call" | custom-call | tf_op jit(solution)/shard_map/pallas_call | solution.py:373
  74.8 4.2 %collective-permute-done.15.came_x = bf16[8,96,128]{2,1,0:T(8,128)(2,1)S(1)} collective-permute-done((bf16[8,96,128]{2,1,0:T(8,128)(2,1)S(1)}, bf16[8,96,128]{2,1,0:T(8,128)(2,1)S(1)}, u32[]{:S(2)}, u32[]{:S(2)}) %collective-permute-start.15) | collective-permute-done | bytes 196640 | tf_op jit(solution)/shard_map/ppermute | solution.py:412
  82.1 4.5 %shard_map.219 = (f32[384,768]{1,0:T(8,128)}, bf16[384,768]{1,0:T(8,128)(2,1)}, bf16[384,768]{1,0:T(8,128)(2,1)}, bf16[192,768]{1,0:T(8,128)(2,1)S(1)}, bf16[192...) custom-call(s32[2]{0:T(128)S(1)} %pad_add_fusion.place, s32[2]{0:T(128)S(1)} %copy-done.3, ...), custom_call_target="tpu_custom_call" | custom-call | tf_op jit(solution)/shard_map/pallas_call | solution.py:373
  89.8 5.4 %shard_map.220 = (bf16[2,2,96,768]{3,2,1,0:T(8,128)(2,1)}, bf16[2,96,768]{2,1,0:T(8,128)(2,1)}, bf16[2,96,768]{2,1,0:T(8,128)(2,1)}, bf16[192,768]{1,0:T(8,128)(...) custom-call(s32[2]{0:T(128)S(1)} %pad_add_fusion.place, ...), custom_call_target="tpu_custom_call" | custom-call | flops 99999997952 | tf_op jit(solution)/shard_map/pallas_call | solution.py:373
  99.1 3.5 %shard_map.221 = (f32[384,768]{1,0:T(8,128)}, bf16[8,96,128]{2,1,0:T(8,128)(2,1)}, bf16[4,32,768]{2,1,0:T(8,128)(2,1)}, bf16[4,32,768]{2,1,0:T(8,128)(2,1)}) custom-call(s32[2]{0:T(128)S(1)} %pad_add_fusion.place, bf16[192,768]{1,0:T(8,128)(2,1)S(1)} %add_convert_fusion.4.own, bf16[192,768]{1,0:T(8,128)(2,1)S(1)} %collective-permute-done.19.other, ...), custom_call_target="tpu_custom_call" | custom-call | tf_op jit(solution)/shard_map/pallas_call | solution.py:373
  102.6 3.6 %all-to-all-start.2 = ((bf16[8,96,128]{2,1,0:T(8,128)(2,1)}), bf16[8,96,128]{2,1,0:T(8,128)(2,1)S(1)}, u32[]{:S(2)}, u32[]{:S(2)}) async-start(bf16[8,96,128]{2,1,0:T(8,128)(2,1)} %get-tuple-element.115), calls=%async_computation.2 | async-start | bytes 393216 | tf_op jit(solution)/shard_map/all_to_all | solution.py:1207
  107.9 4.4 %collective-permute-done.23.refs_1_ = bf16[4,96,768]{2,1,0:T(8,128)(2,1)S(1)} collective-permute-done((bf16[4,96,768]{2,1,0:T(8,128)(2,1)}, bf16[4,96,768]{2,1,0:T(8,128)(2,1)S(1)}, u32[]{:S(2)}, u32[]{:S(2)}) %collective-permute-start.23) | collective-permute-done | bytes 589856 | tf_op jit(solution)/shard_map/ppermute | solution.py:412
  116.1 5.8 %shard_map.224 = bf16[8,304,128]{2,1,0:T(8,128)(2,1)} custom-call(s32[2]{0:T(128)S(1)} %pad_add_fusion.place, s32[2]{0:T(128)S(1)} %copy-done.3, s32[2]{0:T(128)S(1)} %copy-done.4, bf16[8,304,128]{2,1,0:T(8,128)(2,1)} %get-tuple-element.119.came, bf16[1536,64]{1,0:T(8,128)(2,1)} %get-tuple-element.120.q_all, bf16[1536,128]{1,0:T(8,128)(2,1)} %get-tuple-element.121.kv_all, ...), custom_call_target="tpu_custom_call" | custom-call | flops 99999997952 | tf_op jit(solution)/shard_map/pallas_call | solution.py:373
  121.9 4.9 %all-to-all-start.3 = ((bf16[8,304,128]{2,1,0:T(8,128)(2,1)}), bf16[8,304,128]{2,1,0:T(8,128)(2,1)S(1)}, u32[]{:S(2)}, u32[]{:S(2)}) async-start(bf16[8,304,128]{2,1,0:T(8,128)(2,1)} %shard_map.224), calls=%async_computation.3 | async-start | bytes 1245184 | tf_op jit(solution)/shard_map/all_to_all | solution.py:1235
  126.9 2.3 %shard_map.225 = (bf16[2,128,768]{2,1,0:T(8,128)(2,1)}, bf16[128,768]{1,0:T(8,128)(2,1)}, bf16[128,768]{1,0:T(8,128)(2,1)}) custom-call(s32[2]{0:T(128)S(1)} %pad_add_fusion.place, bf16[4,96,768]{2,1,0:T(8,128)(2,1)} %get-tuple-element.130.refs_0_, bf16[4,96,768]{2,1,0:T(8,128)(2,1)} %copy-done.16, bf16[4,32,768]{2,1,0:T(8,128)(2,1)} %get-tuple-element.132.refs_2_, ...), custom_call_target="tpu_custom_call" | custom-call | flops 99999997952 | tf_op jit(solution)/shard_map/pallas_call | solution.py:373
  135.6 6.1 %all-to-all-done.3.came = bf16[8,304,128]{2,1,0:T(8,128)(2,1)S(1)} async-done(((bf16[8,304,128]{2,1,0:T(8,128)(2,1)}), bf16[8,304,128]{2,1,0:T(8,128)(2,1)S(1)}, u32[]{:S(2)}, u32[]{:S(2)}) %all-to-all-start.3) | async-done | bytes 622624 | tf_op jit(solution)/shard_map/all_to_all | solution.py:1235
  141.7 4.0 %shard_map.227 = (bf16[4,432,128]{2,1,0:T(8,128)(2,1)}, bf16[4,432,128]{2,1,0:T(8,128)(2,1)S(1)}, bf16[192,768]{1,0:T(8,128)(2,1)S(1)}, bf16[192,768]{1,0:T(8,128)(2,1)S(1)}, f32[9,24]{1,0:T(8,128)}) custom-call(s32[2]{0:T(128)S(1)} %pad_add_fusion.place, bf16[8,304,128]{2,1,0:T(8,128)(2,1)S(1)} %all-to-all-done.3.came, ...), custom_call_target="tpu_custom_call" | custom-call | flops 99999997952 | tf_op jit(solution)/shard_map/pallas_call | solution.py:373
  152.4 6.3 %collective-permute-done.29.refs_1_ = bf16[4,432,128]{2,1,0:T(8,128)(2,1)S(1)} collective-permute-done((bf16[4,432,128]{2,1,0:T(8,128)(2,1)S(1)}, bf16[4,432,128]{2,1,0:T(8,128)(2,1)S(1)}, u32[]{:S(2)}, u32[]{:S(2)}) %collective-permute-start.29) | collective-permute-done | bytes 442400 | tf_op jit(solution)/shard_map/ppermute | solution.py:412
  159.8 2.8 %collective-permute-start.33 = (bf16[432,128]{1,0:T(8,128)(2,1)S(1)}, bf16[432,128]{1,0:T(8,128)(2,1)S(1)}, u32[]{:S(2)}, u32[]{:S(2)}) collective-permute-start(bf16[432,128]{1,0:T(8,128)(2,1)S(1)} %get-tuple-element.149), channel_id=1, source_target_pairs={{0,24},{4,28},{8,16},{12,20},{16,8},{20,12},{24,0},{28,4},{1,25},{... | collective-permute-start | bytes 331784 | tf_op jit(solution)/shard_map/ppermute | solution.py:412
  169.3 2.6 %collective-permute-done.32.b2 = bf16[432,128]{1,0:T(8,128)(2,1)S(1)} collective-permute-done((bf16[432,128]{1,0:T(8,128)(2,1)S(1)}, bf16[432,128]{1,0:T(8,128)(2,1)S(1)}, u32[]{:S(2)}, u32[]{:S(2)}) %collective-permute-start.32) | collective-permute-done | bytes 110624 | tf_op jit(solution)/shard_map/ppermute | solution.py:412
  176.2 3.0 %shard_map.232 = (f32[2,128,768]{2,1,0:T(8,128)}, f32[2,64,768]{2,1,0:T(8,128)}) custom-call(s32[2]{0:T(128)S(1)} %pad_add_fusion.place, bf16[192,768]{1,0:T(8,128)(2,1)S(1)} %add_convert_fusion.own, bf16[192,768]{1,0:T(8,128)(2,1)S(1)} %collective-permute-done.30.other, f32[384,768]{1,0:T(8,128)} %get-tuple-element.157.grad_mid, ...), custom_call_target="tpu_custom_call" | custom-call | tf_op jit(solution)/shard_map/pallas_call | solution.py:373
  (132 shorter events, 66.2 us)
Async XLA Ops:
  1.7 13.7 %collective-permute-start.6 = (bf16[448,128]{1,0:T(8,128)(2,1)S(1)}, bf16[448,128]{1,0:T(8,128)(2,1)S(1)}, u32[]{:S(2)}, u32[]{:S(2)}) collective-permute-start(bf16[448,128]{1,0:T(8,128)(2,1)S(1)} %shard_map.212.refs_0_), channel_id=1, source_target_pairs={{0,24},{4,28},{8,16},{12,20},{16,8},{20,12},{24,0},{28,4},{1,25},{... | collective-permute-start | bytes 344072 | tf_op jit(solution)/shard_map/ppermute | solution.py:412
  6.8 9.7 %collective-permute-start.4 = (bf16[448,128]{1,0:T(8,128)(2,1)S(1)}, bf16[448,128]{1,0:T(8,128)(2,1)S(1)}, u32[]{:S(2)}, u32[]{:S(2)}) collective-permute-start(bf16[448,128]{1,0:T(8,128)(2,1)S(1)} %shard_map.212.refs_0_), channel_id=1, source_target_pairs={{0,16},{4,20},{8,24},{12,28},{16,0},{20,4},{24,8},{28,12},{1,17},{... | collective-permute-start | bytes 344072 | tf_op jit(solution)/shard_map/ppermute | solution.py:412
  6.8 11.2 %collective-permute-start.2 = (bf16[448,128]{1,0:T(8,128)(2,1)S(1)}, bf16[448,128]{1,0:T(8,128)(2,1)S(1)}, u32[]{:S(2)}, u32[]{:S(2)}) collective-permute-start(bf16[448,128]{1,0:T(8,128)(2,1)S(1)} %shard_map.212.refs_0_), channel_id=1, source_target_pairs={{0,8},{4,12},{8,0},{12,4},{16,24},{20,28},{24,16},{28,20},{1,9},{5... | collective-permute-start | bytes 344072 | tf_op jit(solution)/shard_map/ppermute | solution.py:412
  18.6 17.8 %collective-permute-start.8 = (bf16[240,768]{1,0:T(8,128)(2,1)S(1)}, bf16[240,768]{1,0:T(8,128)(2,1)S(1)}, u32[]{:S(2)}, u32[]{:S(2)}) collective-permute-start(bf16[240,768]{1,0:T(8,128)(2,1)S(1)} %shard_map.214.refs_0_), channel_id=1, source_target_pairs={{0,4},{4,0},{8,12},{12,8},{16,20},{20,16},{24,28},{28,24},{1,5},{5... | collective-permute-start | bytes 1105928 | tf_op jit(solution)/shard_map/ppermute | solution.py:412
  20.1 18.1 %collective-permute-start.10 = (bf16[240,768]{1,0:T(8,128)(2,1)S(1)}, bf16[240,768]{1,0:T(8,128)(2,1)S(1)}, u32[]{:S(2)}, u32[]{:S(2)}) collective-permute-start(bf16[240,768]{1,0:T(8,128)(2,1)S(1)} %shard_map.214.refs_0_), channel_id=1, source_target_pairs={{0,16},{4,20},{8,24},{12,28},{16,0},{20,4},{24,8},{28,12},{1,17},{... | collective-permute-start | bytes 1105928 | tf_op jit(solution)/shard_map/ppermute | solution.py:412
  22.1 18.7 %collective-permute-start.9 = (bf16[240,768]{1,0:T(8,128)(2,1)S(1)}, bf16[240,768]{1,0:T(8,128)(2,1)S(1)}, u32[]{:S(2)}, u32[]{:S(2)}) collective-permute-start(bf16[240,768]{1,0:T(8,128)(2,1)S(1)} %shard_map.214.refs_0_), channel_id=1, source_target_pairs={{0,8},{4,12},{8,0},{12,4},{16,24},{20,28},{24,16},{28,20},{1,9},{5... | collective-permute-start | bytes 1105928 | tf_op jit(solution)/shard_map/ppermute | solution.py:412
  29.3 26.7 %all-to-all-start = ((bf16[8,304,128]{2,1,0:T(8,128)(2,1)}), bf16[8,304,128]{2,1,0:T(8,128)(2,1)S(1)}, u32[]{:S(2)}, u32[]{:S(2)}) async-start(bf16[8,304,128]{2,1,0:T(8,128)(2,1)} %get-tuple-element.90), calls=%async_computation | async-start | bytes 1245184 | tf_op jit(solution)/shard_map/all_to_all | solution.py:1115
  38.2 17.3 %collective-permute-start.13 = (bf16[240,768]{1,0:T(8,128)(2,1)S(1)}, bf16[240,768]{1,0:T(8,128)(2,1)S(1)}, u32[]{:S(2)}, u32[]{:S(2)}) collective-permute-start(bf16[240,768]{1,0:T(8,128)(2,1)S(1)} %collective-permute-done.10.refs_4_), channel_id=1, source_target_pairs={{0,8},{4,12},{8,0},{12,4},{16,24},{20,28},{24,16},{28,20},{1,9},{5... | collective-permute-start | bytes 1105928 | tf_op jit(solution)/shard_map/ppermute | solution.py:412
  38.5 26.7 %collective-permute-start.12 = (bf16[240,768]{1,0:T(8,128)(2,1)S(1)}, bf16[240,768]{1,0:T(8,128)(2,1)S(1)}, u32[]{:S(2)}, u32[]{:S(2)}) collective-permute-start(bf16[240,768]{1,0:T(8,128)(2,1)S(1)} %collective-permute-done.10.refs_4_), channel_id=1, source_target_pairs={{0,4},{4,0},{8,12},{12,8},{16,20},{20,16},{24,28},{28,24},{1,5},{5... | collective-permute-start | bytes 1105928 | tf_op jit(solution)/shard_map/ppermute | solution.py:412
  40.8 24.4 %collective-permute-start.11 = (bf16[240,768]{1,0:T(8,128)(2,1)S(1)}, bf16[240,768]{1,0:T(8,128)(2,1)S(1)}, u32[]{:S(2)}, u32[]{:S(2)}) collective-permute-start(bf16[240,768]{1,0:T(8,128)(2,1)S(1)} %collective-permute-done.9.refs_2_), channel_id=1, source_target_pairs={{0,4},{4,0},{8,12},{12,8},{16,20},{20,16},{24,28},{28,24},{1,5},{5... | collective-permute-start | bytes 1105928 | tf_op jit(solution)/shard_map/ppermute | solution.py:412
  55.5 14.1 %collective-permute-start.14 = (bf16[240,768]{1,0:T(8,128)(2,1)S(1)}, bf16[240,768]{1,0:T(8,128)(2,1)}, u32[]{:S(2)}, u32[]{:S(2)}) collective-permute-start(bf16[240,768]{1,0:T(8,128)(2,1)S(1)} %collective-permute-done.13.refs_6_), channel_id=1, source_target_pairs={{0,4},{4,0},{8,12},{12,8},{16,20},{20,16},{24,28},{28,24},{1,5},{5... | collective-permute-start | bytes 1105928 | tf_op jit(solution)/shard_map/ppermute | solution.py:412
  60.6 12.6 %all-to-all-start.1 = ((bf16[8,96,128]{2,1,0:T(8,128)(2,1)}), bf16[8,96,128]{2,1,0:T(8,128)(2,1)S(1)}, u32[]{:S(2)}, u32[]{:S(2)}) async-start(bf16[8,96,128]{2,1,0:T(8,128)(2,1)} %get-tuple-element.91), calls=%async_computation.1 | async-start | bytes 393216 | tf_op jit(solution)/shard_map/all_to_all | solution.py:1136
  95.1 17.2 %collective-permute-start.23 = (bf16[4,96,768]{2,1,0:T(8,128)(2,1)}, bf16[4,96,768]{2,1,0:T(8,128)(2,1)S(1)}, u32[]{:S(2)}, u32[]{:S(2)}) collective-permute-start(bf16[4,96,768]{2,1,0:T(8,128)(2,1)} %get-tuple-element.125), channel_id=1, source_target_pairs={{0,4},{4,0},{8,12},{12,8},{16,20},{20,16},{24,28},{28,24},{1,5},{5... | collective-permute-start | bytes 1769480 | tf_op jit(solution)/shard_map/ppermute | solution.py:412
  95.1 17.2 %collective-permute-start.24 = (bf16[2,2,96,768]{3,2,1,0:T(8,128)(2,1)}, bf16[2,2,96,768]{3,2,1,0:T(8,128)(2,1)S(1)}, u32[]{:S(2)}, u32[]{:S(2)}) collective-permute-start(bf16[2,2,96,768]{3,2,1,0:T(8,128)(2,1)} %get-tuple-element.127), channel_id=1, source_target_pairs={{0,8},{4,12},{8,0},{12,4},{16,24},{20,28},{24,16},{28,20},{1,9},{5... | collective-permute-start | bytes 1769480 | tf_op jit(solution)/shard_map/ppermute | solution.py:412
  102.6 13.5 %all-to-all-start.2 = ((bf16[8,96,128]{2,1,0:T(8,128)(2,1)}), bf16[8,96,128]{2,1,0:T(8,128)(2,1)S(1)}, u32[]{:S(2)}, u32[]{:S(2)}) async-start(bf16[8,96,128]{2,1,0:T(8,128)(2,1)} %get-tuple-element.115), calls=%async_computation.2 | async-start | bytes 393216 | tf_op jit(solution)/shard_map/all_to_all | solution.py:1207
  106.2 20.7 %collective-permute-start.25 = (bf16[4,32,768]{2,1,0:T(8,128)(2,1)}, bf16[4,32,768]{2,1,0:T(8,128)(2,1)}, u32[]{:S(2)}, u32[]{:S(2)}) collective-permute-start(bf16[4,32,768]{2,1,0:T(8,128)(2,1)} %get-tuple-element.133), channel_id=1, source_target_pairs={{0,4},{4,0},{8,12},{12,8},{16,20},{20,16},{24,28},{28,24},{1,5},{5... | collective-permute-start | bytes 589832 | tf_op jit(solution)/shard_map/ppermute | solution.py:412
  115.1 16.2 %collective-permute-start.26 = (bf16[2,96,768]{2,1,0:T(8,128)(2,1)}, bf16[2,96,768]{2,1,0:T(8,128)(2,1)}, u32[]{:S(2)}, u32[]{:S(2)}) collective-permute-start(bf16[2,96,768]{2,1,0:T(8,128)(2,1)} %shard_map.223), channel_id=1, source_target_pairs={{0,16},{4,20},{8,24},{12,28},{16,0},{20,4},{24,8},{28,12},{1,17},{... | collective-permute-start | bytes 884744 | tf_op jit(solution)/shard_map/ppermute | solution.py:412
  116.0 10.7 %collective-permute-start.21 = (bf16[192,768]{1,0:T(8,128)(2,1)S(1)}, bf16[192,768]{1,0:T(8,128)(2,1)S(1)}, u32[]{:S(2)}, u32[]{:S(2)}) collective-permute-start(bf16[192,768]{1,0:T(8,128)(2,1)S(1)} %add_convert_fusion.3), channel_id=1, source_target_pairs={{0,2},{1,3},{2,0},{3,1},{4,6},{5,7},{6,4},{7,5},{8,10},{9,11},{10,... | collective-permute-start | bytes 884744 | tf_op jit(solution)/shard_map/ppermute | solution.py:412
  121.9 19.8 %all-to-all-start.3 = ((bf16[8,304,128]{2,1,0:T(8,128)(2,1)}), bf16[8,304,128]{2,1,0:T(8,128)(2,1)S(1)}, u32[]{:S(2)}, u32[]{:S(2)}) async-start(bf16[8,304,128]{2,1,0:T(8,128)(2,1)} %shard_map.224), calls=%async_computation.3 | async-start | bytes 1245184 | tf_op jit(solution)/shard_map/all_to_all | solution.py:1235
  129.3 18.4 %collective-permute-start.34 = (bf16[2,128,768]{2,1,0:T(8,128)(2,1)}, bf16[2,128,768]{2,1,0:T(8,128)(2,1)S(1)}, u32[]{:S(2)}, u32[]{:S(2)}) collective-permute-start(bf16[2,128,768]{2,1,0:T(8,128)(2,1)} %get-tuple-element.151), channel_id=1, source_target_pairs={{0,8},{4,12},{8,0},{12,4},{16,24},{20,28},{24,16},{28,20},{1,9},{5... | collective-permute-start | bytes 1179656 | tf_op jit(solution)/shard_map/ppermute | solution.py:412
  145.7 13.0 %collective-permute-start.29 = (bf16[4,432,128]{2,1,0:T(8,128)(2,1)S(1)}, bf16[4,432,128]{2,1,0:T(8,128)(2,1)S(1)}, u32[]{:S(2)}, u32[]{:S(2)}) collective-permute-start(bf16[4,432,128]{2,1,0:T(8,128)(2,1)S(1)} %get-tuple-element.142), channel_id=1, source_target_pairs={{0,4},{4,0},{8,12},{12,8},{16,20},{20,16},{24,28},{28,24},{1,5},{5... | collective-permute-start | bytes 1327112 | tf_op jit(solution)/shard_map/ppermute | solution.py:412
  147.0 15.6 %collective-permute-start.36 = (bf16[96,768]{1,0:T(8,128)(2,1)S(1)}, bf16[96,768]{1,0:T(8,128)(2,1)S(1)}, u32[]{:S(2)}, u32[]{:S(2)}) collective-permute-start(bf16[96,768]{1,0:T(8,128)(2,1)S(1)} %copy-done.18), channel_id=1, source_target_pairs={{0,4},{4,0},{8,12},{12,8},{16,20},{20,16},{24,28},{28,24},{1,5},{5... | collective-permute-start | bytes 442376 | tf_op jit(solution)/shard_map/ppermute | solution.py:412
  150.3 14.0 %collective-permute-start.35 = (bf16[128,768]{1,0:T(8,128)(2,1)}, bf16[128,768]{1,0:T(8,128)(2,1)S(1)}, u32[]{:S(2)}, u32[]{:S(2)}) collective-permute-start(bf16[128,768]{1,0:T(8,128)(2,1)} %shard_map.229), channel_id=1, source_target_pairs={{0,16},{4,20},{8,24},{12,28},{16,0},{20,4},{24,8},{28,12},{1,17},{... | collective-permute-start | bytes 589832 | tf_op jit(solution)/shard_map/ppermute | solution.py:412
  151.3 22.3 %collective-permute-start.28 = (bf16[192,768]{1,0:T(8,128)(2,1)S(1)}, bf16[192,768]{1,0:T(8,128)(2,1)S(1)}, u32[]{:S(2)}, u32[]{:S(2)}) collective-permute-start(bf16[192,768]{1,0:T(8,128)(2,1)S(1)} %add_convert_fusion.1), channel_id=1, source_target_pairs={{0,2},{1,3},{2,0},{3,1},{4,6},{5,7},{6,4},{7,5},{8,10},{9,11},{10,... | collective-permute-start | bytes 884744 | tf_op jit(solution)/shard_map/ppermute | solution.py:412
  (38 other events, 297.8 us)

commit v8 on v7

--- a/solution.py
+++ b/solution.py
@@ -1143,13 +1143,12 @@
         far(after(ffn_packed, att_send), ffn_1, ffn_2, ffn_3, ffn_4, ffn_5, ffn_6, ffn_7),
     )
     att_0 = after(att_0, out_full)
-    att_x = exchange(att_0, "head", 2)
+    att_x = exchange(after(att_0, ffn_7), "head", 2)
     att, own = in_vmem(
         out_proj_body,
         [((tokens, local), BF16, "far"), ((tokens, width), BF16)],
         (),
         (att_0, att_x, out_now, out_x),
-        fence=True,
     )
     other = exchange(own, "head", 1)
     mid, squared, grad_out, keep, send, normed_ffn, grad_up = in_vmem(

time: 181 us -> 181 us (level)
  no operation moved by 1% of the time
where the time goes in v8:
time: 181 us; the launch traced here: 180 us
  starting transfers between devices  60.1 us (33%)
  waiting for transfers between devices  58.3 us (32%)
  Pallas kernels  57.1 us (32%)
  local copies, waits for them, and re-layouts  2.82 us (2%)
    pallas_call x21, Pallas kernels, in_vmem(): pl.pallas_call(body, out_shape=[pltpu.HBM(*out[:2]) if len(out) == 3 else...  57.1 us
    ppermute x39, waiting for transfers between devices, exchange(): return lax.ppermute(array, axis, [(i, i ^ mask) for i in range(size)])  52.2 us
    ppermute x39, starting transfers between devices, exchange(): return lax.ppermute(array, axis, [(i, i ^ mask) for i in range(size)])  40.1 us
    all_to_all x1, starting transfers between devices, pair_shards(): came = lax.all_to_all(send, 'seq', 0, 0, tiled=True)  7.02 us
    all_to_all x1, waiting for transfers between devices, pair_shards(): mixed_came = lax.all_to_all(send, 'seq', 0, 0, tiled=True)  6.06 us
    all_to_all x1, starting transfers between devices, pair_shards(): mixed_came = lax.all_to_all(send, 'seq', 0, 0, tiled=True)  4.85 us
    all_to_all x1, starting transfers between devices, pair_shards(): att_0 = lax.all_to_all(att_send, 'seq', 0, 0, tiled=True)  4.53 us
  transfers between devices with their start and end apart: 43, of which 18 were waited for; matrix products, arithmetic and copies ran while one was open for 0% of the time, Pallas kernels for 28%

profile of v8, /device:TPU:0, one launch (start us, length us, event | category | flops | bytes accessed | tf_op | source)
XLA Modules:
  0.0 179.7 jit_solution(9878677157200304282)
XLA Ops:
  1.7 5.1 %collective-permute-start.6 = (bf16[448,128]{1,0:T(8,128)(2,1)S(1)}, bf16[448,128]{1,0:T(8,128)(2,1)S(1)}, u32[]{:S(2)}, u32[]{:S(2)}) collective-permute-start(bf16[448,128]{1,0:T(8,128)(2,1)S(1)} %shard_map.212.refs_0_), channel_id=1, source_target_pairs={{0,24},{4,28},{8,16},{12,20},{16,8},{20,12},{24,0},{28,4},{1,25},{... | collective-permute-start | bytes 344072 | tf_op jit(solution)/shard_map/ppermute | solution.py:412
  10.0 2.5 %collective-permute-done.out_x = bf16[32,768]{1,0:T(8,128)(2,1)S(1)} collective-permute-done((bf16[32,768]{1,0:T(8,128)(2,1)S(1)}, bf16[32,768]{1,0:T(8,128)(2,1)S(1)}, u32[]{:S(2)}, u32[]{:S(2)}) %collective-permute-start) | collective-permute-done | bytes 49184 | tf_op jit(solution)/shard_map/ppermute | solution.py:412
  26.3 3.0 %shard_map.215 = (bf16[8,304,128]{2,1,0:T(8,128)(2,1)}, bf16[384,768]{1,0:T(8,128)(2,1)}, bf16[3,768,192]{2,1,0:T(8,128)(2,1)}, f32[1,768]{1,0:T(1,128)}) custom-call(s32[2]{0:T(128)S(1)} %pad_add_fusion.place, bf16[448,128]{1,0:T(8,128)(2,1)S(1)} %shard_map.212.refs_0_, bf16[448,128]{1,0:T(8,128)(2,1)S(1)} %collective-permute-done.1.refs_1_, ...), custom_call_target="tpu_custom_call" | custom-call | flops 99999997952 | tf_op jit(solution)/shard_map/pallas_call | solution.py:373
  29.3 7.0 %all-to-all-start = ((bf16[8,304,128]{2,1,0:T(8,128)(2,1)}), bf16[8,304,128]{2,1,0:T(8,128)(2,1)S(1)}, u32[]{:S(2)}, u32[]{:S(2)}) async-start(bf16[8,304,128]{2,1,0:T(8,128)(2,1)} %get-tuple-element.91), calls=%async_computation | async-start | bytes 1245184 | tf_op jit(solution)/shard_map/all_to_all | solution.py:1115
  40.8 14.7 %collective-permute-done.13.refs_6_ = bf16[240,768]{1,0:T(8,128)(2,1)S(1)} collective-permute-done((bf16[240,768]{1,0:T(8,128)(2,1)S(1)}, bf16[240,768]{1,0:T(8,128)(2,1)S(1)}, u32[]{:S(2)}, u32[]{:S(2)}) %collective-permute-start.13) | collective-permute-done | bytes 368672 | tf_op jit(solution)/shard_map/ppermute | solution.py:412
  56.0 4.5 %shard_map.216 = (bf16[8,96,128]{2,1,0:T(8,128)(2,1)}, bf16[1536,64]{1,0:T(8,128)(2,1)}, bf16[1536,128]{1,0:T(8,128)(2,1)}, f32[64,1536]{1,0:T(8,128)}, f32[1,1536]{1,0:T(1,128)}, /*index=5*/bf16[8,304,128]{2,1,0:T(8,128)(2,1)}) custom-call(s32[2]{0:T(128)S(1)} %pad_add_fusion.place, s32[2]{0:T(128)S(1)} %copy-done.3, s32[2]{0:T(128)S(1)} %copy-done.4, ...), custom_call_target="tpu_custom_call" | custom-call | flops 99999997952 | tf_op jit(solution)/shard_map/pallas_call | solution.py:373
  60.6 4.5 %all-to-all-start.1 = ((bf16[8,96,128]{2,1,0:T(8,128)(2,1)}), bf16[8,96,128]{2,1,0:T(8,128)(2,1)S(1)}, u32[]{:S(2)}, u32[]{:S(2)}) async-start(bf16[8,96,128]{2,1,0:T(8,128)(2,1)} %get-tuple-element.92), calls=%async_computation.1 | async-start | bytes 393216 | tf_op jit(solution)/shard_map/all_to_all | solution.py:1136
  65.2 4.5 %collective-permute-done.14.refs_7_ = bf16[240,768]{1,0:T(8,128)(2,1)} collective-permute-done((bf16[240,768]{1,0:T(8,128)(2,1)S(1)}, bf16[240,768]{1,0:T(8,128)(2,1)}, u32[]{:S(2)}, u32[]{:S(2)}) %collective-permute-start.14) | collective-permute-done | bytes 368672 | tf_op jit(solution)/shard_map/ppermute | solution.py:412
  69.7 3.6 %shard_map.217 = (bf16[768,768]{1,0:T(8,128)(2,1)}, bf16[768,768]{1,0:T(8,128)(2,1)}, bf16[768,192]{1,0:T(8,128)(2,1)}, bf16[768,192]{1,0:T(8,128)(2,1)S(1)}, bf16[768,192]{1,0:T(8,128)(2,1)S(1)}) custom-call(s32[2]{0:T(128)S(1)} %pad_add_fusion.place, bf16[240,768]{1,0:T(8,128)(2,1)} %copy-done, bf16[240,768]{1,0:T(8,128)(2,1)} %copy-done.7, ...), custom_call_target="tpu_custom_call" | custom-call | tf_op jit(solution)/shard_map/pallas_call | solution.py:373
  74.8 4.2 %collective-permute-done.15.came_x = bf16[8,96,128]{2,1,0:T(8,128)(2,1)S(1)} collective-permute-done((bf16[8,96,128]{2,1,0:T(8,128)(2,1)S(1)}, bf16[8,96,128]{2,1,0:T(8,128)(2,1)S(1)}, u32[]{:S(2)}, u32[]{:S(2)}) %collective-permute-start.15) | collective-permute-done | bytes 196640 | tf_op jit(solution)/shard_map/ppermute | solution.py:412
  82.1 4.5 %shard_map.219 = (f32[384,768]{1,0:T(8,128)}, bf16[384,768]{1,0:T(8,128)(2,1)}, bf16[384,768]{1,0:T(8,128)(2,1)}, bf16[192,768]{1,0:T(8,128)(2,1)S(1)}, bf16[192...) custom-call(s32[2]{0:T(128)S(1)} %pad_add_fusion.place, s32[2]{0:T(128)S(1)} %copy-done.3, ...), custom_call_target="tpu_custom_call" | custom-call | tf_op jit(solution)/shard_map/pallas_call | solution.py:373
  89.8 5.4 %shard_map.220 = (bf16[2,2,96,768]{3,2,1,0:T(8,128)(2,1)}, bf16[2,96,768]{2,1,0:T(8,128)(2,1)}, bf16[2,96,768]{2,1,0:T(8,128)(2,1)}, bf16[192,768]{1,0:T(8,128)(...) custom-call(s32[2]{0:T(128)S(1)} %pad_add_fusion.place, ...), custom_call_target="tpu_custom_call" | custom-call | flops 99999997952 | tf_op jit(solution)/shard_map/pallas_call | solution.py:373
  99.1 3.5 %shard_map.221 = (f32[384,768]{1,0:T(8,128)}, bf16[8,96,128]{2,1,0:T(8,128)(2,1)}, bf16[4,32,768]{2,1,0:T(8,128)(2,1)}, bf16[4,32,768]{2,1,0:T(8,128)(2,1)}) custom-call(s32[2]{0:T(128)S(1)} %pad_add_fusion.place, bf16[192,768]{1,0:T(8,128)(2,1)S(1)} %add_convert_fusion.4.own, bf16[192,768]{1,0:T(8,128)(2,1)S(1)} %collective-permute-done.19.other, ...), custom_call_target="tpu_custom_call" | custom-call | tf_op jit(solution)/shard_map/pallas_call | solution.py:373
  102.6 3.6 %all-to-all-start.2 = ((bf16[8,96,128]{2,1,0:T(8,128)(2,1)}), bf16[8,96,128]{2,1,0:T(8,128)(2,1)S(1)}, u32[]{:S(2)}, u32[]{:S(2)}) async-start(bf16[8,96,128]{2,1,0:T(8,128)(2,1)} %get-tuple-element.117), calls=%async_computation.2 | async-start | bytes 393216 | tf_op jit(solution)/shard_map/all_to_all | solution.py:1206
  107.9 4.4 %collective-permute-done.23.refs_1_ = bf16[4,96,768]{2,1,0:T(8,128)(2,1)S(1)} collective-permute-done((bf16[4,96,768]{2,1,0:T(8,128)(2,1)}, bf16[4,96,768]{2,1,0:T(8,128)(2,1)S(1)}, u32[]{:S(2)}, u32[]{:S(2)}) %collective-permute-start.23) | collective-permute-done | bytes 589856 | tf_op jit(solution)/shard_map/ppermute | solution.py:412
  116.1 5.8 %shard_map.224 = bf16[8,304,128]{2,1,0:T(8,128)(2,1)} custom-call(s32[2]{0:T(128)S(1)} %pad_add_fusion.place, s32[2]{0:T(128)S(1)} %copy-done.3, s32[2]{0:T(128)S(1)} %copy-done.4, bf16[8,304,128]{2,1,0:T(8,128)(2,1)} %get-tuple-element.121.came, bf16[1536,64]{1,0:T(8,128)(2,1)} %get-tuple-element.122.q_all, bf16[1536,128]{1,0:T(8,128)(2,1)} %get-tuple-element.123.kv_all, ...), custom_call_target="tpu_custom_call" | custom-call | flops 99999997952 | tf_op jit(solution)/shard_map/pallas_call | solution.py:373
  121.9 4.9 %all-to-all-start.3 = ((bf16[8,304,128]{2,1,0:T(8,128)(2,1)}), bf16[8,304,128]{2,1,0:T(8,128)(2,1)S(1)}, u32[]{:S(2)}, u32[]{:S(2)}) async-start(bf16[8,304,128]{2,1,0:T(8,128)(2,1)} %shard_map.224), calls=%async_computation.3 | async-start | bytes 1245184 | tf_op jit(solution)/shard_map/all_to_all | solution.py:1234
  126.9 2.3 %shard_map.225 = (bf16[2,128,768]{2,1,0:T(8,128)(2,1)}, bf16[128,768]{1,0:T(8,128)(2,1)}, bf16[128,768]{1,0:T(8,128)(2,1)}) custom-call(s32[2]{0:T(128)S(1)} %pad_add_fusion.place, bf16[4,96,768]{2,1,0:T(8,128)(2,1)} %get-tuple-element.132.refs_0_, bf16[4,96,768]{2,1,0:T(8,128)(2,1)} %copy-done.16, bf16[4,32,768]{2,1,0:T(8,128)(2,1)} %get-tuple-element.134.refs_2_, ...), custom_call_target="tpu_custom_call" | custom-call | flops 99999997952 | tf_op jit(solution)/shard_map/pallas_call | solution.py:373
  135.6 6.1 %all-to-all-done.3.came = bf16[8,304,128]{2,1,0:T(8,128)(2,1)S(1)} async-done(((bf16[8,304,128]{2,1,0:T(8,128)(2,1)}), bf16[8,304,128]{2,1,0:T(8,128)(2,1)S(1)}, u32[]{:S(2)}, u32[]{:S(2)}) %all-to-all-start.3) | async-done | bytes 622624 | tf_op jit(solution)/shard_map/all_to_all | solution.py:1234
  141.7 4.0 %shard_map.227 = (bf16[4,432,128]{2,1,0:T(8,128)(2,1)}, bf16[4,432,128]{2,1,0:T(8,128)(2,1)S(1)}, bf16[192,768]{1,0:T(8,128)(2,1)S(1)}, bf16[192,768]{1,0:T(8,128)(2,1)S(1)}, f32[9,24]{1,0:T(8,128)}) custom-call(s32[2]{0:T(128)S(1)} %pad_add_fusion.place, bf16[8,304,128]{2,1,0:T(8,128)(2,1)S(1)} %all-to-all-done.3.came, ...), custom_call_target="tpu_custom_call" | custom-call | flops 99999997952 | tf_op jit(solution)/shard_map/pallas_call | solution.py:373
  152.4 6.3 %collective-permute-done.29.refs_1_ = bf16[4,432,128]{2,1,0:T(8,128)(2,1)S(1)} collective-permute-done((bf16[4,432,128]{2,1,0:T(8,128)(2,1)S(1)}, bf16[4,432,128]{2,1,0:T(8,128)(2,1)S(1)}, u32[]{:S(2)}, u32[]{:S(2)}) %collective-permute-start.29) | collective-permute-done | bytes 442400 | tf_op jit(solution)/shard_map/ppermute | solution.py:412
  159.8 2.8 %collective-permute-start.33 = (bf16[432,128]{1,0:T(8,128)(2,1)S(1)}, bf16[432,128]{1,0:T(8,128)(2,1)S(1)}, u32[]{:S(2)}, u32[]{:S(2)}) collective-permute-start(bf16[432,128]{1,0:T(8,128)(2,1)S(1)} %get-tuple-element.151), channel_id=1, source_target_pairs={{0,24},{4,28},{8,16},{12,20},{16,8},{20,12},{24,0},{28,4},{1,25},{... | collective-permute-start | bytes 331784 | tf_op jit(solution)/shard_map/ppermute | solution.py:412
  169.3 2.6 %collective-permute-done.32.b2 = bf16[432,128]{1,0:T(8,128)(2,1)S(1)} collective-permute-done((bf16[432,128]{1,0:T(8,128)(2,1)S(1)}, bf16[432,128]{1,0:T(8,128)(2,1)S(1)}, u32[]{:S(2)}, u32[]{:S(2)}) %collective-permute-start.32) | collective-permute-done | bytes 110624 | tf_op jit(solution)/shard_map/ppermute | solution.py:412
  176.2 3.0 %shard_map.232 = (f32[2,128,768]{2,1,0:T(8,128)}, f32[2,64,768]{2,1,0:T(8,128)}) custom-call(s32[2]{0:T(128)S(1)} %pad_add_fusion.place, bf16[192,768]{1,0:T(8,128)(2,1)S(1)} %add_convert_fusion.own, bf16[192,768]{1,0:T(8,128)(2,1)S(1)} %collective-permute-done.30.other, f32[384,768]{1,0:T(8,128)} %get-tuple-element.159.grad_mid, ...), custom_call_target="tpu_custom_call" | custom-call | tf_op jit(solution)/shard_map/pallas_call | solution.py:373
  (132 shorter events, 66.2 us)
Async XLA Ops:
  1.7 13.7 %collective-permute-start.6 = (bf16[448,128]{1,0:T(8,128)(2,1)S(1)}, bf16[448,128]{1,0:T(8,128)(2,1)S(1)}, u32[]{:S(2)}, u32[]{:S(2)}) collective-permute-start(bf16[448,128]{1,0:T(8,128)(2,1)S(1)} %shard_map.212.refs_0_), channel_id=1, source_target_pairs={{0,24},{4,28},{8,16},{12,20},{16,8},{20,12},{24,0},{28,4},{1,25},{... | collective-permute-start | bytes 344072 | tf_op jit(solution)/shard_map/ppermute | solution.py:412
  6.8 9.7 %collective-permute-start.4 = (bf16[448,128]{1,0:T(8,128)(2,1)S(1)}, bf16[448,128]{1,0:T(8,128)(2,1)S(1)}, u32[]{:S(2)}, u32[]{:S(2)}) collective-permute-start(bf16[448,128]{1,0:T(8,128)(2,1)S(1)} %shard_map.212.refs_0_), channel_id=1, source_target_pairs={{0,16},{4,20},{8,24},{12,28},{16,0},{20,4},{24,8},{28,12},{1,17},{... | collective-permute-start | bytes 344072 | tf_op jit(solution)/shard_map/ppermute | solution.py:412
  6.8 11.2 %collective-permute-start.2 = (bf16[448,128]{1,0:T(8,128)(2,1)S(1)}, bf16[448,128]{1,0:T(8,128)(2,1)S(1)}, u32[]{:S(2)}, u32[]{:S(2)}) collective-permute-start(bf16[448,128]{1,0:T(8,128)(2,1)S(1)} %shard_map.212.refs_0_), channel_id=1, source_target_pairs={{0,8},{4,12},{8,0},{12,4},{16,24},{20,28},{24,16},{28,20},{1,9},{5... | collective-permute-start | bytes 344072 | tf_op jit(solution)/shard_map/ppermute | solution.py:412
  18.6 17.8 %collective-permute-start.8 = (bf16[240,768]{1,0:T(8,128)(2,1)S(1)}, bf16[240,768]{1,0:T(8,128)(2,1)S(1)}, u32[]{:S(2)}, u32[]{:S(2)}) collective-permute-start(bf16[240,768]{1,0:T(8,128)(2,1)S(1)} %shard_map.214.refs_0_), channel_id=1, source_target_pairs={{0,4},{4,0},{8,12},{12,8},{16,20},{20,16},{24,28},{28,24},{1,5},{5... | collective-permute-start | bytes 1105928 | tf_op jit(solution)/shard_map/ppermute | solution.py:412
  20.1 18.1 %collective-permute-start.10 = (bf16[240,768]{1,0:T(8,128)(2,1)S(1)}, bf16[240,768]{1,0:T(8,128)(2,1)S(1)}, u32[]{:S(2)}, u32[]{:S(2)}) collective-permute-start(bf16[240,768]{1,0:T(8,128)(2,1)S(1)} %shard_map.214.refs_0_), channel_id=1, source_target_pairs={{0,16},{4,20},{8,24},{12,28},{16,0},{20,4},{24,8},{28,12},{1,17},{... | collective-permute-start | bytes 1105928 | tf_op jit(solution)/shard_map/ppermute | solution.py:412
  22.1 18.7 %collective-permute-start.9 = (bf16[240,768]{1,0:T(8,128)(2,1)S(1)}, bf16[240,768]{1,0:T(8,128)(2,1)S(1)}, u32[]{:S(2)}, u32[]{:S(2)}) collective-permute-start(bf16[240,768]{1,0:T(8,128)(2,1)S(1)} %shard_map.214.refs_0_), channel_id=1, source_target_pairs={{0,8},{4,12},{8,0},{12,4},{16,24},{20,28},{24,16},{28,20},{1,9},{5... | collective-permute-start | bytes 1105928 | tf_op jit(solution)/shard_map/ppermute | solution.py:412
  29.3 26.7 %all-to-all-start = ((bf16[8,304,128]{2,1,0:T(8,128)(2,1)}), bf16[8,304,128]{2,1,0:T(8,128)(2,1)S(1)}, u32[]{:S(2)}, u32[]{:S(2)}) async-start(bf16[8,304,128]{2,1,0:T(8,128)(2,1)} %get-tuple-element.91), calls=%async_computation | async-start | bytes 1245184 | tf_op jit(solution)/shard_map/all_to_all | solution.py:1115
  38.2 17.3 %collective-permute-start.13 = (bf16[240,768]{1,0:T(8,128)(2,1)S(1)}, bf16[240,768]{1,0:T(8,128)(2,1)S(1)}, u32[]{:S(2)}, u32[]{:S(2)}) collective-permute-start(bf16[240,768]{1,0:T(8,128)(2,1)S(1)} %collective-permute-done.10.refs_4_), channel_id=1, source_target_pairs={{0,8},{4,12},{8,0},{12,4},{16,24},{20,28},{24,16},{28,20},{1,9},{5... | collective-permute-start | bytes 1105928 | tf_op jit(solution)/shard_map/ppermute | solution.py:412
  38.5 26.7 %collective-permute-start.12 = (bf16[240,768]{1,0:T(8,128)(2,1)S(1)}, bf16[240,768]{1,0:T(8,128)(2,1)S(1)}, u32[]{:S(2)}, u32[]{:S(2)}) collective-permute-start(bf16[240,768]{1,0:T(8,128)(2,1)S(1)} %collective-permute-done.10.refs_4_), channel_id=1, source_target_pairs={{0,4},{4,0},{8,12},{12,8},{16,20},{20,16},{24,28},{28,24},{1,5},{5... | collective-permute-start | bytes 1105928 | tf_op jit(solution)/shard_map/ppermute | solution.py:412
  40.8 24.4 %collective-permute-start.11 = (bf16[240,768]{1,0:T(8,128)(2,1)S(1)}, bf16[240,768]{1,0:T(8,128)(2,1)S(1)}, u32[]{:S(2)}, u32[]{:S(2)}) collective-permute-start(bf16[240,768]{1,0:T(8,128)(2,1)S(1)} %collective-permute-done.9.refs_2_), channel_id=1, source_target_pairs={{0,4},{4,0},{8,12},{12,8},{16,20},{20,16},{24,28},{28,24},{1,5},{5... | collective-permute-start | bytes 1105928 | tf_op jit(solution)/shard_map/ppermute | solution.py:412
  55.5 14.1 %collective-permute-start.14 = (bf16[240,768]{1,0:T(8,128)(2,1)S(1)}, bf16[240,768]{1,0:T(8,128)(2,1)}, u32[]{:S(2)}, u32[]{:S(2)}) collective-permute-start(bf16[240,768]{1,0:T(8,128)(2,1)S(1)} %collective-permute-done.13.refs_6_), channel_id=1, source_target_pairs={{0,4},{4,0},{8,12},{12,8},{16,20},{20,16},{24,28},{28,24},{1,5},{5... | collective-permute-start | bytes 1105928 | tf_op jit(solution)/shard_map/ppermute | solution.py:412
  60.6 12.6 %all-to-all-start.1 = ((bf16[8,96,128]{2,1,0:T(8,128)(2,1)}), bf16[8,96,128]{2,1,0:T(8,128)(2,1)S(1)}, u32[]{:S(2)}, u32[]{:S(2)}) async-start(bf16[8,96,128]{2,1,0:T(8,128)(2,1)} %get-tuple-element.92), calls=%async_computation.1 | async-start | bytes 393216 | tf_op jit(solution)/shard_map/all_to_all | solution.py:1136
  95.1 17.2 %collective-permute-start.23 = (bf16[4,96,768]{2,1,0:T(8,128)(2,1)}, bf16[4,96,768]{2,1,0:T(8,128)(2,1)S(1)}, u32[]{:S(2)}, u32[]{:S(2)}) collective-permute-start(bf16[4,96,768]{2,1,0:T(8,128)(2,1)} %get-tuple-element.127), channel_id=1, source_target_pairs={{0,4},{4,0},{8,12},{12,8},{16,20},{20,16},{24,28},{28,24},{1,5},{5... | collective-permute-start | bytes 1769480 | tf_op jit(solution)/shard_map/ppermute | solution.py:412
  95.1 17.2 %collective-permute-start.24 = (bf16[2,2,96,768]{3,2,1,0:T(8,128)(2,1)}, bf16[2,2,96,768]{3,2,1,0:T(8,128)(2,1)S(1)}, u32[]{:S(2)}, u32[]{:S(2)}) collective-permute-start(bf16[2,2,96,768]{3,2,1,0:T(8,128)(2,1)} %get-tuple-element.129), channel_id=1, source_target_pairs={{0,8},{4,12},{8,0},{12,4},{16,24},{20,28},{24,16},{28,20},{1,9},{5... | collective-permute-start | bytes 1769480 | tf_op jit(solution)/shard_map/ppermute | solution.py:412
  102.6 13.5 %all-to-all-start.2 = ((bf16[8,96,128]{2,1,0:T(8,128)(2,1)}), bf16[8,96,128]{2,1,0:T(8,128)(2,1)S(1)}, u32[]{:S(2)}, u32[]{:S(2)}) async-start(bf16[8,96,128]{2,1,0:T(8,128)(2,1)} %get-tuple-element.117), calls=%async_computation.2 | async-start | bytes 393216 | tf_op jit(solution)/shard_map/all_to_all | solution.py:1206
  106.2 20.7 %collective-permute-start.25 = (bf16[4,32,768]{2,1,0:T(8,128)(2,1)}, bf16[4,32,768]{2,1,0:T(8,128)(2,1)}, u32[]{:S(2)}, u32[]{:S(2)}) collective-permute-start(bf16[4,32,768]{2,1,0:T(8,128)(2,1)} %get-tuple-element.135), channel_id=1, source_target_pairs={{0,4},{4,0},{8,12},{12,8},{16,20},{20,16},{24,28},{28,24},{1,5},{5... | collective-permute-start | bytes 589832 | tf_op jit(solution)/shard_map/ppermute | solution.py:412
  115.1 16.2 %collective-permute-start.26 = (bf16[2,96,768]{2,1,0:T(8,128)(2,1)}, bf16[2,96,768]{2,1,0:T(8,128)(2,1)}, u32[]{:S(2)}, u32[]{:S(2)}) collective-permute-start(bf16[2,96,768]{2,1,0:T(8,128)(2,1)} %shard_map.223), channel_id=1, source_target_pairs={{0,16},{4,20},{8,24},{12,28},{16,0},{20,4},{24,8},{28,12},{1,17},{... | collective-permute-start | bytes 884744 | tf_op jit(solution)/shard_map/ppermute | solution.py:412
  116.0 10.7 %collective-permute-start.21 = (bf16[192,768]{1,0:T(8,128)(2,1)S(1)}, bf16[192,768]{1,0:T(8,128)(2,1)S(1)}, u32[]{:S(2)}, u32[]{:S(2)}) collective-permute-start(bf16[192,768]{1,0:T(8,128)(2,1)S(1)} %add_convert_fusion.3), channel_id=1, source_target_pairs={{0,2},{1,3},{2,0},{3,1},{4,6},{5,7},{6,4},{7,5},{8,10},{9,11},{10,... | collective-permute-start | bytes 884744 | tf_op jit(solution)/shard_map/ppermute | solution.py:412
  121.9 19.8 %all-to-all-start.3 = ((bf16[8,304,128]{2,1,0:T(8,128)(2,1)}), bf16[8,304,128]{2,1,0:T(8,128)(2,1)S(1)}, u32[]{:S(2)}, u32[]{:S(2)}) async-start(bf16[8,304,128]{2,1,0:T(8,128)(2,1)} %shard_map.224), calls=%async_computation.3 | async-start | bytes 1245184 | tf_op jit(solution)/shard_map/all_to_all | solution.py:1234
  129.3 18.4 %collective-permute-start.34 = (bf16[2,128,768]{2,1,0:T(8,128)(2,1)}, bf16[2,128,768]{2,1,0:T(8,128)(2,1)S(1)}, u32[]{:S(2)}, u32[]{:S(2)}) collective-permute-start(bf16[2,128,768]{2,1,0:T(8,128)(2,1)} %get-tuple-element.153), channel_id=1, source_target_pairs={{0,8},{4,12},{8,0},{12,4},{16,24},{20,28},{24,16},{28,20},{1,9},{5... | collective-permute-start | bytes 1179656 | tf_op jit(solution)/shard_map/ppermute | solution.py:412
  145.7 13.0 %collective-permute-start.29 = (bf16[4,432,128]{2,1,0:T(8,128)(2,1)S(1)}, bf16[4,432,128]{2,1,0:T(8,128)(2,1)S(1)}, u32[]{:S(2)}, u32[]{:S(2)}) collective-permute-start(bf16[4,432,128]{2,1,0:T(8,128)(2,1)S(1)} %get-tuple-element.144), channel_id=1, source_target_pairs={{0,4},{4,0},{8,12},{12,8},{16,20},{20,16},{24,28},{28,24},{1,5},{5... | collective-permute-start | bytes 1327112 | tf_op jit(solution)/shard_map/ppermute | solution.py:412
  147.0 15.6 %collective-permute-start.36 = (bf16[96,768]{1,0:T(8,128)(2,1)S(1)}, bf16[96,768]{1,0:T(8,128)(2,1)S(1)}, u32[]{:S(2)}, u32[]{:S(2)}) collective-permute-start(bf16[96,768]{1,0:T(8,128)(2,1)S(1)} %copy-done.18), channel_id=1, source_target_pairs={{0,4},{4,0},{8,12},{12,8},{16,20},{20,16},{24,28},{28,24},{1,5},{5... | collective-permute-start | bytes 442376 | tf_op jit(solution)/shard_map/ppermute | solution.py:412
  150.3 14.0 %collective-permute-start.35 = (bf16[128,768]{1,0:T(8,128)(2,1)}, bf16[128,768]{1,0:T(8,128)(2,1)S(1)}, u32[]{:S(2)}, u32[]{:S(2)}) collective-permute-start(bf16[128,768]{1,0:T(8,128)(2,1)} %shard_map.229), channel_id=1, source_target_pairs={{0,16},{4,20},{8,24},{12,28},{16,0},{20,4},{24,8},{28,12},{1,17},{... | collective-permute-start | bytes 589832 | tf_op jit(solution)/shard_map/ppermute | solution.py:412
  151.3 22.3 %collective-permute-start.28 = (bf16[192,768]{1,0:T(8,128)(2,1)S(1)}, bf16[192,768]{1,0:T(8,128)(2,1)S(1)}, u32[]{:S(2)}, u32[]{:S(2)}) collective-permute-start(bf16[192,768]{1,0:T(8,128)(2,1)S(1)} %add_convert_fusion.1), channel_id=1, source_target_pairs={{0,2},{1,3},{2,0},{3,1},{4,6},{5,7},{6,4},{7,5},{8,10},{9,11},{10,... | collective-permute-start | bytes 884744 | tf_op jit(solution)/shard_map/ppermute | solution.py:412
  (38 other events, 297.8 us)
